TPU v7x, 256 devices: a whole 4x4x8 slice. The times are simulated.
256 devices in a mesh: role: 4 (over y), batch: 8 (over z_hi, core), tensor: 8 (over z_lo, x).
Axes of the slice: x: 4, y: 4, z: 8 (z_hi: 4, z_lo: 2; z = z_hi * 2 + z_lo), core: 2. Of those that a mesh axis runs over, the one named last changes fastest.
Arguments:
- span: bfloat16 [8192, 5120], P('batch', ('role', 'tensor')), may hold values from -6 to 6
- key_value_weight: bfloat16 [5120, 8, 256], P('role', 'tensor'), may hold values from -0.078125 to 0.078125
- queries: bfloat16 [3, 128, 64, 128], P(None, 'batch', 'tensor'), may hold values from -6 to 6
- cache_codes: bfloat16 [3, 128, 8, 256, 256], P(None, 'batch', 'tensor'), may hold values from -127 to 127
- cache_scales: float32 [3, 128, 8, 16, 2], P(None, 'batch', 'tensor'), may hold values from 0.005 to 0.05
- cache_len: int32 [3, 128], P(None, 'batch'), may hold values from 2 to 256
- block_dest: int32 [512, 1], replicated, may hold values from 0 to 23; in each aligned block of 64 rows (0 to 63, 64 to 127, ...) at most 5 rows name the same one
- block_row: int32 [512], replicated, may hold values from 0 to 15
Outputs:
- judged: bfloat16 [3, 128, 8192], P(None, 'batch', 'tensor')
Inputs may be any that keep to these rules, and one draw needn't show every extreme that they name: `block_dest`: within the 64 blocks of each batch index's prompt (aligned blocks of rows), no value is named more than 5 times.
All inputs are finite; a program needn't handle non-finite values.
Results may differ from a plain program's by a relative error of at most 0.025.
Values may be sent and summed in bfloat16 or wider, within the bound.
No kernel may reach another device: no remote copies, remote signals or barrier semaphores. Data moves between devices by JAX's collectives and lax.ppermute only.
A program may use at most 64 MiB of HBM per device.

v0:
```python
import jax
import jax.numpy as jnp
from jax import lax
from jax.sharding import PartitionSpec as P

BLOCK_TOKENS = 16


def block_quantize(kv, heads, head_size, block):
    tokens = kv.shape[0]
    shaped = kv.reshape(tokens // block, block, heads, 2, head_size)
    largest = jnp.max(jnp.abs(shaped), axis=(1, 4))
    block_scales = (largest + 1e-06) / 127.0
    integer_codes = (shaped / block_scales[:, None, :, :, None]).astype(jnp.bfloat16)
    integer_codes = jnp.transpose(integer_codes, (0, 2, 1, 3, 4)).reshape(
        tokens // block, heads, block, 2 * head_size
    )
    return (integer_codes, block_scales)


def attend(query, res_codes, res_scales, length, new_codes, new_scales, target, block):
    rows, qheads, head_size = query.shape
    kv_heads = res_codes.shape[1]
    slots = res_codes.shape[2]
    grouped = query.reshape(rows, kv_heads, qheads // kv_heads, head_size)
    inverse = head_size ** (-0.5)
    key_scale = jnp.repeat(res_scales[..., 0], block, axis=2)
    value_scale = jnp.repeat(res_scales[..., 1], block, axis=2)
    resident = jnp.einsum(
        "rhgd,rhpd->rhgp", grouped, res_codes[..., :head_size], preferred_element_type=jnp.float32
    )
    resident = resident * (key_scale * inverse)[:, :, None, :]
    live = jnp.arange(slots)[None, :] < length[:, None]
    resident = jnp.where(live[:, None, None, :], resident, -jnp.inf)
    fresh = jnp.einsum(
        "rhgd,shtd->rhgst", grouped, new_codes[..., :head_size], preferred_element_type=jnp.float32
    )
    fresh = fresh * (new_scales[..., 0].T * inverse)[None, :, None, :, None]
    joined = target[None, :] == jnp.arange(rows)[:, None]
    fresh = jnp.where(joined[:, None, None, :, None], fresh, -jnp.inf)
    top = jnp.maximum(jnp.max(resident, axis=-1), jnp.max(fresh, axis=(-2, -1)))
    exp_res = jnp.exp(resident - top[..., None])
    exp_new = jnp.exp(fresh - top[..., None, None])
    total = jnp.sum(exp_res, axis=-1) + jnp.sum(exp_new, axis=(-2, -1))
    weight_res = (exp_res * value_scale[:, :, None, :]).astype(jnp.bfloat16)
    weight_new = (exp_new * new_scales[..., 1].T[None, :, None, :, None]).astype(jnp.bfloat16)
    summed = jnp.einsum(
        "rhgp,rhpd->rhgd",
        weight_res,
        res_codes[..., head_size:],
        preferred_element_type=jnp.float32,
    )
    summed = summed + jnp.einsum(
        "rhgst,shtd->rhgd",
        weight_new,
        new_codes[..., head_size:],
        preferred_element_type=jnp.float32,
    )
    return (summed / total[..., None]).reshape(rows, qheads * head_size).astype(jnp.bfloat16)


def body(
    span, key_value_weight, queries, cache_codes, cache_scales, cache_len, block_dest, block_row
):
    role = lax.axis_index("role")
    batch_index = lax.axis_index("batch")
    n_batch = lax.axis_size("batch")
    n_role = lax.axis_size("role")
    kv_heads = key_value_weight.shape[1]
    head_size = queries.shape[-1]
    flat_weight = key_value_weight.reshape(key_value_weight.shape[0], kv_heads * 2 * head_size)
    partial_rows = jnp.dot(
        lax.all_gather(span, "tensor", axis=1, tiled=True),
        flat_weight,
        preferred_element_type=jnp.float32,
    )
    projected_rows = lax.psum(partial_rows.astype(jnp.bfloat16), "role").astype(jnp.float32)
    integer_codes, block_scales = block_quantize(projected_rows, kv_heads, head_size, BLOCK_TOKENS)
    dest_all = block_dest[:, 0]
    group = jnp.clip(role - 1, 0, n_role - 2)
    all_codes, all_scales = (
        lax.all_gather(integer_codes, "batch", axis=0, tiled=True),
        lax.all_gather(block_scales.astype(jnp.bfloat16), "batch", axis=0, tiled=True).astype(
            block_scales.dtype
        ),
    )
    mine = group * n_batch + batch_index
    target = jnp.where(dest_all == mine, block_row, -1)
    got_codes, got_scales, got_target = (all_codes, all_scales, target)
    query = lax.dynamic_index_in_dim(queries, group, 0, keepdims=False)
    res_codes = lax.dynamic_index_in_dim(cache_codes, group, 0, keepdims=False)
    res_scales = lax.dynamic_index_in_dim(cache_scales, group, 0, keepdims=False)
    length = lax.dynamic_index_in_dim(cache_len, group, 0, keepdims=False)
    own = attend(
        query, res_codes, res_scales, length, got_codes, got_scales, got_target, BLOCK_TOKENS
    )
    collected = lax.all_gather(own[None], "role", axis=0, tiled=True)
    return collected[1:]


def solution(mesh):
    return jax.shard_map(
        body,
        mesh=mesh,
        in_specs=(
            P("batch", ("role", "tensor")),
            P("role", "tensor", None),
            P(None, "batch", "tensor", None),
            P(None, "batch", "tensor", None, None),
            P(None, "batch", "tensor", None, None),
            P(None, "batch"),
            P(),
            P(),
        ),
        out_specs=P(None, "batch", "tensor"),
        check_vma=False,
    )
```

profile of v0, /device:TPU:6, one launch (start us, length us, event | category | flops | bytes accessed | tf_op | source)
XLA Modules:
  0.0 199.4 jit_solution(11359962655978412874)
XLA Ops:
  6.5 0.7 all-gather.5.cloned.1.call-update
  7.3 48.1 %all-gather.5.cloned.1.call-done = bf16[1024,1280]{0,1:T(8,128)(2,1)} async-done(((bf16[1024,160]{0,1:T(8,128)(2,1)}), bf16[1024,1280]{0,1:T(8,128)(2,1)}) %all-gather.5.cloned.1.call-update) | async-done | bytes 2621456 | tf_op jit(solution)/shard_map/all_gather | solution.py:73
  55.4 3.4 %convolution_convert_fusion = bf16[1024,256]{1,0:T(8,128)(2,1)} fusion(bf16[1024,1280]{0,1:T(8,128)(2,1)} %all-gather.5.cloned.1.call-done, bf16[1280,1,256]{2,0,1:T(8,128)(2,1)S(1)} %copy-done), kind=kOutput, calls=%fused_computation.13 | convolution fusion | flops 671350784 | bytes 3801088 | tf_op jit(solution)/shard_map/dot_general | solution.py:72
  58.9 49.3 %all-reduce.2.cloned.1.call-done = bf16[1024,256]{1,0:T(8,128)(2,1)} async-done(((bf16[1024,256]{1,0:T(8,128)(2,1)}), bf16[1024,256]{1,0:T(8,128)(2,1)}) %all-reduce.2.cloned.1.call-update) | async-done | bytes 524304 | tf_op jit(solution)/shard_map/psum | solution.py:77
  108.3 1.2 convert_abs_fusion
  109.5 0.5 abs.15
  110.1 0.4 reduce_max.28
  110.5 0.1 copy.40
  110.6 0.1 div.37
  110.8 0.1 convert
  110.9 1.4 fusion.13
  112.3 0.7 dynamic-slice_bitcast_fusion.2
  113.1 0.1 broadcast_in_dim.50
  113.2 0.1 mul.79
  113.3 0.7 fusion.20
  114.0 0.8 dynamic-slice_bitcast_fusion.1
  114.7 1.7 dynamic-slice_bitcast_fusion
  116.4 0.1 iota_compare_fusion.1
  116.5 0.5 fusion.22
  117.1 0.1 broadcast_in_dim.55
  117.2 0.1 broadcast_in_dim.56
  117.3 12.8 %all-gather.1 = bf16[8,64,2]{1,2,0:T(2,128)(2,1)S(1)} all-gather(bf16[1,64,2]{1,2,0:T(2,128)(2,1)S(1)} %get-tuple-element.11), channel_id=2, replica_groups=mesh['role'=4,'batch'=8,'tensor'=8] {'batch'}, dimensions={0}, use_global_device_ids=true | all-gather | bytes 2304 | tf_op jit(solution)/shard_map/all_gather | solution.py:83
  130.1 0.1 reshape.247
  130.2 35.9 %all-gather.7.cloned.1.call-done = bf16[512,1,16,256]{3,0,2,1:T(8,128)(2,1)} async-done(((bf16[64,1,16,256]{3,0,2,1:T(8,128)(2,1)}), bf16[512,1,16,256]{3,0,2,1:T(8,128)(2,1)}) %all-gather.7.cloned.1.call-update) | async-done | bytes 4194320 | tf_op jit(solution)/shard_map/all_gather | solution.py:82
  166.1 4.3 %fusion.1 = (f32[16,8]{0,1:T(8,128)S(1)}, f32[512,16,16,8]{0,2,3,1:T(8,128)}) fusion(f32[512]{0:T(512)S(1)} %bitcast.100, pred[16,512]{1,0:T(8,128)(4,1)S(1)} %iota_compare_fusion, bf16[16,8,128]{2,1,0:T(8,128)(2,1)S(1)} %dynamic-slice_bitcast_fusion.1, bf16[512,1,16,256]{3,0,2,1:T(8,128)(2,1)} %all-gather.7.cloned.1.call-done), kind=kOutput, calls=%fused_computation.5 | convolution fusion | flops 271581056 | bytes 6334976 | tf_op jit(solution)/shard_map/rhgd,shtd->rhgst/dot_general | solution.py:35
  170.3 0.1 copy.45
  170.4 5.3 %fusion = (f32[16,8]{0,1:T(8,128)S(1)}, bf16[16,8,512,16]{2,0,1,3:T(8,128)(2,1)}) fusion(f32[512,16,16,8]{0,2,3,1:T(8,128)} %get-tuple-element.16, f32[16,8]{0,1:T(8,128)S(1)} %max.18, f32[512]{0:T(512)S(1)} %bitcast.101, pred[16,512]{1,0:T(8,128)(4,1)S(1)} %iota_compare_fusion, f32[512]{0:T(512)S(1)} %bitcast.102), kind=kLoop, calls=%fused_computation.4 | loop fusion | flops 6291328 | bytes 6304768 | tf_op jit(solution)/shard_map/reduce_sum | solution.py:44
  175.7 0.2 fusion.15
  175.9 3.6 %fusion.7 = f32[16,1,8,128]{3,2,0,1:T(8,128)S(1)} fusion(bf16[16,8,512,16]{2,0,1,3:T(8,128)(2,1)} %get-tuple-element.6, bf16[512,1,16,256]{3,0,2,1:T(8,128)(2,1)} %all-gather.7.cloned.1.call-done), kind=kOutput, calls=%fused_computation.16 | convolution fusion | flops 268435456 | bytes 4259840 | tf_op jit(solution)/shard_map/rhgst,shtd->rhgd/dot_general | solution.py:53
  179.5 0.3 fusion.12
  179.9 12.3 %all_gather.15 = bf16[4,16,1024]{2,1,0:T(8,128)(2,1)S(1)} all-gather(bf16[1,16,1024]{2,1,0:T(8,128)(2,1)S(1)} %convert_element_type.64), channel_id=1, replica_groups=mesh['role'=4,'batch'=8,'tensor'=8] {'role'}, dimensions={0}, use_global_device_ids=true | all-gather | bytes 163840 | tf_op jit(solution)/shard_map/all_gather | solution.py:97
  192.2 0.6 slice.44
  (27 shorter events, 0.5 us)
Async XLA Ops:
  6.5 48.9 %copy-start = (bf16[1280,1,256]{2,0,1:T(8,128)(2,1)S(1)}, bf16[1280,1,256]{2,0,1:T(8,128)(2,1)}, u32[]{:S(2)}) copy-start(bf16[1280,1,256]{2,0,1:T(8,128)(2,1)} %param.9) | copy-start | bytes 1966084
  6.5 48.9 %all-gather.5.cloned.1.call-start = ((), (), s32[]{:S(2)}) async-start(), calls=%async_computation | async-start | bytes 2949120 | tf_op jit(solution)/shard_map/all_gather | solution.py:73
  7.3 101.0 %all-reduce.2.cloned.1.call-start = ((), (), s32[]{:S(2)}) async-start(), calls=%async_computation.1 | async-start | bytes 1048576 | tf_op jit(solution)/shard_map/psum | solution.py:77
  58.9 107.2 %all-gather.7.cloned.1.call-start = ((), (), s32[]{:S(2)}) async-start(), calls=%async_computation.2 | async-start | bytes 4718592 | tf_op jit(solution)/shard_map/all_gather | solution.py:82
  108.3 2.5 %copy-start.1 = (bf16[1024,256]{1,0:T(8,128)(2,1)S(1)}, bf16[1024,256]{1,0:T(8,128)(2,1)}, u32[]{:S(2)}) copy-start(bf16[1024,256]{1,0:T(8,128)(2,1)} %all-reduce.2.cloned.1.call-done) | copy-start | bytes 1572868
  110.9 6.4 %copy-start.2 = (s32[512,1]{0,1:T(1,128)S(1)}, s32[512,1]{0,1:T(1,128)}, u32[]{:S(2)}) copy-start(s32[512,1]{0,1:T(1,128)} %param.14) | copy-start | bytes 6148
  110.9 6.4 %copy-start.3 = (s32[512]{0:T(512)S(1)}, s32[512]{0:T(512)}, u32[]{:S(2)}) copy-start(s32[512]{0:T(512)} %param.15) | copy-start | bytes 6148
Sparse Core Ops, SparseCore 0:
  9.1 46.2 all-gather.4
  59.0 49.2 all-reduce.1
  112.4 53.5 all-gather.6
where the time goes:
time: 200 us; the launch traced here: 199 us
  waiting for transfers between devices  134 us (67%)
  blocking collectives  25.1 us (13%)
  between operations  13.3 us (7%)
  matrix products  12.1 us (6%)
  other arithmetic  8.63 us (4%)
  local copies, waits for them, and re-layouts  6.15 us (3%)
    psum x1, waiting for transfers between devices, body(): lax.psum(partial_rows.astype(jnp.bfloat16), 'role').astype(jnp.float32)  49.3 us
    all_gather x1, waiting for transfers between devices, body(): lax.all_gather(span, 'tensor', axis=1, tiled=True)  48.1 us
    all_gather x1, waiting for transfers between devices, body(): lax.all_gather(integer_codes, 'batch', axis=0, tiled=True)  35.9 us
    all_gather x1, blocking collectives, body(): lax.all_gather(block_scales.astype(jnp.bfloat16), 'batch', axis=0, tiled=...  12.8 us
    all_gather x1, blocking collectives, body(): collected = lax.all_gather(own[None], 'role', axis=0, tiled=True)  12.3 us
    reduce_sum x2, other arithmetic, attend(): total = jnp.sum(exp_res, axis=-1) + jnp.sum(exp_new, axis=(-2, -1))  5.42 us
    dot_general x1, matrix products, attend(): jnp.einsum('rhgd,shtd->rhgst', grouped, new_codes[..., :head_size], prefe...  4.27 us
  transfers between devices with their start and end apart: 3, of which 3 were waited for; matrix products, arithmetic and copies ran while one was open for 3% of the time, Pallas kernels for 0%

commit v1 on v0

v1 whole, which is shorter than its diff:
```python
import jax
import jax.numpy as jnp
from jax import lax
from jax.experimental import pallas as pl
from jax.experimental.pallas import tpu as pltpu
from jax.sharding import PartitionSpec as P

BLOCK = 16
LOW = -1e38
F32 = jnp.float32
BF16 = jnp.bfloat16
VMEM = pl.BlockSpec(memory_space=pltpu.VMEM)
SMEM = pl.BlockSpec(memory_space=pltpu.SMEM)


def call(kernel, outs, args, specs, scratch=(), flops=0, nbytes=0):
    return pl.pallas_call(
        kernel,
        out_shape=outs,
        in_specs=specs,
        out_specs=jax.tree.map(lambda _: VMEM, outs),
        scratch_shapes=list(scratch),
        compiler_params=pltpu.CompilerParams(vmem_limit_bytes=40 * 1024 * 1024),
        cost_estimate=pl.CostEstimate(flops=flops, bytes_accessed=nbytes, transcendentals=0),
    )(*args)


def dot(a, b, ca, cb):
    return lax.dot_general(a, b, (((ca,), (cb,)), ((), ())), preferred_element_type=F32)


def three(v):
    hi = v.astype(BF16).astype(F32)
    mid = (v - hi).astype(BF16).astype(F32)
    return hi, mid, v - hi - mid


def cut_kernel(role_ref, x_ref, *outs):
    role = role_ref[0]
    tokens = x_ref.shape[0] // 4
    feats = x_ref.shape[1]
    for d in range(4):
        quarter = lax.rem(role + d, 4)
        rows = x_ref[pl.ds(pl.multiple_of(quarter * tokens, tokens), tokens), :].astype(F32)
        rows = jnp.concatenate([rows, jnp.zeros((tokens, 256 - feats), F32)], axis=1)
        outs[d][...] = jnp.transpose(rows)[:feats].astype(BF16)


def weight_kernel(slot_ref, core_ref, w_ref, own_ref, oth_ref, tmp):
    rows = w_ref.shape[0] // 8
    for s in range(8):
        start = pl.multiple_of(slot_ref[s] * rows, rows)
        tmp[pl.ds(s * rows, rows), :] = w_ref[pl.ds(start, rows), :].astype(F32)
    first = core_ref[0] == 0
    keys = jnp.transpose(tmp[:, :128]).astype(BF16)
    values = jnp.transpose(tmp[:, 128:]).astype(BF16)
    own_ref[...] = jnp.where(first, keys, values)
    oth_ref[...] = jnp.where(first, values, keys)


def pick_kernel(code_ref, q_ref, own_ref, oth_ref):
    q = q_ref[...]
    row = lax.broadcasted_iota(jnp.int32, (q.shape[0], 128), 0)
    for d in range(8):
        sel = jnp.where(row == code_ref[d : d + 1, :], 1.0, 0.0).astype(BF16)
        piece = dot(q, sel, 0, 0).astype(BF16)
        if d < 4:
            own_ref[d] = piece
        else:
            oth_ref[d - 4] = piece


def add_kernel(a_ref, b_ref, *outs):
    for d in range(4):
        outs[d][...] = a_ref[d] + b_ref[d]


def resident_kernel(len_ref, q_ref, c_ref, ks_ref, vs_ref, out_ref):
    base = pl.program_id(0) * 4
    lane = lax.broadcasted_iota(jnp.int32, (8, 256), 1)
    lane128 = lax.broadcasted_iota(jnp.int32, (8, 128), 1)
    for n in range(4):
        codes = c_ref[0, n, 0]
        ks = ks_ref[0, 0, n : n + 1, :] * (128.0**-0.5)
        vs = vs_ref[0, 0, n : n + 1, :]
        s = dot(q_ref[0, n], codes[:, :128], 1, 1) * ks
        live = lane < len_ref[base + n]
        s = jnp.where(live, s, -jnp.inf)
        m = jnp.max(s, axis=1, keepdims=True)
        e = jnp.exp(s - m)
        den = jnp.sum(e, axis=1, keepdims=True)
        acc = dot((e * vs).astype(BF16), codes[:, 128:], 1, 0)
        out_ref[pl.ds(n * 8, 8), :128] = acc
        out_ref[pl.ds(n * 8, 8), 128:] = jnp.where(lane128 == 0, m, den)


def resident(g, clen, queries, codes, ks, vs):
    return pl.pallas_call(
        resident_kernel,
        out_shape=jax.ShapeDtypeStruct((128, 256), F32),
        grid_spec=pltpu.PrefetchScalarGridSpec(
            num_scalar_prefetch=1,
            grid=(4,),
            in_specs=[
                pl.BlockSpec((1, 4, 8, 128), lambda i, s: (g, i, 0, 0)),
                pl.BlockSpec((1, 4, 1, 256, 256), lambda i, s: (g, i, 0, 0, 0)),
                pl.BlockSpec((1, 1, 4, 256), lambda i, s: (g, i, 0, 0)),
                pl.BlockSpec((1, 1, 4, 256), lambda i, s: (g, i, 0, 0)),
            ],
            out_specs=pl.BlockSpec((32, 256), lambda i, s: (i, 0)),
        ),
        compiler_params=pltpu.CompilerParams(vmem_limit_bytes=16 * 1024 * 1024),
        cost_estimate=pl.CostEstimate(flops=200_000_000, bytes_accessed=2_200_000, transcendentals=0),
    )(clen[g], queries, codes, ks, vs)


def group_max(v):
    lane = lax.broadcasted_iota(jnp.int32, v.shape, 1)
    n = v.shape[1]
    for s in (1, 2, 4, 8):
        other = jnp.where((lane & s) == 0, pltpu.roll(v, n - s, 1), pltpu.roll(v, s, 1))
        v = jnp.maximum(v, other)
    return v


def quantize(kv):
    largest = group_max(jnp.max(jnp.abs(kv), axis=0, keepdims=True))
    scale = (largest + 1e-6) / 127.0
    return (kv / scale).astype(BF16), scale


def block_kernel(core_ref, *refs):
    wa, wb, p, (q0, q1, q2, q3, out_ref) = refs[:4], refs[4:8], refs[8:17], refs[17:]
    feats = p[0].shape[0] // 4
    kv = None
    for k in range(4):
        rows = [p[s][pl.ds(k * feats, feats), :] for s in range(7)]
        rows.append(p[7 + k // 2][pl.ds((k % 2) * feats, feats), :])
        weight = jnp.concatenate([wa[k][...], wb[k][...]], axis=0)
        term = dot(weight, jnp.concatenate(rows, axis=0), 1, 0)
        kv = term if kv is None else kv + term
    first = core_ref[0] == 0
    key_codes, key_scale = quantize(jnp.where(first, kv[:128], kv[128:]))
    value_codes, value_scale = quantize(jnp.where(first, kv[128:], kv[:128]))
    q = q0[...] + q1[...] + q2[...] + q3[...]
    s = dot(q, key_codes, 0, 0) * (key_scale * (128.0**-0.5))
    row = lax.broadcasted_iota(jnp.int32, s.shape, 0)
    lane = lax.broadcasted_iota(jnp.int32, s.shape, 1)
    inside = (row >> 3) == (lane >> 4)
    s = jnp.where(inside, s, -jnp.inf)
    m = jnp.max(s, axis=1, keepdims=True)
    e = jnp.exp(s - m)
    den = jnp.sum(e, axis=1, keepdims=True)
    acc = dot((e * value_scale).astype(BF16), value_codes, 1, 1)
    stats = pack_columns(three(m) + three(den))
    out_ref[pl.ds(0, 128), :] = jnp.transpose(acc).astype(BF16)
    out_ref[pl.ds(128, 16), :] = jnp.transpose(stats)[:16].astype(BF16)


def pack_columns(columns):
    lane = lax.broadcasted_iota(jnp.int32, (columns[0].shape[0], 128), 1)
    out = jnp.zeros(lane.shape, F32)
    for i, c in enumerate(columns):
        out = jnp.where(lane == i, c, out)
    return out


def pack_rows(rows, height):
    sub = lax.broadcasted_iota(jnp.int32, (height, rows[0].shape[1]), 0)
    out = jnp.zeros(sub.shape, F32)
    for i, c in enumerate(rows):
        out = jnp.where(sub == i, c, out)
    return out


def join_kernel(code_ref, *refs):
    parts, out_ref = refs[:8], refs[8]
    stats = jnp.concatenate([r[pl.ds(128, 16), :].astype(F32) for r in parts], axis=0)
    columns = jnp.transpose(stats)
    codes = jnp.transpose(jnp.concatenate([code_ref[...].astype(F32), jnp.zeros((120, 128), F32)], axis=0))
    lane = lax.broadcasted_iota(jnp.int32, (128, 384), 1).astype(F32)
    top = jnp.full((1, 384), LOW, F32)
    joined, tops = [], []
    for b in range(8):
        c = [columns[:, b * 16 + i : b * 16 + i + 1] for i in range(6)]
        m = (c[0] + c[1]) + c[2]
        hit = codes[:, b : b + 1] == lane
        top = jnp.maximum(top, jnp.max(jnp.where(hit, m, LOW), axis=0, keepdims=True))
        joined.append(hit)
        tops.append((m, (c[3] + c[4]) + c[5]))
    den = jnp.zeros((1, 384), F32)
    acc = jnp.zeros((128, 384), F32)
    for b in range(8):
        m, d = tops[b]
        share = jnp.exp(jnp.where(joined[b], m - top, -jnp.inf))
        den = den + jnp.sum(share * d, axis=0, keepdims=True)
        acc = acc + dot(parts[b][pl.ds(0, 128), :], share.astype(BF16), 1, 0)
    out_ref[pl.ds(0, 128), :] = acc.astype(BF16)
    out_ref[pl.ds(128, 16), :] = pack_rows(three(top) + three(den), 16).astype(BF16)


def final_kernel(u0, u1, u2, u3, r0, r1, r2, out_ref, tmp):
    us = (u0, u1, u2, u3)
    tops, dens = [], []
    for u in us:
        rows = [u[pl.ds(128, 16), :].astype(F32)[i : i + 1] for i in range(6)]
        tops.append((rows[0] + rows[1]) + rows[2])
        dens.append((rows[3] + rows[4]) + rows[5])
    top = jnp.maximum(jnp.maximum(tops[0], tops[1]), jnp.maximum(tops[2], tops[3]))
    acc = jnp.zeros((128, 384), F32)
    den = jnp.zeros((1, 384), F32)
    for u, m, d in zip(us, tops, dens):
        share = jnp.exp(m - top)
        acc = acc + u[pl.ds(0, 128), :].astype(F32) * share
        den = den + d * share
    acc = jnp.transpose(acc)
    columns = jnp.transpose(pack_rows((top, den), 128))
    for g, r in enumerate((r0, r1, r2)):
        rows = slice(g * 128, g * 128 + 128)
        new_top, new_den = columns[rows, 0:1], columns[rows, 1:2]
        old_top, old_den = r[:, 128:129], r[:, 129:130]
        best = jnp.maximum(new_top, old_top)
        new_share, old_share = jnp.exp(new_top - best), jnp.exp(old_top - best)
        total = new_den * new_share + old_den * old_share
        tmp[pl.ds(g * 128, 128), :] = (acc[rows] * new_share + r[:, :128] * old_share) / total
    for q in range(8):
        out_ref[:, q * 128 : q * 128 + 128] = tmp[pl.ds(q, 48, stride=8), :].astype(BF16)


def shape(*dims, dtype=BF16):
    return jax.ShapeDtypeStruct(dims, dtype)


def role_shift(v, d):
    return lax.ppermute(v, "role", [(i, (i + d) % 4) for i in range(4)])


def x_shift(v, d):
    return lax.ppermute(v, "tensor", [(z * 4 + x, z * 4 + (x + d) % 4) for z in range(2) for x in range(4)])


def z_swap(v):
    return lax.ppermute(v, "tensor", [(t, (t + 4) % 8) for t in range(8)])


def zh_shift(v, d):
    return lax.ppermute(v, "batch", [(i, (i + 2 * d) % 8) for i in range(8)])


def core_swap(v):
    return lax.ppermute(v, "batch", [(i, i ^ 1) for i in range(8)])


def body(span, weight, queries, codes, scales, clen, bdest, brow):
    role = lax.axis_index("role")
    batch = lax.axis_index("batch")
    tensor = lax.axis_index("tensor")
    zh, core = batch // 2, batch % 2
    zl, x = tensor // 4, tensor % 4
    role1, core1 = role.reshape(1), core.reshape(1)
    tokens, feats = span.shape[0] // 4, span.shape[1]

    cut = call(cut_kernel, [shape(feats, tokens)] * 4, (role1, span), [SMEM, VMEM])
    own = jnp.concatenate([cut[0]] + [role_shift(cut[d], d) for d in (1, 2, 3)], axis=0)

    near = [(0, 0), (-1, 0), (1, 0), (0, 1), (2, 0), (1, 1), (-1, 1), (2, 1)]
    slots = jnp.stack([((zl + b) % 2) * 4 + (x + a) % 4 for a, b in near])
    half = [shape(128, weight.shape[0])] * 2
    wa0, wb0 = call(
        weight_kernel, half, (slots, core1, weight.reshape(weight.shape[0], 256)), [SMEM, SMEM, VMEM],
        scratch=[pltpu.VMEM((weight.shape[0], 256), F32)],
    )
    wa = [wa0] + [role_shift(wa0, d) for d in (1, 2, 3)]
    wb = [wb0] + [core_swap(v) for v in wa[1:]]

    dest = lax.dynamic_index_in_dim(bdest[:, 0].reshape(8, 4, 16), role, 1, keepdims=False)
    row = lax.dynamic_index_in_dim(brow.reshape(8, 4, 16), role, 1, keepdims=False)
    request = jnp.where(dest % 8 == batch, (dest // 8) * 16 + row, -1)
    lanes = jnp.repeat(request, 8, axis=1)
    lanes = jnp.where(lanes < 0, -1, lanes * 8 + jnp.arange(128, dtype=jnp.int32)[None, :] % 8)
    mine = jnp.stack([((zh + d) % 4) * 2 + core for d in range(4)])
    theirs = mine + 1 - 2 * core
    out_codes = lanes[jnp.concatenate([mine, theirs])]
    flat = queries.reshape(384, 128)
    q_own, q_oth = call(pick_kernel, [shape(4, 128, 128)] * 2, (out_codes, flat), [VMEM, VMEM])
    q_sum = call(add_kernel, [shape(128, 128)] * 4, (q_own, core_swap(q_oth)), [VMEM, VMEM])
    q_in = [q_sum[0]] + [zh_shift(q_sum[d], d) for d in (1, 2, 3)]

    ks = jnp.repeat(scales[:, :, 0, :, 0], BLOCK, axis=2).reshape(3, 4, 4, 256)
    vs = jnp.repeat(scales[:, :, 0, :, 1], BLOCK, axis=2).reshape(3, 4, 4, 256)
    res = [resident(g, clen, queries, codes, ks, vs) for g in range(3)]

    p1, p2, p3 = x_shift(own, 1), x_shift(own, -1), z_swap(own)
    p4, p5, p6 = x_shift(p1, 1), x_shift(p3, -1), z_swap(p1)
    cutoff = p6.shape[0] // 2
    p7a, p7b = x_shift(p6[:cutoff], 1), x_shift(p5[cutoff:], -1)

    blocks = call(
        block_kernel, shape(144, 128), (core1, *wa, *wb, own, p1, p2, p3, p4, p5, p6, p7a, p7b, *q_in),
        [SMEM] + [VMEM] * 21,
    )

    parts = [blocks] + [zh_shift(blocks, d) for d in (1, 2, 3)]
    parts = parts + [core_swap(v) for v in parts]
    origin = jnp.stack([((zh - d) % 4) * 2 + core for d in range(4)])
    in_codes = lanes[jnp.concatenate([origin, origin + 1 - 2 * core])]
    sums = call(join_kernel, shape(144, 384), (in_codes, *parts), [VMEM] * 9)
    sums = [sums] + [role_shift(sums, d) for d in (1, 2, 3)]
    out = call(
        final_kernel, shape(48, 1024), (*sums, *res), [VMEM] * 7, scratch=[pltpu.VMEM((384, 128), F32)]
    )
    return out.reshape(3, 16, 1024)


def solution(mesh):
    return jax.shard_map(
        body,
        mesh=mesh,
        in_specs=(
            P("batch", ("role", "tensor")),
            P("role", "tensor", None),
            P(None, "batch", "tensor", None),
            P(None, "batch", "tensor", None, None),
            P(None, "batch", "tensor", None, None),
            P(None, "batch"),
            P(),
            P(),
        ),
        out_specs=P(None, "batch", "tensor"),
        check_vma=False,
    )
```

time: 200 us -> 108 us (0.54)
  waiting for transfers between devices: 134 us -> 27 us
  starting transfers between devices: 0.08 us -> 45.7 us
  blocking collectives: 25.1 us -> 0 us
  Pallas kernels: 0 us -> 20.1 us
  between operations: 13.3 us -> 0.41 us
  matrix products: 12.1 us -> 0 us
  other arithmetic: 8.63 us -> 1.52 us
  local copies, waits for them, and re-layouts: 6.15 us -> 12.8 us
    all_gather x2 -> x0, waiting for transfers between devices: 84 us -> none  [the longest x1 48.1 us: body(): lax.all_gather(span, 'tensor', axis=1, tiled=True)]
    psum x1 -> x0, waiting for transfers between devices: 49.3 us -> none  [body(): lax.psum(partial_rows.astype(jnp.bfloat16), 'role').astype(jnp.float32)]
    ppermute x0 -> x31, starting transfers between devices: none -> 45.7 us  [the longest x6 20.6 us: zh_shift(): return lax.ppermute(v, 'batch', [(i, (i + 2 * d) % 8) for i in range(8)])]
    ppermute x0 -> x31, waiting for transfers between devices: none -> 27 us  [the longest x6 12.7 us: x_shift(): lax.ppermute(v, 'tensor', [(z * 4 + x, z * 4 + (x + d) % 4) for z in rang...]
    all_gather x2 -> x0, blocking collectives: 25.1 us -> none  [the longest x1 12.8 us: body(): lax.all_gather(block_scales.astype(jnp.bfloat16), 'batch', axis=0, tiled=...]
    pallas_call x0 -> x10, Pallas kernels: none -> 20.1 us  [the longest x3 14.3 us: resident(): pl.pallas_call(resident_kernel, out_shape=jax.ShapeDtypeStruct((128, 256)...]
    dot_general x5 -> x0, matrix products: 12.1 us -> none  [the longest x1 4.27 us: attend(): jnp.einsum('rhgd,shtd->rhgst', grouped, new_codes[..., :head_size], prefe...]
    unnamed x9 -> x19, local copies, waits for them, and re-layouts: 0.03 us -> 9.39 us
  transfers between devices with their start and end apart: 3 -> 31, of which waited for: 3 -> 14; matrix products, arithmetic and copies ran while one was open for 3% -> 5% of each run, Pallas kernels for 0% -> 14%
where the time goes in v1:
time: 108 us
  starting transfers between devices  45.7 us (42%)
  waiting for transfers between devices  27 us (25%)
  Pallas kernels  20.1 us (19%)
  local copies, waits for them, and re-layouts  12.8 us (12%)
  other arithmetic  1.52 us (1%)
    ppermute x6, starting transfers between devices, zh_shift(): return lax.ppermute(v, 'batch', [(i, (i + 2 * d) % 8) for i in range(8)])  20.6 us
    ppermute x9, starting transfers between devices, role_shift(): return lax.ppermute(v, 'role', [(i, (i + d) % 4) for i in range(4)])  16.6 us
    pallas_call x3, Pallas kernels, resident(): pl.pallas_call(resident_kernel, out_shape=jax.ShapeDtypeStruct((128, 256)...  14.3 us
    ppermute x6, waiting for transfers between devices, x_shift(): lax.ppermute(v, 'tensor', [(z * 4 + x, z * 4 + (x + d) % 4) for z in rang...  12.7 us
    ppermute x6, waiting for transfers between devices, zh_shift(): return lax.ppermute(v, 'batch', [(i, (i + 2 * d) % 8) for i in range(8)])  9.61 us
    unnamed x19, local copies, waits for them, and re-layouts  9.39 us
    pallas_call x7, Pallas kernels, call(): pl.pallas_call(kernel, out_shape=outs, in_specs=specs, out_specs=jax.tree...  5.73 us
    ppermute x6, starting transfers between devices, x_shift(): lax.ppermute(v, 'tensor', [(z * 4 + x, z * 4 + (x + d) % 4) for z in rang...  5.24 us
  transfers between devices with their start and end apart: 31, of which 14 were waited for; matrix products, arithmetic and copies ran while one was open for 5% of the time, Pallas kernels for 14%

profile of v1, /device:TPU:6, one launch (start us, length us, event | category | flops | bytes accessed | tf_op | source)
XLA Modules:
  0.0 107.6 jit_solution(4391308632486580552)
XLA Ops:
  1.4 1.7 %collective-permute-start.6 = (bf16[160,256]{1,0:T(8,128)(2,1)S(1)}, bf16[160,256]{1,0:T(8,128)(2,1)S(1)}, u32[]{:S(2)}, u32[]{:S(2)}) collective-permute-start(bf16[160,256]{1,0:T(8,128)(2,1)S(1)} %get-tuple-element.20), channel_id=1, source_target_pairs={{0,64},{64,128},{128,192},{192,0},{1,65},{65,129},{129,193},{193,1... | collective-permute-start | bytes 245768 | tf_op jit(solution)/shard_map/ppermute | solution.py:235
  3.1 2.9 %collective-permute-start.7 = (bf16[160,256]{1,0:T(8,128)(2,1)S(1)}, bf16[160,256]{1,0:T(8,128)(2,1)S(1)}, u32[]{:S(2)}, u32[]{:S(2)}) collective-permute-start(bf16[160,256]{1,0:T(8,128)(2,1)S(1)} %get-tuple-element.21), channel_id=1, source_target_pairs={{0,128},{64,192},{128,0},{192,64},{1,129},{65,193},{129,1},{193,65... | collective-permute-start | bytes 245768 | tf_op jit(solution)/shard_map/ppermute | solution.py:235
  6.0 1.3 %collective-permute-start.8 = (bf16[160,256]{1,0:T(8,128)(2,1)S(1)}, bf16[160,256]{1,0:T(8,128)(2,1)S(1)}, u32[]{:S(2)}, u32[]{:S(2)}) collective-permute-start(bf16[160,256]{1,0:T(8,128)(2,1)S(1)} %get-tuple-element.22), channel_id=1, source_target_pairs={{0,192},{64,0},{128,64},{192,128},{1,193},{65,1},{129,65},{193,129... | collective-permute-start | bytes 245768 | tf_op jit(solution)/shard_map/ppermute | solution.py:235
  7.9 1.3 %reduce.3 = s32[512]{0:T(512)S(1)} reduce(s32[512,1]{0,1:T(1,128)} %param.14, s32[]{:T(128)} %broadcast.173), dimensions={1}, to_apply=%param.14.reduce_sub_computation.3 | reduce | bytes 4100 | tf_op args[6]
  11.6 1.9 %collective-permute-start.11 = (bf16[640,256]{1,0:T(8,128)(2,1)S(1)}, bf16[640,256]{1,0:T(8,128)(2,1)S(1)}, u32[]{:S(2)}, u32[]{:S(2)}) collective-permute-start(bf16[640,256]{1,0:T(8,128)(2,1)S(1)} %constant_dynamic-update-slice_fusion.refs_8_), channel_id=1, source_target_pairs={{0,4},{1,5},{2,6},{3,7},{4,0},{5,1},{6,2},{7,3},{8,12},{9,13},{10,... | collective-permute-start | bytes 983048 | tf_op jit(solution)/shard_map/ppermute | solution.py:243
  18.3 2.7 %collective-permute-start.1 = (bf16[128,1280]{1,0:T(8,128)(2,1)S(1)}, bf16[128,1280]{1,0:T(8,128)(2,1)S(1)}, u32[]{:S(2)}, u32[]{:S(2)}) collective-permute-start(bf16[128,1280]{1,0:T(8,128)(2,1)S(1)} %get-tuple-element.17.refs_0_), channel_id=1, source_target_pairs={{0,128},{64,192},{128,0},{192,64},{1,129},{65,193},{129,1},{193,65... | collective-permute-start | bytes 983048 | tf_op jit(solution)/shard_map/ppermute | solution.py:235
  21.1 3.3 %collective-permute-start.18 = (bf16[128,128]{1,0:T(8,128)(2,1)S(1)}, bf16[128,128]{1,0:T(8,128)(2,1)S(1)}, u32[]{:S(2)}, u32[]{:S(2)}) collective-permute-start(bf16[128,128]{1,0:T(8,128)(2,1)S(1)} %get-tuple-element.26), channel_id=1, source_target_pairs={{0,16},{8,24},{16,32},{24,40},{32,48},{40,56},{48,0},{56,8},{1,17}... | collective-permute-start | bytes 98312 | tf_op jit(solution)/shard_map/ppermute | solution.py:247
  24.4 4.0 %collective-permute-done.18.refs_18_ = bf16[128,128]{1,0:T(8,128)(2,1)S(1)} collective-permute-done((bf16[128,128]{1,0:T(8,128)(2,1)S(1)}, bf16[128,128]{1,0:T(8,128)(2,1)S(1)}, u32[]{:S(2)}, u32[]{:S(2)}) %collective-permute-start.18) | collective-permute-done | bytes 32800 | tf_op jit(solution)/shard_map/ppermute | solution.py:247
  28.4 5.0 %collective-permute-start.19 = (bf16[128,128]{1,0:T(8,128)(2,1)S(1)}, bf16[128,128]{1,0:T(8,128)(2,1)S(1)}, u32[]{:S(2)}, u32[]{:S(2)}) collective-permute-start(bf16[128,128]{1,0:T(8,128)(2,1)S(1)} %get-tuple-element.27), channel_id=1, source_target_pairs={{0,32},{8,40},{16,48},{24,56},{32,0},{40,8},{48,16},{56,24},{1,33}... | collective-permute-start | bytes 98312 | tf_op jit(solution)/shard_map/ppermute | solution.py:247
  33.5 2.8 %collective-permute-done.19.refs_19_ = bf16[128,128]{1,0:T(8,128)(2,1)S(1)} collective-permute-done((bf16[128,128]{1,0:T(8,128)(2,1)S(1)}, bf16[128,128]{1,0:T(8,128)(2,1)S(1)}, u32[]{:S(2)}, u32[]{:S(2)}) %collective-permute-start.19) | collective-permute-done | bytes 32800 | tf_op jit(solution)/shard_map/ppermute | solution.py:247
  36.3 3.0 %collective-permute-start.20 = (bf16[128,128]{1,0:T(8,128)(2,1)S(1)}, bf16[128,128]{1,0:T(8,128)(2,1)S(1)}, u32[]{:S(2)}, u32[]{:S(2)}) collective-permute-start(bf16[128,128]{1,0:T(8,128)(2,1)S(1)} %get-tuple-element.28), channel_id=1, source_target_pairs={{0,48},{8,56},{16,0},{24,8},{32,16},{40,24},{48,32},{56,40},{1,49}... | collective-permute-start | bytes 98312 | tf_op jit(solution)/shard_map/ppermute | solution.py:247
  39.3 1.8 %collective-permute-done.20.refs_20_ = bf16[128,128]{1,0:T(8,128)(2,1)S(1)} collective-permute-done((bf16[128,128]{1,0:T(8,128)(2,1)S(1)}, bf16[128,128]{1,0:T(8,128)(2,1)S(1)}, u32[]{:S(2)}, u32[]{:S(2)}) %collective-permute-start.20) | collective-permute-done | bytes 32800 | tf_op jit(solution)/shard_map/ppermute | solution.py:247
  42.8 1.5 %collective-permute-start.13 = (bf16[640,256]{1,0:T(8,128)(2,1)S(1)}, bf16[640,256]{1,0:T(8,128)(2,1)S(1)}, u32[]{:S(2)}, u32[]{:S(2)}) collective-permute-start(bf16[640,256]{1,0:T(8,128)(2,1)S(1)} %collective-permute-done.11.refs_11_), channel_id=1, source_target_pairs={{0,3},{1,0},{2,1},{3,2},{4,7},{5,4},{6,5},{7,6},{8,11},{9,8},{10,9... | collective-permute-start | bytes 983048 | tf_op jit(solution)/shard_map/ppermute | solution.py:239
  45.2 3.0 %collective-permute-done.2.refs_3_ = bf16[128,1280]{1,0:T(8,128)(2,1)S(1)} collective-permute-done((bf16[128,1280]{1,0:T(8,128)(2,1)S(1)}, bf16[128,1280]{1,0:T(8,128)(2,1)S(1)}, u32[]{:S(2)}, u32[]{:S(2)}) %collective-permute-start.2) | collective-permute-done | bytes 327712 | tf_op jit(solution)/shard_map/ppermute | solution.py:235
  49.5 3.9 %collective-permute-done.13.refs_13_ = bf16[640,256]{1,0:T(8,128)(2,1)S(1)} collective-permute-done((bf16[640,256]{1,0:T(8,128)(2,1)S(1)}, bf16[640,256]{1,0:T(8,128)(2,1)S(1)}, u32[]{:S(2)}, u32[]{:S(2)}) %collective-permute-start.13) | collective-permute-done | bytes 327712 | tf_op jit(solution)/shard_map/ppermute | solution.py:239
  53.7 3.7 %collective-permute-done.10.refs_10_ = bf16[640,256]{1,0:T(8,128)(2,1)S(1)} collective-permute-done((bf16[640,256]{1,0:T(8,128)(2,1)S(1)}, bf16[640,256]{1,0:T(8,128)(2,1)S(1)}, u32[]{:S(2)}, u32[]{:S(2)}) %collective-permute-start.10) | collective-permute-done | bytes 327712 | tf_op jit(solution)/shard_map/ppermute | solution.py:239
  58.0 1.5 %collective-permute-start.16 = (bf16[320,256]{1,0:T(8,128)(2,1)S(1)}, bf16[320,256]{1,0:T(8,128)(2,1)S(1)}, u32[]{:S(2)}, u32[]{:S(2)}) collective-permute-start(bf16[320,256]{1,0:T(8,128)(2,1)S(1)} %slice.33), channel_id=1, source_target_pairs={{0,3},{1,0},{2,1},{3,2},{4,7},{5,4},{6,5},{7,6},{8,11},{9,8},{10,9... | collective-permute-start | bytes 491528 | tf_op jit(solution)/shard_map/ppermute | solution.py:239
  59.5 1.9 %collective-permute-done.12.refs_12_ = bf16[640,256]{1,0:T(8,128)(2,1)S(1)} collective-permute-done((bf16[640,256]{1,0:T(8,128)(2,1)S(1)}, bf16[640,256]{1,0:T(8,128)(2,1)S(1)}, u32[]{:S(2)}, u32[]{:S(2)}) %collective-permute-start.12) | collective-permute-done | bytes 327712 | tf_op jit(solution)/shard_map/ppermute | solution.py:239
  61.4 1.8 %collective-permute-done.15.refs_15_ = bf16[320,256]{1,0:T(8,128)(2,1)S(1)} collective-permute-done((bf16[320,256]{1,0:T(8,128)(2,1)S(1)}, bf16[320,256]{1,0:T(8,128)(2,1)S(1)}, u32[]{:S(2)}, u32[]{:S(2)}) %collective-permute-start.15) | collective-permute-done | bytes 163872 | tf_op jit(solution)/shard_map/ppermute | solution.py:239
  63.1 1.4 %collective-permute-done.16.refs_16_ = bf16[320,256]{1,0:T(8,128)(2,1)S(1)} collective-permute-done((bf16[320,256]{1,0:T(8,128)(2,1)S(1)}, bf16[320,256]{1,0:T(8,128)(2,1)S(1)}, u32[]{:S(2)}, u32[]{:S(2)}) %collective-permute-start.16) | collective-permute-done | bytes 163872 | tf_op jit(solution)/shard_map/ppermute | solution.py:239
  64.5 1.7 %shard_map.86.refs_0_ = bf16[144,128]{1,0:T(8,128)(2,1)S(1)} custom-call(s32[1]{0:T(128)} %bitcast.12.core_ref, bf16[128,1280]{1,0:T(8,128)(2,1)S(1)} %get-tuple-element.17.refs_0_, bf16[128,1280]{1,0:T(8,128)(2,1)S(1)} %collective-permute-done.refs_1_, bf16[128,1280]{1,0:T(8,128)(2,1)S(1)} %collective-permute-done.1.refs_2_, ...), custom_call_target="tpu_custom_call" | custom-call | tf_op jit(solution)/shard_map/pallas_call | solution.py:17
  66.2 2.7 %collective-permute-start.21 = (bf16[144,128]{1,0:T(8,128)(2,1)S(1)}, bf16[144,128]{1,0:T(8,128)(2,1)S(1)}, u32[]{:S(2)}, u32[]{:S(2)}) collective-permute-start(bf16[144,128]{1,0:T(8,128)(2,1)S(1)} %shard_map.86.refs_0_), channel_id=1, source_target_pairs={{0,16},{8,24},{16,32},{24,40},{32,48},{40,56},{48,0},{56,8},{1,17}... | collective-permute-start | bytes 110600 | tf_op jit(solution)/shard_map/ppermute | solution.py:247
  68.9 2.9 %collective-permute-start.22 = (bf16[144,128]{1,0:T(8,128)(2,1)S(1)}, bf16[144,128]{1,0:T(8,128)(2,1)S(1)}, u32[]{:S(2)}, u32[]{:S(2)}) collective-permute-start(bf16[144,128]{1,0:T(8,128)(2,1)S(1)} %shard_map.86.refs_0_), channel_id=1, source_target_pairs={{0,32},{8,40},{16,48},{24,56},{32,0},{40,8},{48,16},{56,24},{1,33}... | collective-permute-start | bytes 110600 | tf_op jit(solution)/shard_map/ppermute | solution.py:247
  71.8 3.6 %collective-permute-start.23 = (bf16[144,128]{1,0:T(8,128)(2,1)S(1)}, bf16[144,128]{1,0:T(8,128)(2,1)S(1)}, u32[]{:S(2)}, u32[]{:S(2)}) collective-permute-start(bf16[144,128]{1,0:T(8,128)(2,1)S(1)} %shard_map.86.refs_0_), channel_id=1, source_target_pairs={{0,48},{8,56},{16,0},{24,8},{32,16},{40,24},{48,32},{56,40},{1,49}... | collective-permute-start | bytes 110600 | tf_op jit(solution)/shard_map/ppermute | solution.py:247
  79.5 2.1 %collective-permute-start.28 = (bf16[144,384]{1,0:T(8,128)(2,1)S(1)}, bf16[144,384]{1,0:T(8,128)(2,1)S(1)}, u32[]{:S(2)}, u32[]{:S(2)}) collective-permute-start(bf16[144,384]{1,0:T(8,128)(2,1)S(1)} %shard_map.87.u0), channel_id=1, source_target_pairs={{0,64},{64,128},{128,192},{192,0},{1,65},{65,129},{129,193},{193,1... | collective-permute-start | bytes 331784 | tf_op jit(solution)/shard_map/ppermute | solution.py:235
  82.9 2.5 %collective-permute-start.30 = (bf16[144,384]{1,0:T(8,128)(2,1)S(1)}, bf16[144,384]{1,0:T(8,128)(2,1)S(1)}, u32[]{:S(2)}, u32[]{:S(2)}) collective-permute-start(bf16[144,384]{1,0:T(8,128)(2,1)S(1)} %shard_map.87.u0), channel_id=1, source_target_pairs={{0,192},{64,0},{128,64},{192,128},{1,193},{65,1},{129,65},{193,129... | collective-permute-start | bytes 331784 | tf_op jit(solution)/shard_map/ppermute | solution.py:235
  86.2 2.8 %copy-done = bf16[3,16,1,256,256]{4,3,2,1,0:T(8,128)(2,1)S(1)} copy-done((bf16[3,16,1,256,256]{4,3,2,1,0:T(8,128)(2,1)S(1)}, bf16[3,16,1,256,256]{4,3,2,1,0:T(8,128)(2,1)}, u32[]{:S(2)}) %copy-start) | copy-done | bytes 6291480
  89.0 4.8 %shard_map.88.r0 = f32[128,256]{1,0:T(8,128)S(1)} custom-call(s32[16]{0:T(128)S(1)} %get-tuple-element.34.len_ref, bf16[3,16,8,128]{3,2,1,0:T(8,128)(2,1)S(1)} %copy-done.3, bf16[3,16,1,256,256]{4,3,2,1,0:T(8,128)(2,1)S(1)} %copy-done, f32[3,4,4,256]{3,2,1,0:T(4,128)S(1)} %reshape_reshape.6.ks_ref, f32[3,4,4,256]{3,2,1,0:T(4,128)S(1)} %reshape_reshape.7.vs_ref), custom_call_target="tpu_custom_call" | custom-call | flops 200000000 | bytes 2200000 | tf_op jit(solution)/shard_map/pallas_call | solution.py:98
  93.8 2.8 %copy-done.1 = bf16[3,16,1,256,256]{4,3,2,1,0:T(8,128)(2,1)S(1)} copy-done((bf16[3,16,1,256,256]{4,3,2,1,0:T(8,128)(2,1)S(1)}, bf16[3,16,1,256,256]{4,3,2,1,0:T(8,128)(2,1)}, u32[]{:S(2)}) %copy-start.1) | copy-done | bytes 6291480
  96.6 4.8 %shard_map.89.r1 = f32[128,256]{1,0:T(8,128)S(1)} custom-call(s32[16]{0:T(128)S(1)} %get-tuple-element.35.len_ref, bf16[3,16,8,128]{3,2,1,0:T(8,128)(2,1)S(1)} %copy-done.3, bf16[3,16,1,256,256]{4,3,2,1,0:T(8,128)(2,1)S(1)} %copy-done.1, f32[3,4,4,256]{3,2,1,0:T(4,128)S(1)} %reshape_reshape.6.ks_ref, f32[3,4,4,256]{3,2,1,0:T(4,128)S(1)} %reshape_reshape.7.vs_ref), custom_call_target="tpu_custom_call" | custom-call | flops 200000000 | bytes 2200000 | tf_op jit(solution)/shard_map/pallas_call | solution.py:98
  101.3 4.8 %shard_map.90.r2 = f32[128,256]{1,0:T(8,128)S(1)} custom-call(s32[16]{0:T(128)S(1)} %get-tuple-element.33.len_ref, bf16[3,16,8,128]{3,2,1,0:T(8,128)(2,1)S(1)} %copy-done.3, bf16[3,16,1,256,256]{4,3,2,1,0:T(8,128)(2,1)S(1)} %copy-done.1, f32[3,4,4,256]{3,2,1,0:T(4,128)S(1)} %reshape_reshape.6.ks_ref, f32[3,4,4,256]{3,2,1,0:T(4,128)S(1)} %reshape_reshape.7.vs_ref), custom_call_target="tpu_custom_call" | custom-call | flops 200000000 | bytes 2200000 | tf_op jit(solution)/shard_map/pallas_call | solution.py:98
  106.2 1.4 %shard_map.91 = bf16[48,1024]{1,0:T(8,128)(2,1)} custom-call(bf16[144,384]{1,0:T(8,128)(2,1)S(1)} %shard_map.87.u0, bf16[144,384]{1,0:T(8,128)(2,1)S(1)} %collective-permute-done.28.u1, bf16[144,384]{1,0:T(8,128)(2,1)S(1)} %collective-permute-done.29.u2, bf16[144,384]{1,0:T(8,128)(2,1)S(1)} %collective-permute-done.30.u3, f32[128,256]{1,0:T(8,128)S(1)} %shard_map.88.r0, ...), custom_call_target="tpu_custom_call" | custom-call | tf_op jit(solution)/shard_map/pallas_call | solution.py:17
  (90 shorter events, 19.8 us)
Async XLA Ops:
  0.0 86.2 %copy-start.3 = (bf16[3,16,8,128]{3,2,1,0:T(8,128)(2,1)S(1)}, bf16[3,16,8,128]{3,2,1,0:T(8,128)(2,1)}, u32[]{:S(2)}) copy-start(bf16[3,16,8,128]{3,2,1,0:T(8,128)(2,1)} %q_ref.5) | copy-start | bytes 294916
  1.4 9.5 %collective-permute-start.6 = (bf16[160,256]{1,0:T(8,128)(2,1)S(1)}, bf16[160,256]{1,0:T(8,128)(2,1)S(1)}, u32[]{:S(2)}, u32[]{:S(2)}) collective-permute-start(bf16[160,256]{1,0:T(8,128)(2,1)S(1)} %get-tuple-element.20), channel_id=1, source_target_pairs={{0,64},{64,128},{128,192},{192,0},{1,65},{65,129},{129,193},{193,1... | collective-permute-start | bytes 245768 | tf_op jit(solution)/shard_map/ppermute | solution.py:235
  3.1 7.8 %collective-permute-start.7 = (bf16[160,256]{1,0:T(8,128)(2,1)S(1)}, bf16[160,256]{1,0:T(8,128)(2,1)S(1)}, u32[]{:S(2)}, u32[]{:S(2)}) collective-permute-start(bf16[160,256]{1,0:T(8,128)(2,1)S(1)} %get-tuple-element.21), channel_id=1, source_target_pairs={{0,128},{64,192},{128,0},{192,64},{1,129},{65,193},{129,1},{193,65... | collective-permute-start | bytes 245768 | tf_op jit(solution)/shard_map/ppermute | solution.py:235
  6.0 5.0 %collective-permute-start.8 = (bf16[160,256]{1,0:T(8,128)(2,1)S(1)}, bf16[160,256]{1,0:T(8,128)(2,1)S(1)}, u32[]{:S(2)}, u32[]{:S(2)}) collective-permute-start(bf16[160,256]{1,0:T(8,128)(2,1)S(1)} %get-tuple-element.22), channel_id=1, source_target_pairs={{0,192},{64,0},{128,64},{192,128},{1,193},{65,1},{129,65},{193,129... | collective-permute-start | bytes 245768 | tf_op jit(solution)/shard_map/ppermute | solution.py:235
  11.0 31.4 %collective-permute-start.9 = (bf16[640,256]{1,0:T(8,128)(2,1)S(1)}, bf16[640,256]{1,0:T(8,128)(2,1)S(1)}, u32[]{:S(2)}, u32[]{:S(2)}) collective-permute-start(bf16[640,256]{1,0:T(8,128)(2,1)S(1)} %constant_dynamic-update-slice_fusion.refs_8_), channel_id=1, source_target_pairs={{0,1},{1,2},{2,3},{3,0},{4,5},{5,6},{6,7},{7,4},{8,9},{9,10},{10,1... | collective-permute-start | bytes 983048 | tf_op jit(solution)/shard_map/ppermute | solution.py:239
  11.6 31.3 %collective-permute-start.11 = (bf16[640,256]{1,0:T(8,128)(2,1)S(1)}, bf16[640,256]{1,0:T(8,128)(2,1)S(1)}, u32[]{:S(2)}, u32[]{:S(2)}) collective-permute-start(bf16[640,256]{1,0:T(8,128)(2,1)S(1)} %constant_dynamic-update-slice_fusion.refs_8_), channel_id=1, source_target_pairs={{0,4},{1,5},{2,6},{3,7},{4,0},{5,1},{6,2},{7,3},{8,12},{9,13},{10,... | collective-permute-start | bytes 983048 | tf_op jit(solution)/shard_map/ppermute | solution.py:243
  15.3 5.7 %collective-permute-start.17 = (bf16[4,128,128]{2,1,0:T(8,128)(2,1)S(1)}, bf16[4,128,128]{2,1,0:T(8,128)(2,1)S(1)}, u32[]{:S(2)}, u32[]{:S(2)}) collective-permute-start(bf16[4,128,128]{2,1,0:T(8,128)(2,1)S(1)} %get-tuple-element.24), channel_id=1, source_target_pairs={{0,8},{8,0},{16,24},{24,16},{32,40},{40,32},{48,56},{56,48},{1,9},... | collective-permute-start | bytes 393224 | tf_op jit(solution)/shard_map/ppermute | solution.py:251
  17.5 26.8 %collective-permute-start = (bf16[128,1280]{1,0:T(8,128)(2,1)S(1)}, bf16[128,1280]{1,0:T(8,128)(2,1)S(1)}, u32[]{:S(2)}, u32[]{:S(2)}) collective-permute-start(bf16[128,1280]{1,0:T(8,128)(2,1)S(1)} %get-tuple-element.17.refs_0_), channel_id=1, source_target_pairs={{0,64},{64,128},{128,192},{192,0},{1,65},{65,129},{129,193},{193,1... | collective-permute-start | bytes 983048 | tf_op jit(solution)/shard_map/ppermute | solution.py:235
  18.3 26.9 %collective-permute-start.1 = (bf16[128,1280]{1,0:T(8,128)(2,1)S(1)}, bf16[128,1280]{1,0:T(8,128)(2,1)S(1)}, u32[]{:S(2)}, u32[]{:S(2)}) collective-permute-start(bf16[128,1280]{1,0:T(8,128)(2,1)S(1)} %get-tuple-element.17.refs_0_), channel_id=1, source_target_pairs={{0,128},{64,192},{128,0},{192,64},{1,129},{65,193},{129,1},{193,65... | collective-permute-start | bytes 983048 | tf_op jit(solution)/shard_map/ppermute | solution.py:235
  21.1 7.4 %collective-permute-start.18 = (bf16[128,128]{1,0:T(8,128)(2,1)S(1)}, bf16[128,128]{1,0:T(8,128)(2,1)S(1)}, u32[]{:S(2)}, u32[]{:S(2)}) collective-permute-start(bf16[128,128]{1,0:T(8,128)(2,1)S(1)} %get-tuple-element.26), channel_id=1, source_target_pairs={{0,16},{8,24},{16,32},{24,40},{32,48},{40,56},{48,0},{56,8},{1,17}... | collective-permute-start | bytes 98312 | tf_op jit(solution)/shard_map/ppermute | solution.py:247
  28.4 7.8 %collective-permute-start.19 = (bf16[128,128]{1,0:T(8,128)(2,1)S(1)}, bf16[128,128]{1,0:T(8,128)(2,1)S(1)}, u32[]{:S(2)}, u32[]{:S(2)}) collective-permute-start(bf16[128,128]{1,0:T(8,128)(2,1)S(1)} %get-tuple-element.27), channel_id=1, source_target_pairs={{0,32},{8,40},{16,48},{24,56},{32,0},{40,8},{48,16},{56,24},{1,33}... | collective-permute-start | bytes 98312 | tf_op jit(solution)/shard_map/ppermute | solution.py:247
  36.3 4.8 %collective-permute-start.20 = (bf16[128,128]{1,0:T(8,128)(2,1)S(1)}, bf16[128,128]{1,0:T(8,128)(2,1)S(1)}, u32[]{:S(2)}, u32[]{:S(2)}) collective-permute-start(bf16[128,128]{1,0:T(8,128)(2,1)S(1)} %get-tuple-element.28), channel_id=1, source_target_pairs={{0,48},{8,56},{16,0},{24,8},{32,16},{40,24},{48,32},{56,40},{1,49}... | collective-permute-start | bytes 98312 | tf_op jit(solution)/shard_map/ppermute | solution.py:247
  41.1 7.1 %collective-permute-start.2 = (bf16[128,1280]{1,0:T(8,128)(2,1)S(1)}, bf16[128,1280]{1,0:T(8,128)(2,1)S(1)}, u32[]{:S(2)}, u32[]{:S(2)}) collective-permute-start(bf16[128,1280]{1,0:T(8,128)(2,1)S(1)} %get-tuple-element.17.refs_0_), channel_id=1, source_target_pairs={{0,192},{64,0},{128,64},{192,128},{1,193},{65,1},{129,65},{193,129... | collective-permute-start | bytes 983048 | tf_op jit(solution)/shard_map/ppermute | solution.py:235
  42.4 7.1 %collective-permute-start.14 = (bf16[640,256]{1,0:T(8,128)(2,1)S(1)}, bf16[640,256]{1,0:T(8,128)(2,1)S(1)}, u32[]{:S(2)}, u32[]{:S(2)}) collective-permute-start(bf16[640,256]{1,0:T(8,128)(2,1)S(1)} %collective-permute-done.9.refs_9_), channel_id=1, source_target_pairs={{0,4},{1,5},{2,6},{3,7},{4,0},{5,1},{6,2},{7,3},{8,12},{9,13},{10,... | collective-permute-start | bytes 983048 | tf_op jit(solution)/shard_map/ppermute | solution.py:243
  42.8 10.6 %collective-permute-start.13 = (bf16[640,256]{1,0:T(8,128)(2,1)S(1)}, bf16[640,256]{1,0:T(8,128)(2,1)S(1)}, u32[]{:S(2)}, u32[]{:S(2)}) collective-permute-start(bf16[640,256]{1,0:T(8,128)(2,1)S(1)} %collective-permute-done.11.refs_11_), channel_id=1, source_target_pairs={{0,3},{1,0},{2,1},{3,2},{4,7},{5,4},{6,5},{7,6},{8,11},{9,8},{10,9... | collective-permute-start | bytes 983048 | tf_op jit(solution)/shard_map/ppermute | solution.py:239
  44.4 13.1 %collective-permute-start.10 = (bf16[640,256]{1,0:T(8,128)(2,1)S(1)}, bf16[640,256]{1,0:T(8,128)(2,1)S(1)}, u32[]{:S(2)}, u32[]{:S(2)}) collective-permute-start(bf16[640,256]{1,0:T(8,128)(2,1)S(1)} %constant_dynamic-update-slice_fusion.refs_8_), channel_id=1, source_target_pairs={{0,3},{1,0},{2,1},{3,2},{4,7},{5,4},{6,5},{7,6},{8,11},{9,8},{10,9... | collective-permute-start | bytes 983048 | tf_op jit(solution)/shard_map/ppermute | solution.py:239
  45.2 12.8 %collective-permute-start.3 = (bf16[128,1280]{1,0:T(8,128)(2,1)S(1)}, bf16[128,1280]{1,0:T(8,128)(2,1)S(1)}, u32[]{:S(2)}, u32[]{:S(2)}) collective-permute-start(bf16[128,1280]{1,0:T(8,128)(2,1)S(1)} %collective-permute-done.refs_1_), channel_id=1, source_target_pairs={{0,8},{8,0},{16,24},{24,16},{32,40},{40,32},{48,56},{56,48},{1,9},... | collective-permute-start | bytes 983048 | tf_op jit(solution)/shard_map/ppermute | solution.py:251
  48.2 11.3 %collective-permute-start.4 = (bf16[128,1280]{1,0:T(8,128)(2,1)S(1)}, bf16[128,1280]{1,0:T(8,128)(2,1)S(1)}, u32[]{:S(2)}, u32[]{:S(2)}) collective-permute-start(bf16[128,1280]{1,0:T(8,128)(2,1)S(1)} %collective-permute-done.1.refs_2_), channel_id=1, source_target_pairs={{0,8},{8,0},{16,24},{24,16},{32,40},{40,32},{48,56},{56,48},{1,9},... | collective-permute-start | bytes 983048 | tf_op jit(solution)/shard_map/ppermute | solution.py:251
  49.5 10.0 %collective-permute-start.5 = (bf16[128,1280]{1,0:T(8,128)(2,1)S(1)}, bf16[128,1280]{1,0:T(8,128)(2,1)S(1)}, u32[]{:S(2)}, u32[]{:S(2)}) collective-permute-start(bf16[128,1280]{1,0:T(8,128)(2,1)S(1)} %collective-permute-done.2.refs_3_), channel_id=1, source_target_pairs={{0,8},{8,0},{16,24},{24,16},{32,40},{40,32},{48,56},{56,48},{1,9},... | collective-permute-start | bytes 983048 | tf_op jit(solution)/shard_map/ppermute | solution.py:251
  53.4 7.9 %collective-permute-start.12 = (bf16[640,256]{1,0:T(8,128)(2,1)S(1)}, bf16[640,256]{1,0:T(8,128)(2,1)S(1)}, u32[]{:S(2)}, u32[]{:S(2)}) collective-permute-start(bf16[640,256]{1,0:T(8,128)(2,1)S(1)} %collective-permute-done.9.refs_9_), channel_id=1, source_target_pairs={{0,1},{1,2},{2,3},{3,0},{4,5},{5,6},{6,7},{7,4},{8,9},{9,10},{10,1... | collective-permute-start | bytes 983048 | tf_op jit(solution)/shard_map/ppermute | solution.py:239
  57.4 5.7 %collective-permute-start.15 = (bf16[320,256]{1,0:T(8,128)(2,1)S(1)}, bf16[320,256]{1,0:T(8,128)(2,1)S(1)}, u32[]{:S(2)}, u32[]{:S(2)}) collective-permute-start(bf16[320,256]{1,0:T(8,128)(2,1)S(1)} %slice.32), channel_id=1, source_target_pairs={{0,1},{1,2},{2,3},{3,0},{4,5},{5,6},{6,7},{7,4},{8,9},{9,10},{10,1... | collective-permute-start | bytes 491528 | tf_op jit(solution)/shard_map/ppermute | solution.py:239
  58.0 6.5 %collective-permute-start.16 = (bf16[320,256]{1,0:T(8,128)(2,1)S(1)}, bf16[320,256]{1,0:T(8,128)(2,1)S(1)}, u32[]{:S(2)}, u32[]{:S(2)}) collective-permute-start(bf16[320,256]{1,0:T(8,128)(2,1)S(1)} %slice.33), channel_id=1, source_target_pairs={{0,3},{1,0},{2,1},{3,2},{4,7},{5,4},{6,5},{7,6},{8,11},{9,8},{10,9... | collective-permute-start | bytes 491528 | tf_op jit(solution)/shard_map/ppermute | solution.py:239
  66.2 9.4 %collective-permute-start.21 = (bf16[144,128]{1,0:T(8,128)(2,1)S(1)}, bf16[144,128]{1,0:T(8,128)(2,1)S(1)}, u32[]{:S(2)}, u32[]{:S(2)}) collective-permute-start(bf16[144,128]{1,0:T(8,128)(2,1)S(1)} %shard_map.86.refs_0_), channel_id=1, source_target_pairs={{0,16},{8,24},{16,32},{24,40},{32,48},{40,56},{48,0},{56,8},{1,17}... | collective-permute-start | bytes 110600 | tf_op jit(solution)/shard_map/ppermute | solution.py:247
  68.9 7.9 %collective-permute-start.22 = (bf16[144,128]{1,0:T(8,128)(2,1)S(1)}, bf16[144,128]{1,0:T(8,128)(2,1)S(1)}, u32[]{:S(2)}, u32[]{:S(2)}) collective-permute-start(bf16[144,128]{1,0:T(8,128)(2,1)S(1)} %shard_map.86.refs_0_), channel_id=1, source_target_pairs={{0,32},{8,40},{16,48},{24,56},{32,0},{40,8},{48,16},{56,24},{1,33}... | collective-permute-start | bytes 110600 | tf_op jit(solution)/shard_map/ppermute | solution.py:247
  71.8 5.2 %collective-permute-start.23 = (bf16[144,128]{1,0:T(8,128)(2,1)S(1)}, bf16[144,128]{1,0:T(8,128)(2,1)S(1)}, u32[]{:S(2)}, u32[]{:S(2)}) collective-permute-start(bf16[144,128]{1,0:T(8,128)(2,1)S(1)} %shard_map.86.refs_0_), channel_id=1, source_target_pairs={{0,48},{8,56},{16,0},{24,8},{32,16},{40,24},{48,32},{56,40},{1,49}... | collective-permute-start | bytes 110600 | tf_op jit(solution)/shard_map/ppermute | solution.py:247
  75.5 2.4 %collective-permute-start.24 = (bf16[144,128]{1,0:T(8,128)(2,1)S(1)}, bf16[144,128]{1,0:T(8,128)(2,1)S(1)}, u32[]{:S(2)}, u32[]{:S(2)}) collective-permute-start(bf16[144,128]{1,0:T(8,128)(2,1)S(1)} %shard_map.86.refs_0_), channel_id=1, source_target_pairs={{0,8},{8,0},{16,24},{24,16},{32,40},{40,32},{48,56},{56,48},{1,9},... | collective-permute-start | bytes 110600 | tf_op jit(solution)/shard_map/ppermute | solution.py:251
  75.6 2.3 %collective-permute-start.25 = (bf16[144,128]{1,0:T(8,128)(2,1)S(1)}, bf16[144,128]{1,0:T(8,128)(2,1)S(1)}, u32[]{:S(2)}, u32[]{:S(2)}) collective-permute-start(bf16[144,128]{1,0:T(8,128)(2,1)S(1)} %collective-permute-done.21.refs_1_), channel_id=1, source_target_pairs={{0,8},{8,0},{16,24},{24,16},{32,40},{40,32},{48,56},{56,48},{1,9},... | collective-permute-start | bytes 110600 | tf_op jit(solution)/shard_map/ppermute | solution.py:251
  76.8 1.2 %collective-permute-start.26 = (bf16[144,128]{1,0:T(8,128)(2,1)S(1)}, bf16[144,128]{1,0:T(8,128)(2,1)S(1)}, u32[]{:S(2)}, u32[]{:S(2)}) collective-permute-start(bf16[144,128]{1,0:T(8,128)(2,1)S(1)} %collective-permute-done.22.refs_2_), channel_id=1, source_target_pairs={{0,8},{8,0},{16,24},{24,16},{32,40},{40,32},{48,56},{56,48},{1,9},... | collective-permute-start | bytes 110600 | tf_op jit(solution)/shard_map/ppermute | solution.py:251
  77.0 1.2 %collective-permute-start.27 = (bf16[144,128]{1,0:T(8,128)(2,1)S(1)}, bf16[144,128]{1,0:T(8,128)(2,1)S(1)}, u32[]{:S(2)}, u32[]{:S(2)}) collective-permute-start(bf16[144,128]{1,0:T(8,128)(2,1)S(1)} %collective-permute-done.23.refs_3_), channel_id=1, source_target_pairs={{0,8},{8,0},{16,24},{24,16},{32,40},{40,32},{48,56},{56,48},{1,9},... | collective-permute-start | bytes 110600 | tf_op jit(solution)/shard_map/ppermute | solution.py:251
  79.5 26.6 %collective-permute-start.28 = (bf16[144,384]{1,0:T(8,128)(2,1)S(1)}, bf16[144,384]{1,0:T(8,128)(2,1)S(1)}, u32[]{:S(2)}, u32[]{:S(2)}) collective-permute-start(bf16[144,384]{1,0:T(8,128)(2,1)S(1)} %shard_map.87.u0), channel_id=1, source_target_pairs={{0,64},{64,128},{128,192},{192,0},{1,65},{65,129},{129,193},{193,1... | collective-permute-start | bytes 331784 | tf_op jit(solution)/shard_map/ppermute | solution.py:235
  81.6 24.6 %collective-permute-start.29 = (bf16[144,384]{1,0:T(8,128)(2,1)S(1)}, bf16[144,384]{1,0:T(8,128)(2,1)S(1)}, u32[]{:S(2)}, u32[]{:S(2)}) collective-permute-start(bf16[144,384]{1,0:T(8,128)(2,1)S(1)} %shard_map.87.u0), channel_id=1, source_target_pairs={{0,128},{64,192},{128,0},{192,64},{1,129},{65,193},{129,1},{193,65... | collective-permute-start | bytes 331784 | tf_op jit(solution)/shard_map/ppermute | solution.py:235
  82.9 23.3 %collective-permute-start.30 = (bf16[144,384]{1,0:T(8,128)(2,1)S(1)}, bf16[144,384]{1,0:T(8,128)(2,1)S(1)}, u32[]{:S(2)}, u32[]{:S(2)}) collective-permute-start(bf16[144,384]{1,0:T(8,128)(2,1)S(1)} %shard_map.87.u0), channel_id=1, source_target_pairs={{0,192},{64,0},{128,64},{192,128},{1,193},{65,1},{129,65},{193,129... | collective-permute-start | bytes 331784 | tf_op jit(solution)/shard_map/ppermute | solution.py:235
  (6 other events, 168.4 us)

commit v2 on v0

v2 whole, which is shorter than its diff:
```python
import jax
import jax.numpy as jnp
from jax import lax
from jax.experimental import pallas as pl
from jax.experimental.pallas import tpu as pltpu
from jax.sharding import PartitionSpec as P

BLOCK = 16
LOW = -1e38
STEPS = (0, 3, 1, 2)
F32 = jnp.float32
BF16 = jnp.bfloat16
VMEM = pl.BlockSpec(memory_space=pltpu.VMEM)
FETCH = pl.BlockSpec()
SMEM = pl.BlockSpec(memory_space=pltpu.SMEM)
ANY = pl.BlockSpec(memory_space=pl.ANY)
def call(kernel, outs, args, specs, scratch=(), cost=1.0):
    return pl.pallas_call(
        kernel,
        out_shape=outs,
        in_specs=specs,
        out_specs=jax.tree.map(lambda _: VMEM, outs),
        scratch_shapes=list(scratch),
        compiler_params=pltpu.CompilerParams(vmem_limit_bytes=48 * 1024 * 1024),
        cost_estimate=pl.CostEstimate(flops=0, bytes_accessed=int(cost * 3_000_000), transcendentals=0),
    )(*args)


def dot(a, b, ca, cb):
    return lax.dot_general(a, b, (((ca,), (cb,)), ((), ())), preferred_element_type=F32)


def three(v):
    hi = v.astype(BF16).astype(F32)
    mid = (v - hi).astype(BF16).astype(F32)
    return hi, mid, v - hi - mid


def pack_columns(columns):
    lane = lax.broadcasted_iota(jnp.int32, (columns[0].shape[0], 128), 1)
    out = jnp.zeros(lane.shape, F32)
    for i, c in enumerate(columns):
        out = jnp.where(lane == i, c, out)
    return out


def pack_rows(rows, height):
    sub = lax.broadcasted_iota(jnp.int32, (height, rows[0].shape[1]), 0)
    out = jnp.zeros(sub.shape, F32)
    for i, c in enumerate(rows):
        out = jnp.where(sub == i, c, out)
    return out


def weight_kernel(w_ref, x_ref, keep_ref, give_ref, p_ref, tmp):
    p_ref[...] = x_ref[...]
    tensor = lax.axis_index("tensor")
    zl, x = tensor // 4, lax.rem(tensor, 4)
    rows = w_ref.shape[0] // 8
    for b, out_ref in enumerate((keep_ref, give_ref)):
        for s in range(4):
            start = (lax.rem(zl + b, 2) * 4 + lax.rem(x + STEPS[s], 4)) * rows
            tmp[pl.ds(s * rows, rows), :] = w_ref[pl.ds(pl.multiple_of(start, rows), rows), :].astype(F32)
        out_ref[pl.ds(0, 128), :] = jnp.transpose(tmp[:, :128]).astype(BF16)
        out_ref[pl.ds(128, 128), :] = jnp.transpose(tmp[:, 128:]).astype(BF16)


def target_kernel(dest_ref, row_ref, out_ref):
    batch, role = lax.axis_index("batch"), lax.axis_index("role")
    lane = lax.broadcasted_iota(jnp.int32, (8, 512), 1)
    sub = lax.broadcasted_iota(jnp.int32, (8, 512), 0)
    block = lax.broadcasted_iota(jnp.int32, (512, 256), 0)
    place = lax.broadcasted_iota(jnp.int32, (512, 256), 1) >> 4
    pick = jnp.where((((block >> 4) & 3) == role) & ((block & 15) == place), 1.0, 0.0).astype(BF16)
    dest, row = [
        dot(jnp.where((lane >> 6) == sub, r[...], 0).astype(F32).astype(BF16), pick, 1, 0).astype(jnp.int32)
        for r in (dest_ref, row_ref)
    ]
    out_ref[...] = jnp.where((dest & 7) == batch, (dest >> 3) * 16 + row, -1)


def resident_kernel(len_ref, q_ref, sc_ref, c_ref, out_ref, buf, sems):
    copies = [
        pltpu.make_async_copy(c_ref.at[i // 2, pl.ds(i % 2 * 8, 8), 0], buf.at[i // 2, pl.ds(i % 2 * 8, 8)], sems.at[i])
        for i in range(6)
    ]
    for c in copies:
        c.start()
    lane = lax.broadcasted_iota(jnp.int32, (8, 256), 1)
    lane128 = lax.broadcasted_iota(jnp.int32, (128, 128), 1)
    column = lax.broadcasted_iota(jnp.int32, (16, 256), 0)
    block = lax.broadcasted_iota(jnp.int32, (16, 256), 1) >> 4
    pick = jnp.where(column == block, 1.0, 0.0).astype(BF16)
    for group in range(3):
        spread = []
        for half in range(2):
            parts = [p.astype(BF16) for p in three(sc_ref[pl.ds(group * 16, 16), half, :])]
            spread.append((dot(parts[0], pick, 1, 0) + dot(parts[1], pick, 1, 0)) + dot(parts[2], pick, 1, 0))
        ks, vs = spread[0] * (128.0**-0.5), spread[1]
        turned = jnp.transpose(jnp.concatenate([q_ref[group, n].astype(F32) for n in range(16)], axis=0))
        s = jnp.zeros((256, 128), F32)
        for n in range(0, 16, 2):
            if n % 8 == 0:
                copies[group * 2 + n // 8].wait()
            keys = jnp.concatenate([buf[group, n, :, :128], buf[group, n + 1, :, :128]], axis=1)
            own = [jnp.where((lane128 >> 3) == n + i, turned, 0.0).astype(BF16) for i in range(2)]
            s = s + dot(keys, jnp.concatenate(own, axis=0), 1, 0)
        s = jnp.transpose(s)
        scores, scale = [], []
        for n in range(16):
            live = lane < len_ref[group, n]
            scores.append(jnp.where(live, s[n * 8 : n * 8 + 8] * ks[n : n + 1], -jnp.inf))
            scale.append(jnp.broadcast_to(vs[n : n + 1], (8, 256)))
        s = jnp.concatenate(scores, axis=0)
        m = jnp.max(s, axis=1, keepdims=True)
        e = jnp.exp(s - m)
        den = jnp.sum(e, axis=1, keepdims=True)
        w = e * jnp.concatenate(scale, axis=0)
        for n in range(16):
            part = w[n * 8 : n * 8 + 8].astype(BF16)
            out_ref[pl.ds(group * 128 + n * 8, 8), :128] = dot(part, buf[group, n, :, 128:], 1, 0)
        out_ref[pl.ds(group * 128, 128), 128:] = jnp.where(lane128 == 0, m, den)


def project_kernel(w_ref, *refs):
    p, outs = refs[:5], refs[5:]
    role = lax.axis_index("role")
    count = p[0].shape[1] // 4
    for d in (2, 1, 3, 0):
        start = pl.multiple_of(lax.rem(role + d, 4) * count, 128)
        rows = jnp.concatenate([r[:, pl.ds(start, count)] for r in p], axis=0)
        outs[d][...] = dot(w_ref[...], rows, 1, 0).astype(outs[d].dtype)


def total_of(parts):
    a, b, c, d = [p[...].astype(F32) for p in parts]
    return (a + b) + (c + d)


def sum_kernel(a, b, c, d, out_ref):
    out_ref[...] = total_of((a, b, c, d)).astype(BF16)


def group_max(v):
    lane = lax.broadcasted_iota(jnp.int32, v.shape, 1)
    n = v.shape[1]
    for s in (1, 2, 4, 8):
        other = jnp.where((lane & s) == 0, pltpu.roll(v, n - s, 1), pltpu.roll(v, s, 1))
        v = jnp.maximum(v, other)
    return v


def quantize(kv):
    largest = group_max(jnp.max(jnp.abs(kv), axis=0, keepdims=True))
    scale = (largest + 1e-6) / 127.0
    return (kv / scale).astype(BF16), scale


def quantize_kernel(a, b, c, d, got, out_ref):
    kv = total_of((a, b, c, d)) + got[...].astype(F32)
    key_codes, key_scale = quantize(kv[:128])
    value_codes, value_scale = quantize(kv[128:])
    out_ref[pl.ds(0, 128), :] = key_codes
    out_ref[pl.ds(128, 128), :] = value_codes
    out_ref[pl.ds(256, 16), :] = pack_rows(three(key_scale) + three(value_scale), 16).astype(BF16)


def join_kernel(target_ref, q_ref, *refs):
    parts, out_ref, tmp = refs[:8], refs[8], refs[9]
    batch = lax.axis_index("batch")
    zh, core = batch // 2, lax.rem(batch, 2)
    q = q_ref[...]
    request = lax.broadcasted_iota(jnp.int32, (384, 256), 0) >> 3
    scales, top = [], jnp.full((384, 256), LOW, F32)
    for i in range(8):
        origin = lax.rem(zh + 4 - i % 4, 4) * 2 + (core if i < 4 else 1 - core)
        rows = parts[i][pl.ds(256, 16), :].astype(F32)
        key_scale = (rows[0:1] + rows[1:2]) + rows[2:3]
        scales.append((rows[3:4] + rows[4:5]) + rows[5:6])
        s = dot(q, parts[i][pl.ds(0, 128), :], 1, 0) * (key_scale * (128.0**-0.5))
        s = jnp.where(request == target_ref[pl.ds(origin, 1), :], s, -jnp.inf)
        tmp[i] = s
        top = jnp.maximum(top, s)
    top = jnp.max(top, axis=1, keepdims=True)
    total = jnp.zeros((384, 256), F32)
    acc = jnp.zeros((384, 128), F32)
    for i in range(8):
        e = jnp.exp(tmp[i] - top)
        total = total + e
        acc = acc + dot((e * scales[i]).astype(BF16), parts[i][pl.ds(128, 128), :], 1, 1)
    den = jnp.sum(total, axis=1, keepdims=True)
    out_ref[pl.ds(0, 128), :] = jnp.transpose(acc).astype(BF16)
    stats = pack_columns(three(top) + three(den))
    out_ref[pl.ds(128, 16), :] = jnp.transpose(stats)[:16].astype(BF16)


def final_kernel(u0, u1, u2, u3, r, out_ref, tmp):
    us = (u0, u1, u2, u3)
    tops, dens = [], []
    for u in us:
        rows = [u[pl.ds(128, 16), :].astype(F32)[i : i + 1] for i in range(6)]
        tops.append((rows[0] + rows[1]) + rows[2])
        dens.append((rows[3] + rows[4]) + rows[5])
    top = jnp.maximum(jnp.maximum(tops[0], tops[1]), jnp.maximum(tops[2], tops[3]))
    acc = jnp.zeros((128, 384), F32)
    den = jnp.zeros((1, 384), F32)
    for u, m, d in zip(us, tops, dens):
        share = jnp.exp(m - top)
        acc = acc + u[pl.ds(0, 128), :].astype(F32) * share
        den = den + d * share
    acc = jnp.transpose(acc)
    columns = jnp.transpose(pack_rows((top, den), 128))
    new_top, new_den = columns[:, 0:1], columns[:, 1:2]
    old_top, old_den = r[:, 128:129], r[:, 129:130]
    best = jnp.maximum(new_top, old_top)
    new_share, old_share = jnp.exp(new_top - best), jnp.exp(old_top - best)
    total = new_den * new_share + old_den * old_share
    tmp[...] = (acc * new_share + r[:, :128] * old_share) / total
    for q in range(8):
        out_ref[:, q * 128 : q * 128 + 128] = tmp[pl.ds(q, 48, stride=8), :].astype(BF16)


def shape(*dims, dtype=BF16):
    return jax.ShapeDtypeStruct(dims, dtype)


def role_shift(v, d):
    return lax.ppermute(v, "role", [(i, (i + d) % 4) for i in range(4)])


def x_shift(v, d):
    return lax.ppermute(v, "tensor", [(z * 4 + x, z * 4 + (x + d) % 4) for z in range(2) for x in range(4)])


def z_swap(v):
    return lax.ppermute(v, "tensor", [(t, (t + 4) % 8) for t in range(8)])


def zh_shift(v, d):
    return lax.ppermute(v, "batch", [(i, (i + 2 * d) % 8) for i in range(8)])


def core_swap(v):
    return lax.ppermute(v, "batch", [(i, i ^ 1) for i in range(8)])


def body(span, weight, queries, codes, scales, clen, bdest, brow):
    p0 = span.T
    p1, p2 = x_shift(p0, 1), x_shift(p0, -1)

    rows = weight.shape[0]
    keep, give, held = call(
        weight_kernel, [shape(256, rows // 2)] * 2 + [shape(*p0.shape)], (weight.reshape(rows, 256), p0), [FETCH] * 2,
        scratch=[pltpu.VMEM((rows // 2, 256), F32)],
    )
    got = z_swap(give)

    target = call(target_kernel, shape(8, 256, dtype=jnp.int32), (bdest.T, brow.reshape(1, 512)), [FETCH] * 2)
    (p1, p2), target = lax.optimization_barrier(((p1, p2), target))

    cutoff = p0.shape[0] // 2
    p3a, p3b = x_shift(p1[:cutoff], 1), x_shift(p2[cutoff:], -1)
    pieces = (held, p1, p2, p3a, p3b)

    count = p0.shape[1] // 4
    outs = [shape(256, count, dtype=F32 if d == 0 else BF16) for d in range(4)]
    far = call(project_kernel, outs, (got, *pieces), [VMEM] * 6)
    far_sums = [far[0]] + [role_shift(far[d], d) for d in (1, 2, 3)]
    pieces, _ = lax.optimization_barrier((pieces, far[0]))
    near = call(project_kernel, outs, (keep, *pieces), [VMEM] * 6)
    sums = [near[0]] + [role_shift(near[d], d) for d in (1, 2, 3)]
    back = z_swap(call(sum_kernel, shape(256, count), far_sums, [VMEM] * 4))
    codes_out = call(quantize_kernel, shape(272, count), (*sums, back), [VMEM] * 5)

    parts = [codes_out] + [zh_shift(codes_out, d) for d in (1, 2, 3)]
    parts = parts + [core_swap(v) for v in parts]
    sums = call(
        join_kernel, shape(144, 384), (target, queries.reshape(384, 128), *parts), [VMEM] * 10,
        scratch=[pltpu.VMEM((8, 384, 256), F32)], cost=2.5,
    )
    sums = [sums] + [role_shift(sums, d) for d in (1, 2, 3)]
    res = call(
        resident_kernel, shape(384, 256, dtype=F32), (clen, queries, jnp.swapaxes(scales, 3, 4).reshape(48, 2, 16), codes),
        [SMEM, VMEM, VMEM, ANY], scratch=[pltpu.VMEM((3, 16, 256, 256), BF16), pltpu.SemaphoreType.DMA((6,))], cost=5,
    )
    out = call(final_kernel, shape(48, 1024), (*sums, res), [VMEM] * 5, scratch=[pltpu.VMEM((384, 128), F32)])
    return out.reshape(3, 16, 1024)


def solution(mesh):
    return jax.shard_map(
        body,
        mesh=mesh,
        in_specs=(
            P("batch", ("role", "tensor")),
            P("role", "tensor", None),
            P(None, "batch", "tensor", None),
            P(None, "batch", "tensor", None, None),
            P(None, "batch", "tensor", None, None),
            P(None, "batch"),
            P(),
            P(),
        ),
        out_specs=P(None, "batch", "tensor"),
        check_vma=False,
    )
```

time: 200 us -> 71 us (0.35)
  waiting for transfers between devices: 134 us -> 19.3 us
  starting transfers between devices: 0.08 us -> 37.7 us
  blocking collectives: 25.1 us -> 0 us
  between operations: 13.3 us -> 0.1 us
  matrix products: 12.1 us -> 0 us
  Pallas kernels: 0 us -> 10.2 us
  other arithmetic: 8.63 us -> 0 us
  local copies, waits for them, and re-layouts: 6.15 us -> 3.46 us
    all_gather x2 -> x0, waiting for transfers between devices: 84 us -> none  [the longest x1 48.1 us: body(): lax.all_gather(span, 'tensor', axis=1, tiled=True)]
    psum x1 -> x0, waiting for transfers between devices: 49.3 us -> none  [body(): lax.psum(partial_rows.astype(jnp.bfloat16), 'role').astype(jnp.float32)]
    ppermute x0 -> x22, starting transfers between devices: none -> 37.7 us  [the longest x9 15.4 us: role_shift(): return lax.ppermute(v, 'role', [(i, (i + d) % 4) for i in range(4)])]
    all_gather x2 -> x0, blocking collectives: 25.1 us -> none  [the longest x1 12.8 us: body(): lax.all_gather(block_scales.astype(jnp.bfloat16), 'batch', axis=0, tiled=...]
    ppermute x0 -> x22, waiting for transfers between devices: none -> 19.3 us  [the longest x4 7.6 us: x_shift(): lax.ppermute(v, 'tensor', [(z * 4 + x, z * 4 + (x + d) % 4) for z in rang...]
    dot_general x5 -> x0, matrix products: 12.1 us -> none  [the longest x1 4.27 us: attend(): jnp.einsum('rhgd,shtd->rhgst', grouped, new_codes[..., :head_size], prefe...]
    pallas_call x0 -> x9, Pallas kernels: none -> 10.2 us  [call(): pl.pallas_call(kernel, out_shape=outs, in_specs=specs, out_specs=jax.tree...]
    reduce_sum x2 -> x0, other arithmetic: 5.42 us -> none  [attend(): total = jnp.sum(exp_res, axis=-1) + jnp.sum(exp_new, axis=(-2, -1))]
  transfers between devices with their start and end apart: 3 -> 22, of which waited for: 3 -> 13; matrix products, arithmetic and copies ran while one was open for 3% -> 0% of each run, Pallas kernels for 0% -> 8%
where the time goes in v2:
time: 71 us; the launch traced here: 70.8 us
  starting transfers between devices  37.7 us (53%)
  waiting for transfers between devices  19.3 us (27%)
  Pallas kernels  10.2 us (14%)
  local copies, waits for them, and re-layouts  3.46 us (5%)
    ppermute x9, starting transfers between devices, role_shift(): return lax.ppermute(v, 'role', [(i, (i + d) % 4) for i in range(4)])  15.4 us
    ppermute x3, starting transfers between devices, zh_shift(): return lax.ppermute(v, 'batch', [(i, (i + 2 * d) % 8) for i in range(8)])  13.6 us
    pallas_call x9, Pallas kernels, call(): pl.pallas_call(kernel, out_shape=outs, in_specs=specs, out_specs=jax.tree...  10.2 us
    ppermute x4, waiting for transfers between devices, x_shift(): lax.ppermute(v, 'tensor', [(z * 4 + x, z * 4 + (x + d) % 4) for z in rang...  7.6 us
    ppermute x4, starting transfers between devices, x_shift(): lax.ppermute(v, 'tensor', [(z * 4 + x, z * 4 + (x + d) % 4) for z in rang...  4.4 us
    ppermute x2, waiting for transfers between devices, z_swap(): return lax.ppermute(v, 'tensor', [(t, (t + 4) % 8) for t in range(8)])  4.2 us
    ppermute x2, starting transfers between devices, z_swap(): return lax.ppermute(v, 'tensor', [(t, (t + 4) % 8) for t in range(8)])  3.8 us
    ppermute x3, waiting for transfers between devices, zh_shift(): return lax.ppermute(v, 'batch', [(i, (i + 2 * d) % 8) for i in range(8)])  3.64 us
  transfers between devices with their start and end apart: 22, of which 13 were waited for; matrix products, arithmetic and copies ran while one was open for 0% of the time, Pallas kernels for 8%

profile of v2, /device:TPU:6, one launch (start us, length us, event | category | flops | bytes accessed | tf_op | source)
XLA Modules:
  0.0 70.8 jit_solution(9595968123444609485)
XLA Ops:
  0.0 2.2 %collective-permute-start = (bf16[160,1024]{1,0:T(8,128)(2,1)}, bf16[160,1024]{1,0:T(8,128)(2,1)S(1)}, u32[]{:S(2)}, u32[]{:S(2)}) collective-permute-start(bf16[160,1024]{1,0:T(8,128)(2,1)} %bitcast.11), channel_id=1, source_target_pairs={{0,1},{1,2},{2,3},{3,0},{4,5},{5,6},{6,7},{7,4},{8,9},{9,10},{10,1... | collective-permute-start | bytes 983048 | tf_op jit(solution)/shard_map/ppermute | solution.py:232
  2.2 1.1 %copy-done = bf16[1280,1,256]{2,0,1:T(8,128)(2,1)S(1)} copy-done((bf16[1280,1,256]{2,0,1:T(8,128)(2,1)S(1)}, bf16[1280,1,256]{2,0,1:T(8,128)(2,1)}, u32[]{:S(2)}) %copy-start) | copy-done | bytes 655384
  3.3 1.0 %copy-done.2 = bf16[1024,160]{0,1:T(8,128)(2,1)S(1)} copy-done((bf16[1024,160]{0,1:T(8,128)(2,1)S(1)}, bf16[1024,160]{0,1:T(8,128)(2,1)}, u32[]{:S(2)}) %copy-start.2) | copy-done | bytes 327704
  4.5 1.8 %collective-permute-start.4 = (bf16[256,640]{1,0:T(8,128)(2,1)S(1)}, bf16[256,640]{1,0:T(8,128)(2,1)S(1)}, u32[]{:S(2)}, u32[]{:S(2)}) collective-permute-start(bf16[256,640]{1,0:T(8,128)(2,1)S(1)} %get-tuple-element.29), channel_id=1, source_target_pairs={{0,4},{1,5},{2,6},{3,7},{4,0},{5,1},{6,2},{7,3},{8,12},{9,13},{10,... | collective-permute-start | bytes 983048 | tf_op jit(solution)/shard_map/ppermute | solution.py:236
  6.3 0.7 copy-done.5
  7.0 0.7 copy-done.6
  7.9 1.7 %collective-permute-done.refs_1_ = bf16[160,1024]{1,0:T(8,128)(2,1)S(1)} collective-permute-done((bf16[160,1024]{1,0:T(8,128)(2,1)}, bf16[160,1024]{1,0:T(8,128)(2,1)S(1)}, u32[]{:S(2)}, u32[]{:S(2)}) %collective-permute-start) | collective-permute-done | bytes 327712 | tf_op jit(solution)/shard_map/ppermute | solution.py:232
  9.7 1.3 %collective-permute-done.1.refs_2_ = bf16[160,1024]{1,0:T(8,128)(2,1)S(1)} collective-permute-done((bf16[160,1024]{1,0:T(8,128)(2,1)}, bf16[160,1024]{1,0:T(8,128)(2,1)S(1)}, u32[]{:S(2)}, u32[]{:S(2)}) %collective-permute-start.1) | collective-permute-done | bytes 327712 | tf_op jit(solution)/shard_map/ppermute | solution.py:232
  11.5 1.7 %collective-permute-start.3 = (bf16[80,1024]{1,0:T(8,128)(2,1)S(1)}, bf16[80,1024]{1,0:T(8,128)(2,1)S(1)}, u32[]{:S(2)}, u32[]{:S(2)}) collective-permute-start(bf16[80,1024]{1,0:T(8,128)(2,1)S(1)} %slice.7), channel_id=1, source_target_pairs={{0,3},{1,0},{2,1},{3,2},{4,7},{5,4},{6,5},{7,6},{8,11},{9,8},{10,9... | collective-permute-start | bytes 491528 | tf_op jit(solution)/shard_map/ppermute | solution.py:232
  13.5 2.9 %collective-permute-done.2.refs_3_ = bf16[80,1024]{1,0:T(8,128)(2,1)S(1)} collective-permute-done((bf16[80,1024]{1,0:T(8,128)(2,1)S(1)}, bf16[80,1024]{1,0:T(8,128)(2,1)S(1)}, u32[]{:S(2)}, u32[]{:S(2)}) %collective-permute-start.2) | collective-permute-done | bytes 163872 | tf_op jit(solution)/shard_map/ppermute | solution.py:232
  16.4 1.7 %collective-permute-done.3.refs_4_ = bf16[80,1024]{1,0:T(8,128)(2,1)S(1)} collective-permute-done((bf16[80,1024]{1,0:T(8,128)(2,1)S(1)}, bf16[80,1024]{1,0:T(8,128)(2,1)S(1)}, u32[]{:S(2)}, u32[]{:S(2)}) %collective-permute-start.3) | collective-permute-done | bytes 163872 | tf_op jit(solution)/shard_map/ppermute | solution.py:232
  18.7 3.1 %collective-permute-start.10 = (bf16[256,256]{1,0:T(8,128)(2,1)S(1)}, bf16[256,256]{1,0:T(8,128)(2,1)S(1)}, u32[]{:S(2)}, u32[]{:S(2)}) collective-permute-start(bf16[256,256]{1,0:T(8,128)(2,1)S(1)} %get-tuple-element.42), channel_id=1, source_target_pairs={{0,192},{64,0},{128,64},{192,128},{1,193},{65,1},{129,65},{193,129... | collective-permute-start | bytes 393224 | tf_op jit(solution)/shard_map/ppermute | solution.py:228
  21.8 2.2 %collective-permute-start.9 = (bf16[256,256]{1,0:T(8,128)(2,1)S(1)}, bf16[256,256]{1,0:T(8,128)(2,1)S(1)}, u32[]{:S(2)}, u32[]{:S(2)}) collective-permute-start(bf16[256,256]{1,0:T(8,128)(2,1)S(1)} %get-tuple-element.41), channel_id=1, source_target_pairs={{0,128},{64,192},{128,0},{192,64},{1,129},{65,193},{129,1},{193,65... | collective-permute-start | bytes 393224 | tf_op jit(solution)/shard_map/ppermute | solution.py:228
  24.6 2.0 %collective-permute-start.5 = (bf16[256,256]{1,0:T(8,128)(2,1)S(1)}, bf16[256,256]{1,0:T(8,128)(2,1)S(1)}, u32[]{:S(2)}, u32[]{:S(2)}) collective-permute-start(bf16[256,256]{1,0:T(8,128)(2,1)S(1)} %get-tuple-element.37), channel_id=1, source_target_pairs={{0,64},{64,128},{128,192},{192,0},{1,65},{65,129},{129,193},{193,1... | collective-permute-start | bytes 393224 | tf_op jit(solution)/shard_map/ppermute | solution.py:228
  26.5 0.6 collective-permute-start.6
  27.1 0.8 %collective-permute-done.10.d = bf16[256,256]{1,0:T(8,128)(2,1)S(1)} collective-permute-done((bf16[256,256]{1,0:T(8,128)(2,1)S(1)}, bf16[256,256]{1,0:T(8,128)(2,1)S(1)}, u32[]{:S(2)}, u32[]{:S(2)}) %collective-permute-start.10) | collective-permute-done | bytes 131104 | tf_op jit(solution)/shard_map/ppermute | solution.py:228
  27.9 4.2 %collective-permute-start.7 = (bf16[256,256]{1,0:T(8,128)(2,1)S(1)}, bf16[256,256]{1,0:T(8,128)(2,1)S(1)}, u32[]{:S(2)}, u32[]{:S(2)}) collective-permute-start(bf16[256,256]{1,0:T(8,128)(2,1)S(1)} %get-tuple-element.39), channel_id=1, source_target_pairs={{0,192},{64,0},{128,64},{192,128},{1,193},{65,1},{129,65},{193,129... | collective-permute-start | bytes 393224 | tf_op jit(solution)/shard_map/ppermute | solution.py:228
  32.2 2.0 %collective-permute-start.11 = (bf16[256,256]{1,0:T(8,128)(2,1)S(1)}, bf16[256,256]{1,0:T(8,128)(2,1)S(1)}, u32[]{:S(2)}, u32[]{:S(2)}) collective-permute-start(bf16[256,256]{1,0:T(8,128)(2,1)S(1)} %shard_map.86), channel_id=1, source_target_pairs={{0,4},{1,5},{2,6},{3,7},{4,0},{5,1},{6,2},{7,3},{8,12},{9,13},{10,... | collective-permute-start | bytes 393224 | tf_op jit(solution)/shard_map/ppermute | solution.py:236
  34.6 3.9 %collective-permute-done.11.got = bf16[256,256]{1,0:T(8,128)(2,1)S(1)} collective-permute-done((bf16[256,256]{1,0:T(8,128)(2,1)S(1)}, bf16[256,256]{1,0:T(8,128)(2,1)S(1)}, u32[]{:S(2)}, u32[]{:S(2)}) %collective-permute-start.11) | collective-permute-done | bytes 131104 | tf_op jit(solution)/shard_map/ppermute | solution.py:236
  38.9 3.6 %collective-permute-start.12 = (bf16[272,256]{1,0:T(8,128)(2,1)S(1)}, bf16[272,256]{1,0:T(8,128)(2,1)S(1)}, u32[]{:S(2)}, u32[]{:S(2)}) collective-permute-start(bf16[272,256]{1,0:T(8,128)(2,1)S(1)} %shard_map.87.refs_0_), channel_id=1, source_target_pairs={{0,16},{8,24},{16,32},{24,40},{32,48},{40,56},{48,0},{56,8},{1,17}... | collective-permute-start | bytes 417800 | tf_op jit(solution)/shard_map/ppermute | solution.py:240
  42.5 6.0 %collective-permute-start.13 = (bf16[272,256]{1,0:T(8,128)(2,1)S(1)}, bf16[272,256]{1,0:T(8,128)(2,1)S(1)}, u32[]{:S(2)}, u32[]{:S(2)}) collective-permute-start(bf16[272,256]{1,0:T(8,128)(2,1)S(1)} %shard_map.87.refs_0_), channel_id=1, source_target_pairs={{0,32},{8,40},{16,48},{24,56},{32,0},{40,8},{48,16},{56,24},{1,33}... | collective-permute-start | bytes 417800 | tf_op jit(solution)/shard_map/ppermute | solution.py:240
  48.5 4.0 %collective-permute-start.14 = (bf16[272,256]{1,0:T(8,128)(2,1)S(1)}, bf16[272,256]{1,0:T(8,128)(2,1)S(1)}, u32[]{:S(2)}, u32[]{:S(2)}) collective-permute-start(bf16[272,256]{1,0:T(8,128)(2,1)S(1)} %shard_map.87.refs_0_), channel_id=1, source_target_pairs={{0,48},{8,56},{16,0},{24,8},{32,16},{40,24},{48,32},{56,40},{1,49}... | collective-permute-start | bytes 417800 | tf_op jit(solution)/shard_map/ppermute | solution.py:240
  53.0 0.8 %collective-permute-done.13.refs_2_ = bf16[272,256]{1,0:T(8,128)(2,1)S(1)} collective-permute-done((bf16[272,256]{1,0:T(8,128)(2,1)S(1)}, bf16[272,256]{1,0:T(8,128)(2,1)S(1)}, u32[]{:S(2)}, u32[]{:S(2)}) %collective-permute-start.13) | collective-permute-done | bytes 139296 | tf_op jit(solution)/shard_map/ppermute | solution.py:240
  53.8 2.8 %collective-permute-done.14.refs_3_ = bf16[272,256]{1,0:T(8,128)(2,1)S(1)} collective-permute-done((bf16[272,256]{1,0:T(8,128)(2,1)S(1)}, bf16[272,256]{1,0:T(8,128)(2,1)S(1)}, u32[]{:S(2)}, u32[]{:S(2)}) %collective-permute-start.14) | collective-permute-done | bytes 139296 | tf_op jit(solution)/shard_map/ppermute | solution.py:240
  56.7 1.3 %collective-permute-done.18.refs_7_ = bf16[272,256]{1,0:T(8,128)(2,1)S(1)} collective-permute-done((bf16[272,256]{1,0:T(8,128)(2,1)S(1)}, bf16[272,256]{1,0:T(8,128)(2,1)S(1)}, u32[]{:S(2)}, u32[]{:S(2)}) %collective-permute-start.18) | collective-permute-done | bytes 139296 | tf_op jit(solution)/shard_map/ppermute | solution.py:244
  58.0 2.2 %shard_map.88.u0 = bf16[144,384]{1,0:T(8,128)(2,1)S(1)} custom-call(s32[8,256]{1,0:T(8,128)S(1)} %shard_map.82.target_ref, bf16[384,128]{1,0:T(8,128)(2,1)S(1)} %bitcast.10, bf16[272,256]{1,0:T(8,128)(2,1)S(1)} %shard_map.87.refs_0_, bf16[272,256]{1,0:T(8,128)(2,1)S(1)} %collective-permute-done.12.refs_1_, ...), custom_call_target="tpu_custom_call" | custom-call | bytes 7500000 | tf_op jit(solution)/shard_map/pallas_call | solution.py:18
  60.3 1.6 %collective-permute-start.20 = (bf16[144,384]{1,0:T(8,128)(2,1)S(1)}, bf16[144,384]{1,0:T(8,128)(2,1)S(1)}, u32[]{:S(2)}, u32[]{:S(2)}) collective-permute-start(bf16[144,384]{1,0:T(8,128)(2,1)S(1)} %shard_map.88.u0), channel_id=1, source_target_pairs={{0,128},{64,192},{128,0},{192,64},{1,129},{65,193},{129,1},{193,65... | collective-permute-start | bytes 331784 | tf_op jit(solution)/shard_map/ppermute | solution.py:228
  61.9 1.7 %collective-permute-start.21 = (bf16[144,384]{1,0:T(8,128)(2,1)S(1)}, bf16[144,384]{1,0:T(8,128)(2,1)S(1)}, u32[]{:S(2)}, u32[]{:S(2)}) collective-permute-start(bf16[144,384]{1,0:T(8,128)(2,1)S(1)} %shard_map.88.u0), channel_id=1, source_target_pairs={{0,192},{64,0},{128,64},{192,128},{1,193},{65,1},{129,65},{193,129... | collective-permute-start | bytes 331784 | tf_op jit(solution)/shard_map/ppermute | solution.py:228
  63.6 4.7 %shard_map.89.r = f32[384,256]{1,0:T(8,128)S(1)} custom-call(s32[3,16]{1,0:T(4,128)S(1)} %copy-done.4, bf16[3,16,8,128]{3,2,1,0:T(8,128)(2,1)S(1)} %copy-done.1, f32[48,2,16]{2,1,0:T(2,128)S(1)} %bitcast.14, bf16[3,16,1,256,256]{4,3,2,1,0:T(8,128)(2,1)} %c_ref.1), custom_call_target="tpu_custom_call" | custom-call | bytes 15000000 | tf_op jit(solution)/shard_map/pallas_call | solution.py:18
  68.3 0.7 collective-permute-done.19.u1
  69.0 0.6 collective-permute-done.21.u3
  69.6 1.2 %shard_map.90 = bf16[48,1024]{1,0:T(8,128)(2,1)} custom-call(bf16[144,384]{1,0:T(8,128)(2,1)S(1)} %shard_map.88.u0, bf16[144,384]{1,0:T(8,128)(2,1)S(1)} %collective-permute-done.19.u1, bf16[144,384]{1,0:T(8,128)(2,1)S(1)} %collective-permute-done.20.u2, bf16[144,384]{1,0:T(8,128)(2,1)S(1)} %collective-permute-done.21.u3, f32[384,256]{1,0:T(8,128)S(1)} %shard_map.89.r), custom_call_target="tpu_custom_call" | custom-call | bytes 3000000 | tf_op jit(solution)/shard_map/pallas_call | solution.py:18
  (37 shorter events, 4.0 us)
Async XLA Ops:
  0.0 63.6 %copy-start.4 = (s32[3,16]{1,0:T(4,128)S(1)}, s32[3,16]{1,0:T(4,128)}, u32[]{:S(2)}) copy-start(s32[3,16]{1,0:T(4,128)} %len_ref.1) | copy-start | bytes 580
  0.0 9.7 %collective-permute-start = (bf16[160,1024]{1,0:T(8,128)(2,1)}, bf16[160,1024]{1,0:T(8,128)(2,1)S(1)}, u32[]{:S(2)}, u32[]{:S(2)}) collective-permute-start(bf16[160,1024]{1,0:T(8,128)(2,1)} %bitcast.11), channel_id=1, source_target_pairs={{0,1},{1,2},{2,3},{3,0},{4,5},{5,6},{6,7},{7,4},{8,9},{9,10},{10,1... | collective-permute-start | bytes 983048 | tf_op jit(solution)/shard_map/ppermute | solution.py:232
  2.2 8.7 %collective-permute-start.1 = (bf16[160,1024]{1,0:T(8,128)(2,1)}, bf16[160,1024]{1,0:T(8,128)(2,1)S(1)}, u32[]{:S(2)}, u32[]{:S(2)}) collective-permute-start(bf16[160,1024]{1,0:T(8,128)(2,1)} %bitcast.12), channel_id=1, source_target_pairs={{0,3},{1,0},{2,1},{3,2},{4,7},{5,4},{6,5},{7,6},{8,11},{9,8},{10,9... | collective-permute-start | bytes 983048 | tf_op jit(solution)/shard_map/ppermute | solution.py:232
  2.2 1.1 %copy-start = (bf16[1280,1,256]{2,0,1:T(8,128)(2,1)S(1)}, bf16[1280,1,256]{2,0,1:T(8,128)(2,1)}, u32[]{:S(2)}) copy-start(bf16[1280,1,256]{2,0,1:T(8,128)(2,1)} %param.9) | copy-start | bytes 1966084
  3.3 1.0 %copy-start.2 = (bf16[1024,160]{0,1:T(8,128)(2,1)S(1)}, bf16[1024,160]{0,1:T(8,128)(2,1)}, u32[]{:S(2)}) copy-start(bf16[1024,160]{0,1:T(8,128)(2,1)} %param.8) | copy-start | bytes 983044
  4.3 53.7 %copy-start.1 = (bf16[3,16,8,128]{3,2,1,0:T(8,128)(2,1)S(1)}, bf16[3,16,8,128]{3,2,1,0:T(8,128)(2,1)}, u32[]{:S(2)}) copy-start(bf16[3,16,8,128]{3,2,1,0:T(8,128)(2,1)} %q_ref.1) | copy-start | bytes 294916
  4.3 59.3 %copy-start.3 = (f32[3,16,1,16,2]{3,4,2,1,0:T(2,128)S(1)}, f32[3,16,1,16,2]{3,4,2,1,0:T(2,128)}, u32[]{:S(2)}) copy-start(f32[3,16,1,16,2]{3,4,2,1,0:T(2,128)} %param.12) | copy-start | bytes 18436
  4.5 9.0 %collective-permute-start.4 = (bf16[256,640]{1,0:T(8,128)(2,1)S(1)}, bf16[256,640]{1,0:T(8,128)(2,1)S(1)}, u32[]{:S(2)}, u32[]{:S(2)}) collective-permute-start(bf16[256,640]{1,0:T(8,128)(2,1)S(1)} %get-tuple-element.29), channel_id=1, source_target_pairs={{0,4},{1,5},{2,6},{3,7},{4,0},{5,1},{6,2},{7,3},{8,12},{9,13},{10,... | collective-permute-start | bytes 983048 | tf_op jit(solution)/shard_map/ppermute | solution.py:236
  6.3 0.7 copy-start.5
  7.0 0.7 copy-start.6
  11.0 5.4 %collective-permute-start.2 = (bf16[80,1024]{1,0:T(8,128)(2,1)S(1)}, bf16[80,1024]{1,0:T(8,128)(2,1)S(1)}, u32[]{:S(2)}, u32[]{:S(2)}) collective-permute-start(bf16[80,1024]{1,0:T(8,128)(2,1)S(1)} %slice.6), channel_id=1, source_target_pairs={{0,1},{1,2},{2,3},{3,0},{4,5},{5,6},{6,7},{7,4},{8,9},{9,10},{10,1... | collective-permute-start | bytes 491528 | tf_op jit(solution)/shard_map/ppermute | solution.py:232
  11.5 6.6 %collective-permute-start.3 = (bf16[80,1024]{1,0:T(8,128)(2,1)S(1)}, bf16[80,1024]{1,0:T(8,128)(2,1)S(1)}, u32[]{:S(2)}, u32[]{:S(2)}) collective-permute-start(bf16[80,1024]{1,0:T(8,128)(2,1)S(1)} %slice.7), channel_id=1, source_target_pairs={{0,3},{1,0},{2,1},{3,2},{4,7},{5,4},{6,5},{7,6},{8,11},{9,8},{10,9... | collective-permute-start | bytes 491528 | tf_op jit(solution)/shard_map/ppermute | solution.py:232
  18.7 9.3 %collective-permute-start.10 = (bf16[256,256]{1,0:T(8,128)(2,1)S(1)}, bf16[256,256]{1,0:T(8,128)(2,1)S(1)}, u32[]{:S(2)}, u32[]{:S(2)}) collective-permute-start(bf16[256,256]{1,0:T(8,128)(2,1)S(1)} %get-tuple-element.42), channel_id=1, source_target_pairs={{0,192},{64,0},{128,64},{192,128},{1,193},{65,1},{129,65},{193,129... | collective-permute-start | bytes 393224 | tf_op jit(solution)/shard_map/ppermute | solution.py:228
  21.8 10.4 %collective-permute-start.8 = (bf16[256,256]{1,0:T(8,128)(2,1)S(1)}, bf16[256,256]{1,0:T(8,128)(2,1)S(1)}, u32[]{:S(2)}, u32[]{:S(2)}) collective-permute-start(bf16[256,256]{1,0:T(8,128)(2,1)S(1)} %get-tuple-element.40), channel_id=1, source_target_pairs={{0,64},{64,128},{128,192},{192,0},{1,65},{65,129},{129,193},{193,1... | collective-permute-start | bytes 393224 | tf_op jit(solution)/shard_map/ppermute | solution.py:228
  21.8 10.4 %collective-permute-start.9 = (bf16[256,256]{1,0:T(8,128)(2,1)S(1)}, bf16[256,256]{1,0:T(8,128)(2,1)S(1)}, u32[]{:S(2)}, u32[]{:S(2)}) collective-permute-start(bf16[256,256]{1,0:T(8,128)(2,1)S(1)} %get-tuple-element.41), channel_id=1, source_target_pairs={{0,128},{64,192},{128,0},{192,64},{1,129},{65,193},{129,1},{193,65... | collective-permute-start | bytes 393224 | tf_op jit(solution)/shard_map/ppermute | solution.py:228
  24.6 9.6 %collective-permute-start.5 = (bf16[256,256]{1,0:T(8,128)(2,1)S(1)}, bf16[256,256]{1,0:T(8,128)(2,1)S(1)}, u32[]{:S(2)}, u32[]{:S(2)}) collective-permute-start(bf16[256,256]{1,0:T(8,128)(2,1)S(1)} %get-tuple-element.37), channel_id=1, source_target_pairs={{0,64},{64,128},{128,192},{192,0},{1,65},{65,129},{129,193},{193,1... | collective-permute-start | bytes 393224 | tf_op jit(solution)/shard_map/ppermute | solution.py:228
  26.5 7.7 %collective-permute-start.6 = (bf16[256,256]{1,0:T(8,128)(2,1)S(1)}, bf16[256,256]{1,0:T(8,128)(2,1)S(1)}, u32[]{:S(2)}, u32[]{:S(2)}) collective-permute-start(bf16[256,256]{1,0:T(8,128)(2,1)S(1)} %get-tuple-element.38), channel_id=1, source_target_pairs={{0,128},{64,192},{128,0},{192,64},{1,129},{65,193},{129,1},{193,65... | collective-permute-start | bytes 393224 | tf_op jit(solution)/shard_map/ppermute | solution.py:228
  27.9 6.7 %collective-permute-start.7 = (bf16[256,256]{1,0:T(8,128)(2,1)S(1)}, bf16[256,256]{1,0:T(8,128)(2,1)S(1)}, u32[]{:S(2)}, u32[]{:S(2)}) collective-permute-start(bf16[256,256]{1,0:T(8,128)(2,1)S(1)} %get-tuple-element.39), channel_id=1, source_target_pairs={{0,192},{64,0},{128,64},{192,128},{1,193},{65,1},{129,65},{193,129... | collective-permute-start | bytes 393224 | tf_op jit(solution)/shard_map/ppermute | solution.py:228
  32.2 6.3 %collective-permute-start.11 = (bf16[256,256]{1,0:T(8,128)(2,1)S(1)}, bf16[256,256]{1,0:T(8,128)(2,1)S(1)}, u32[]{:S(2)}, u32[]{:S(2)}) collective-permute-start(bf16[256,256]{1,0:T(8,128)(2,1)S(1)} %shard_map.86), channel_id=1, source_target_pairs={{0,4},{1,5},{2,6},{3,7},{4,0},{5,1},{6,2},{7,3},{8,12},{9,13},{10,... | collective-permute-start | bytes 393224 | tf_op jit(solution)/shard_map/ppermute | solution.py:236
  38.9 13.6 %collective-permute-start.12 = (bf16[272,256]{1,0:T(8,128)(2,1)S(1)}, bf16[272,256]{1,0:T(8,128)(2,1)S(1)}, u32[]{:S(2)}, u32[]{:S(2)}) collective-permute-start(bf16[272,256]{1,0:T(8,128)(2,1)S(1)} %shard_map.87.refs_0_), channel_id=1, source_target_pairs={{0,16},{8,24},{16,32},{24,40},{32,48},{40,56},{48,0},{56,8},{1,17}... | collective-permute-start | bytes 417800 | tf_op jit(solution)/shard_map/ppermute | solution.py:240
  42.5 11.3 %collective-permute-start.13 = (bf16[272,256]{1,0:T(8,128)(2,1)S(1)}, bf16[272,256]{1,0:T(8,128)(2,1)S(1)}, u32[]{:S(2)}, u32[]{:S(2)}) collective-permute-start(bf16[272,256]{1,0:T(8,128)(2,1)S(1)} %shard_map.87.refs_0_), channel_id=1, source_target_pairs={{0,32},{8,40},{16,48},{24,56},{32,0},{40,8},{48,16},{56,24},{1,33}... | collective-permute-start | bytes 417800 | tf_op jit(solution)/shard_map/ppermute | solution.py:240
  48.5 8.2 %collective-permute-start.14 = (bf16[272,256]{1,0:T(8,128)(2,1)S(1)}, bf16[272,256]{1,0:T(8,128)(2,1)S(1)}, u32[]{:S(2)}, u32[]{:S(2)}) collective-permute-start(bf16[272,256]{1,0:T(8,128)(2,1)S(1)} %shard_map.87.refs_0_), channel_id=1, source_target_pairs={{0,48},{8,56},{16,0},{24,8},{32,16},{40,24},{48,32},{56,40},{1,49}... | collective-permute-start | bytes 417800 | tf_op jit(solution)/shard_map/ppermute | solution.py:240
  52.5 4.2 %collective-permute-start.15 = (bf16[272,256]{1,0:T(8,128)(2,1)S(1)}, bf16[272,256]{1,0:T(8,128)(2,1)S(1)}, u32[]{:S(2)}, u32[]{:S(2)}) collective-permute-start(bf16[272,256]{1,0:T(8,128)(2,1)S(1)} %shard_map.87.refs_0_), channel_id=1, source_target_pairs={{0,8},{8,0},{16,24},{24,16},{32,40},{40,32},{48,56},{56,48},{1,9},... | collective-permute-start | bytes 417800 | tf_op jit(solution)/shard_map/ppermute | solution.py:244
  52.5 4.2 %collective-permute-start.16 = (bf16[272,256]{1,0:T(8,128)(2,1)S(1)}, bf16[272,256]{1,0:T(8,128)(2,1)S(1)}, u32[]{:S(2)}, u32[]{:S(2)}) collective-permute-start(bf16[272,256]{1,0:T(8,128)(2,1)S(1)} %collective-permute-done.12.refs_1_), channel_id=1, source_target_pairs={{0,8},{8,0},{16,24},{24,16},{32,40},{40,32},{48,56},{56,48},{1,9},... | collective-permute-start | bytes 417800 | tf_op jit(solution)/shard_map/ppermute | solution.py:244
  53.8 2.8 %collective-permute-start.17 = (bf16[272,256]{1,0:T(8,128)(2,1)S(1)}, bf16[272,256]{1,0:T(8,128)(2,1)S(1)}, u32[]{:S(2)}, u32[]{:S(2)}) collective-permute-start(bf16[272,256]{1,0:T(8,128)(2,1)S(1)} %collective-permute-done.13.refs_2_), channel_id=1, source_target_pairs={{0,8},{8,0},{16,24},{24,16},{32,40},{40,32},{48,56},{56,48},{1,9},... | collective-permute-start | bytes 417800 | tf_op jit(solution)/shard_map/ppermute | solution.py:244
  56.7 1.4 %collective-permute-start.18 = (bf16[272,256]{1,0:T(8,128)(2,1)S(1)}, bf16[272,256]{1,0:T(8,128)(2,1)S(1)}, u32[]{:S(2)}, u32[]{:S(2)}) collective-permute-start(bf16[272,256]{1,0:T(8,128)(2,1)S(1)} %collective-permute-done.14.refs_3_), channel_id=1, source_target_pairs={{0,8},{8,0},{16,24},{24,16},{32,40},{40,32},{48,56},{56,48},{1,9},... | collective-permute-start | bytes 417800 | tf_op jit(solution)/shard_map/ppermute | solution.py:244
  60.2 8.8 %collective-permute-start.19 = (bf16[144,384]{1,0:T(8,128)(2,1)S(1)}, bf16[144,384]{1,0:T(8,128)(2,1)S(1)}, u32[]{:S(2)}, u32[]{:S(2)}) collective-permute-start(bf16[144,384]{1,0:T(8,128)(2,1)S(1)} %shard_map.88.u0), channel_id=1, source_target_pairs={{0,64},{64,128},{128,192},{192,0},{1,65},{65,129},{129,193},{193,1... | collective-permute-start | bytes 331784 | tf_op jit(solution)/shard_map/ppermute | solution.py:228
  60.3 8.7 %collective-permute-start.20 = (bf16[144,384]{1,0:T(8,128)(2,1)S(1)}, bf16[144,384]{1,0:T(8,128)(2,1)S(1)}, u32[]{:S(2)}, u32[]{:S(2)}) collective-permute-start(bf16[144,384]{1,0:T(8,128)(2,1)S(1)} %shard_map.88.u0), channel_id=1, source_target_pairs={{0,128},{64,192},{128,0},{192,64},{1,129},{65,193},{129,1},{193,65... | collective-permute-start | bytes 331784 | tf_op jit(solution)/shard_map/ppermute | solution.py:228
  61.9 7.7 %collective-permute-start.21 = (bf16[144,384]{1,0:T(8,128)(2,1)S(1)}, bf16[144,384]{1,0:T(8,128)(2,1)S(1)}, u32[]{:S(2)}, u32[]{:S(2)}) collective-permute-start(bf16[144,384]{1,0:T(8,128)(2,1)S(1)} %shard_map.88.u0), channel_id=1, source_target_pairs={{0,192},{64,0},{128,64},{192,128},{1,193},{65,1},{129,65},{193,129... | collective-permute-start | bytes 331784 | tf_op jit(solution)/shard_map/ppermute | solution.py:228

commit v3 on v2

--- a/solution.py
+++ b/solution.py
@@ -122,23 +122,19 @@
         out_ref[pl.ds(group * 128, 128), 128:] = jnp.where(lane128 == 0, m, den)
 
 
-def project_kernel(w_ref, *refs):
-    p, outs = refs[:5], refs[5:]
-    role = lax.axis_index("role")
+def project_kernel(keep_ref, got_ref, *refs):
+    p, out_ref = refs[:5], refs[5]
+    zl = lax.axis_index("tensor") // 4
     count = p[0].shape[1] // 4
-    for d in (2, 1, 3, 0):
-        start = pl.multiple_of(lax.rem(role + d, 4) * count, 128)
-        rows = jnp.concatenate([r[:, pl.ds(start, count)] for r in p], axis=0)
-        outs[d][...] = dot(w_ref[...], rows, 1, 0).astype(outs[d].dtype)
-
-
-def total_of(parts):
-    a, b, c, d = [p[...].astype(F32) for p in parts]
-    return (a + b) + (c + d)
-
-
-def sum_kernel(a, b, c, d, out_ref):
-    out_ref[...] = total_of((a, b, c, d)).astype(BF16)
+    for r in range(4):
+        rows = jnp.concatenate([ref[:, pl.ds(r * count, count)] for ref in p], axis=0)
+        out_ref[r * 2 + zl] = dot(keep_ref[...], rows, 1, 0).astype(BF16)
+        out_ref[r * 2 + 1 - zl] = dot(got_ref[...], rows, 1, 0).astype(BF16)
+
+
+def total_of(ref):
+    a = [ref[i].astype(F32) for i in range(8)]
+    return ((a[0] + a[1]) + (a[2] + a[3])) + ((a[4] + a[5]) + (a[6] + a[7]))
 
 
 def group_max(v):
@@ -156,8 +152,8 @@
     return (kv / scale).astype(BF16), scale
 
 
-def quantize_kernel(a, b, c, d, got, out_ref):
-    kv = total_of((a, b, c, d)) + got[...].astype(F32)
+def quantize_kernel(sum_ref, out_ref):
+    kv = total_of(sum_ref)
     key_codes, key_scale = quantize(kv[:128])
     value_codes, value_scale = quantize(kv[128:])
     out_ref[pl.ds(0, 128), :] = key_codes
@@ -263,14 +259,10 @@
     pieces = (held, p1, p2, p3a, p3b)
 
     count = p0.shape[1] // 4
-    outs = [shape(256, count, dtype=F32 if d == 0 else BF16) for d in range(4)]
-    far = call(project_kernel, outs, (got, *pieces), [VMEM] * 6)
-    far_sums = [far[0]] + [role_shift(far[d], d) for d in (1, 2, 3)]
-    pieces, _ = lax.optimization_barrier((pieces, far[0]))
-    near = call(project_kernel, outs, (keep, *pieces), [VMEM] * 6)
-    sums = [near[0]] + [role_shift(near[d], d) for d in (1, 2, 3)]
-    back = z_swap(call(sum_kernel, shape(256, count), far_sums, [VMEM] * 4))
-    codes_out = call(quantize_kernel, shape(272, count), (*sums, back), [VMEM] * 5)
+    outs = call(project_kernel, shape(8, 256, count), (keep, got, *pieces), [VMEM] * 7)
+    groups = [[r * 8 + z * 4 + x for r in range(4) for z in range(2)] for x in range(4)]
+    sums = lax.all_to_all(outs, ("role", "tensor"), 0, 0, axis_index_groups=groups)
+    codes_out = call(quantize_kernel, shape(272, count), (sums,), [VMEM])
 
     parts = [codes_out] + [zh_shift(codes_out, d) for d in (1, 2, 3)]
     parts = parts + [core_swap(v) for v in parts]

time: 71 us -> 69.9 us (0.985)
  blocking collectives: 0 us -> 19 us
  starting transfers between devices: 37.7 us -> 20.9 us
  waiting for transfers between devices: 19.3 us -> 16.3 us
    all_to_all x0 -> x1, blocking collectives: none -> 19 us  [body(): lax.all_to_all(outs, ('role', 'tensor'), 0, 0, axis_index_groups=groups)]
    ppermute x9 -> x3, starting transfers between devices: 15.4 us -> 4.13 us  [role_shift(): return lax.ppermute(v, 'role', [(i, (i + d) % 4) for i in range(4)])]
    ppermute x2 -> x1, waiting for transfers between devices: 4.2 us -> 0.33 us  [z_swap(): return lax.ppermute(v, 'tensor', [(t, (t + 4) % 8) for t in range(8)])]
    ppermute x3, starting transfers between devices: 13.6 us -> 10.5 us  [zh_shift(): return lax.ppermute(v, 'batch', [(i, (i + 2 * d) % 8) for i in range(8)])]
    ppermute x3, waiting for transfers between devices: 3.64 us -> 6.33 us  [zh_shift(): return lax.ppermute(v, 'batch', [(i, (i + 2 * d) % 8) for i in range(8)])]
    ppermute x2 -> x1, starting transfers between devices: 3.8 us -> 1.81 us  [z_swap(): return lax.ppermute(v, 'tensor', [(t, (t + 4) % 8) for t in range(8)])]
    ppermute x9 -> x3, waiting for transfers between devices: 2.56 us -> 0.65 us  [role_shift(): return lax.ppermute(v, 'role', [(i, (i + d) % 4) for i in range(4)])]
    pallas_call x9 -> x7, Pallas kernels: 10.2 us -> 10 us  [call(): pl.pallas_call(kernel, out_shape=outs, in_specs=specs, out_specs=jax.tree...]
  transfers between devices with their start and end apart: 22 -> 15, of which waited for: 13 -> 11; matrix products, arithmetic and copies ran while one was open for 0% -> 0% of each run, Pallas kernels for 8% -> 7%
where the time goes in v3:
time: 69.9 us; the launch traced here: 69.7 us
  starting transfers between devices  20.9 us (30%)
  blocking collectives  19 us (27%)
  waiting for transfers between devices  16.3 us (23%)
  Pallas kernels  10 us (14%)
  local copies, waits for them, and re-layouts  3.46 us (5%)
    all_to_all x1, blocking collectives, body(): lax.all_to_all(outs, ('role', 'tensor'), 0, 0, axis_index_groups=groups)  19 us
    ppermute x3, starting transfers between devices, zh_shift(): return lax.ppermute(v, 'batch', [(i, (i + 2 * d) % 8) for i in range(8)])  10.5 us
    pallas_call x7, Pallas kernels, call(): pl.pallas_call(kernel, out_shape=outs, in_specs=specs, out_specs=jax.tree...  10 us
    ppermute x4, waiting for transfers between devices, x_shift(): lax.ppermute(v, 'tensor', [(z * 4 + x, z * 4 + (x + d) % 4) for z in rang...  7.6 us
    ppermute x3, waiting for transfers between devices, zh_shift(): return lax.ppermute(v, 'batch', [(i, (i + 2 * d) % 8) for i in range(8)])  6.33 us
    ppermute x4, starting transfers between devices, x_shift(): lax.ppermute(v, 'tensor', [(z * 4 + x, z * 4 + (x + d) % 4) for z in rang...  4.4 us
    ppermute x3, starting transfers between devices, role_shift(): return lax.ppermute(v, 'role', [(i, (i + d) % 4) for i in range(4)])  4.13 us
    unnamed x14, local copies, waits for them, and re-layouts  3.43 us
  transfers between devices with their start and end apart: 15, of which 11 were waited for; matrix products, arithmetic and copies ran while one was open for 0% of the time, Pallas kernels for 7%

profile of v3, /device:TPU:6, one launch (start us, length us, event | category | flops | bytes accessed | tf_op | source)
XLA Modules:
  0.0 69.7 jit_solution(4519165116052395450)
XLA Ops:
  0.0 2.2 %collective-permute-start = (bf16[160,1024]{1,0:T(8,128)(2,1)}, bf16[160,1024]{1,0:T(8,128)(2,1)S(1)}, u32[]{:S(2)}, u32[]{:S(2)}) collective-permute-start(bf16[160,1024]{1,0:T(8,128)(2,1)} %bitcast.11), channel_id=1, source_target_pairs={{0,1},{1,2},{2,3},{3,0},{4,5},{5,6},{6,7},{7,4},{8,9},{9,10},{10,1... | collective-permute-start | bytes 983048 | tf_op jit(solution)/shard_map/ppermute | solution.py:228
  2.2 1.1 %copy-done = bf16[1280,1,256]{2,0,1:T(8,128)(2,1)S(1)} copy-done((bf16[1280,1,256]{2,0,1:T(8,128)(2,1)S(1)}, bf16[1280,1,256]{2,0,1:T(8,128)(2,1)}, u32[]{:S(2)}) %copy-start) | copy-done | bytes 655384
  3.3 1.0 %copy-done.2 = bf16[1024,160]{0,1:T(8,128)(2,1)S(1)} copy-done((bf16[1024,160]{0,1:T(8,128)(2,1)S(1)}, bf16[1024,160]{0,1:T(8,128)(2,1)}, u32[]{:S(2)}) %copy-start.2) | copy-done | bytes 327704
  4.3 0.2 shard_map.83
  4.5 1.8 %collective-permute-start.2 = (bf16[256,640]{1,0:T(8,128)(2,1)S(1)}, bf16[256,640]{1,0:T(8,128)(2,1)S(1)}, u32[]{:S(2)}, u32[]{:S(2)}) collective-permute-start(bf16[256,640]{1,0:T(8,128)(2,1)S(1)} %get-tuple-element.13), channel_id=1, source_target_pairs={{0,4},{1,5},{2,6},{3,7},{4,0},{5,1},{6,2},{7,3},{8,12},{9,13},{10,... | collective-permute-start | bytes 983048 | tf_op jit(solution)/shard_map/ppermute | solution.py:232
  6.3 0.7 copy-done.5
  7.0 0.7 copy-done.6
  7.7 0.2 shard_map.82.target_ref
  7.9 1.7 %collective-permute-done.refs_1_ = bf16[160,1024]{1,0:T(8,128)(2,1)S(1)} collective-permute-done((bf16[160,1024]{1,0:T(8,128)(2,1)}, bf16[160,1024]{1,0:T(8,128)(2,1)S(1)}, u32[]{:S(2)}, u32[]{:S(2)}) %collective-permute-start) | collective-permute-done | bytes 327712 | tf_op jit(solution)/shard_map/ppermute | solution.py:228
  9.7 1.3 %collective-permute-done.1.refs_2_ = bf16[160,1024]{1,0:T(8,128)(2,1)S(1)} collective-permute-done((bf16[160,1024]{1,0:T(8,128)(2,1)}, bf16[160,1024]{1,0:T(8,128)(2,1)S(1)}, u32[]{:S(2)}, u32[]{:S(2)}) %collective-permute-start.1) | collective-permute-done | bytes 327712 | tf_op jit(solution)/shard_map/ppermute | solution.py:228
  11.0 0.5 collective-permute-start.3
  11.5 1.7 %collective-permute-start.4 = (bf16[80,1024]{1,0:T(8,128)(2,1)S(1)}, bf16[80,1024]{1,0:T(8,128)(2,1)S(1)}, u32[]{:S(2)}, u32[]{:S(2)}) collective-permute-start(bf16[80,1024]{1,0:T(8,128)(2,1)S(1)} %slice.7), channel_id=1, source_target_pairs={{0,3},{1,0},{2,1},{3,2},{4,7},{5,4},{6,5},{7,6},{8,11},{9,8},{10,9... | collective-permute-start | bytes 491528 | tf_op jit(solution)/shard_map/ppermute | solution.py:228
  13.2 0.3 collective-permute-done.2.got_ref
  13.5 2.9 %collective-permute-done.3.refs_3_ = bf16[80,1024]{1,0:T(8,128)(2,1)S(1)} collective-permute-done((bf16[80,1024]{1,0:T(8,128)(2,1)S(1)}, bf16[80,1024]{1,0:T(8,128)(2,1)S(1)}, u32[]{:S(2)}, u32[]{:S(2)}) %collective-permute-start.3) | collective-permute-done | bytes 163872 | tf_op jit(solution)/shard_map/ppermute | solution.py:228
  16.4 1.7 %collective-permute-done.4.refs_4_ = bf16[80,1024]{1,0:T(8,128)(2,1)S(1)} collective-permute-done((bf16[80,1024]{1,0:T(8,128)(2,1)S(1)}, bf16[80,1024]{1,0:T(8,128)(2,1)S(1)}, u32[]{:S(2)}, u32[]{:S(2)}) %collective-permute-start.4) | collective-permute-done | bytes 163872 | tf_op jit(solution)/shard_map/ppermute | solution.py:228
  18.1 1.0 %shard_map.84 = bf16[8,256,256]{2,1,0:T(8,128)(2,1)S(1)} custom-call(bf16[256,640]{1,0:T(8,128)(2,1)S(1)} %get-tuple-element.12.keep_ref, bf16[256,640]{1,0:T(8,128)(2,1)S(1)} %collective-permute-done.2.got_ref, bf16[160,1024]{1,0:T(8,128)(2,1)S(1)} %get-tuple-element.14.refs_0_, bf16[160,1024]{1,0:T(8,128)(2,1)S(1)} %collective-permute-done.refs_1_, ...), custom_call_target="tpu_custom_call" | custom-call | bytes 3000000 | tf_op jit(solution)/shard_map/pallas_call | solution.py:18
  19.1 19.0 %all_to_all.5.sum_ref = bf16[8,256,256]{2,1,0:T(8,128)(2,1)S(1)} all-to-all(bf16[8,256,256]{2,1,0:T(8,128)(2,1)S(1)} %shard_map.84), channel_id=1, replica_groups={{0,4,64,68,128,132,192,196},{1,5,65,69,129,133,193,197},{2,6,66,70,130,..., dimensions={0} | all-to-all | bytes 2097152 | tf_op jit(solution)/shard_map/all_to_all | solution.py:264
  38.1 0.5 shard_map.85.refs_0_
  38.6 3.3 %collective-permute-start.5 = (bf16[272,256]{1,0:T(8,128)(2,1)S(1)}, bf16[272,256]{1,0:T(8,128)(2,1)S(1)}, u32[]{:S(2)}, u32[]{:S(2)}) collective-permute-start(bf16[272,256]{1,0:T(8,128)(2,1)S(1)} %shard_map.85.refs_0_), channel_id=1, source_target_pairs={{0,16},{8,24},{16,32},{24,40},{32,48},{40,56},{48,0},{56,8},{1,17}... | collective-permute-start | bytes 417800 | tf_op jit(solution)/shard_map/ppermute | solution.py:236
  41.9 4.5 %collective-permute-start.6 = (bf16[272,256]{1,0:T(8,128)(2,1)S(1)}, bf16[272,256]{1,0:T(8,128)(2,1)S(1)}, u32[]{:S(2)}, u32[]{:S(2)}) collective-permute-start(bf16[272,256]{1,0:T(8,128)(2,1)S(1)} %shard_map.85.refs_0_), channel_id=1, source_target_pairs={{0,32},{8,40},{16,48},{24,56},{32,0},{40,8},{48,16},{56,24},{1,33}... | collective-permute-start | bytes 417800 | tf_op jit(solution)/shard_map/ppermute | solution.py:236
  46.4 2.7 %collective-permute-start.7 = (bf16[272,256]{1,0:T(8,128)(2,1)S(1)}, bf16[272,256]{1,0:T(8,128)(2,1)S(1)}, u32[]{:S(2)}, u32[]{:S(2)}) collective-permute-start(bf16[272,256]{1,0:T(8,128)(2,1)S(1)} %shard_map.85.refs_0_), channel_id=1, source_target_pairs={{0,48},{8,56},{16,0},{24,8},{32,16},{40,24},{48,32},{56,40},{1,49}... | collective-permute-start | bytes 417800 | tf_op jit(solution)/shard_map/ppermute | solution.py:236
  49.1 1.0 %collective-permute-done.5.refs_1_ = bf16[272,256]{1,0:T(8,128)(2,1)S(1)} collective-permute-done((bf16[272,256]{1,0:T(8,128)(2,1)S(1)}, bf16[272,256]{1,0:T(8,128)(2,1)S(1)}, u32[]{:S(2)}, u32[]{:S(2)}) %collective-permute-start.5) | collective-permute-done | bytes 139296 | tf_op jit(solution)/shard_map/ppermute | solution.py:236
  50.1 3.4 %collective-permute-done.6.refs_2_ = bf16[272,256]{1,0:T(8,128)(2,1)S(1)} collective-permute-done((bf16[272,256]{1,0:T(8,128)(2,1)S(1)}, bf16[272,256]{1,0:T(8,128)(2,1)S(1)}, u32[]{:S(2)}, u32[]{:S(2)}) %collective-permute-start.6) | collective-permute-done | bytes 139296 | tf_op jit(solution)/shard_map/ppermute | solution.py:236
  53.5 1.9 %collective-permute-done.7.refs_3_ = bf16[272,256]{1,0:T(8,128)(2,1)S(1)} collective-permute-done((bf16[272,256]{1,0:T(8,128)(2,1)S(1)}, bf16[272,256]{1,0:T(8,128)(2,1)S(1)}, u32[]{:S(2)}, u32[]{:S(2)}) %collective-permute-start.7) | collective-permute-done | bytes 139296 | tf_op jit(solution)/shard_map/ppermute | solution.py:236
  55.4 1.3 %collective-permute-done.11.refs_7_ = bf16[272,256]{1,0:T(8,128)(2,1)S(1)} collective-permute-done((bf16[272,256]{1,0:T(8,128)(2,1)S(1)}, bf16[272,256]{1,0:T(8,128)(2,1)S(1)}, u32[]{:S(2)}, u32[]{:S(2)}) %collective-permute-start.11) | collective-permute-done | bytes 139296 | tf_op jit(solution)/shard_map/ppermute | solution.py:240
  56.8 2.2 %shard_map.86.u0 = bf16[144,384]{1,0:T(8,128)(2,1)S(1)} custom-call(s32[8,256]{1,0:T(8,128)S(1)} %shard_map.82.target_ref, bf16[384,128]{1,0:T(8,128)(2,1)S(1)} %bitcast.10, bf16[272,256]{1,0:T(8,128)(2,1)S(1)} %shard_map.85.refs_0_, bf16[272,256]{1,0:T(8,128)(2,1)S(1)} %collective-permute-done.5.refs_1_, ...), custom_call_target="tpu_custom_call" | custom-call | bytes 7500000 | tf_op jit(solution)/shard_map/pallas_call | solution.py:18
  59.0 1.3 %collective-permute-start.12 = (bf16[144,384]{1,0:T(8,128)(2,1)S(1)}, bf16[144,384]{1,0:T(8,128)(2,1)S(1)}, u32[]{:S(2)}, u32[]{:S(2)}) collective-permute-start(bf16[144,384]{1,0:T(8,128)(2,1)S(1)} %shard_map.86.u0), channel_id=1, source_target_pairs={{0,64},{64,128},{128,192},{192,0},{1,65},{65,129},{129,193},{193,1... | collective-permute-start | bytes 331784 | tf_op jit(solution)/shard_map/ppermute | solution.py:224
  60.3 0.3 collective-permute-start.13
  60.6 2.5 %collective-permute-start.14 = (bf16[144,384]{1,0:T(8,128)(2,1)S(1)}, bf16[144,384]{1,0:T(8,128)(2,1)S(1)}, u32[]{:S(2)}, u32[]{:S(2)}) collective-permute-start(bf16[144,384]{1,0:T(8,128)(2,1)S(1)} %shard_map.86.u0), channel_id=1, source_target_pairs={{0,192},{64,0},{128,64},{192,128},{1,193},{65,1},{129,65},{193,129... | collective-permute-start | bytes 331784 | tf_op jit(solution)/shard_map/ppermute | solution.py:224
  63.1 4.7 %shard_map.87.r = f32[384,256]{1,0:T(8,128)S(1)} custom-call(s32[3,16]{1,0:T(4,128)S(1)} %copy-done.4, bf16[3,16,8,128]{3,2,1,0:T(8,128)(2,1)S(1)} %copy-done.1, f32[48,2,16]{2,1,0:T(2,128)S(1)} %bitcast.14, bf16[3,16,1,256,256]{4,3,2,1,0:T(8,128)(2,1)} %c_ref.1), custom_call_target="tpu_custom_call" | custom-call | bytes 15000000 | tf_op jit(solution)/shard_map/pallas_call | solution.py:18
  67.9 0.6 collective-permute-done.14.u3
  68.5 1.2 %shard_map.88 = bf16[48,1024]{1,0:T(8,128)(2,1)} custom-call(bf16[144,384]{1,0:T(8,128)(2,1)S(1)} %shard_map.86.u0, bf16[144,384]{1,0:T(8,128)(2,1)S(1)} %collective-permute-done.12.u1, bf16[144,384]{1,0:T(8,128)(2,1)S(1)} %collective-permute-done.13.u2, bf16[144,384]{1,0:T(8,128)(2,1)S(1)} %collective-permute-done.14.u3, f32[384,256]{1,0:T(8,128)S(1)} %shard_map.87.r), custom_call_target="tpu_custom_call" | custom-call | bytes 3000000 | tf_op jit(solution)/shard_map/pallas_call | solution.py:18
  (22 shorter events, 0.1 us)
Async XLA Ops:
  0.0 63.1 %copy-start.4 = (s32[3,16]{1,0:T(4,128)S(1)}, s32[3,16]{1,0:T(4,128)}, u32[]{:S(2)}) copy-start(s32[3,16]{1,0:T(4,128)} %len_ref.1) | copy-start | bytes 580
  0.0 9.7 %collective-permute-start = (bf16[160,1024]{1,0:T(8,128)(2,1)}, bf16[160,1024]{1,0:T(8,128)(2,1)S(1)}, u32[]{:S(2)}, u32[]{:S(2)}) collective-permute-start(bf16[160,1024]{1,0:T(8,128)(2,1)} %bitcast.11), channel_id=1, source_target_pairs={{0,1},{1,2},{2,3},{3,0},{4,5},{5,6},{6,7},{7,4},{8,9},{9,10},{10,1... | collective-permute-start | bytes 983048 | tf_op jit(solution)/shard_map/ppermute | solution.py:228
  2.2 8.7 %collective-permute-start.1 = (bf16[160,1024]{1,0:T(8,128)(2,1)}, bf16[160,1024]{1,0:T(8,128)(2,1)S(1)}, u32[]{:S(2)}, u32[]{:S(2)}) collective-permute-start(bf16[160,1024]{1,0:T(8,128)(2,1)} %bitcast.12), channel_id=1, source_target_pairs={{0,3},{1,0},{2,1},{3,2},{4,7},{5,4},{6,5},{7,6},{8,11},{9,8},{10,9... | collective-permute-start | bytes 983048 | tf_op jit(solution)/shard_map/ppermute | solution.py:228
  2.2 1.1 %copy-start = (bf16[1280,1,256]{2,0,1:T(8,128)(2,1)S(1)}, bf16[1280,1,256]{2,0,1:T(8,128)(2,1)}, u32[]{:S(2)}) copy-start(bf16[1280,1,256]{2,0,1:T(8,128)(2,1)} %param.9) | copy-start | bytes 1966084
  3.3 1.0 %copy-start.2 = (bf16[1024,160]{0,1:T(8,128)(2,1)S(1)}, bf16[1024,160]{0,1:T(8,128)(2,1)}, u32[]{:S(2)}) copy-start(bf16[1024,160]{0,1:T(8,128)(2,1)} %param.8) | copy-start | bytes 983044
  4.3 52.5 %copy-start.1 = (bf16[3,16,8,128]{3,2,1,0:T(8,128)(2,1)S(1)}, bf16[3,16,8,128]{3,2,1,0:T(8,128)(2,1)}, u32[]{:S(2)}) copy-start(bf16[3,16,8,128]{3,2,1,0:T(8,128)(2,1)} %q_ref.1) | copy-start | bytes 294916
  4.3 58.8 %copy-start.3 = (f32[3,16,1,16,2]{3,4,2,1,0:T(2,128)S(1)}, f32[3,16,1,16,2]{3,4,2,1,0:T(2,128)}, u32[]{:S(2)}) copy-start(f32[3,16,1,16,2]{3,4,2,1,0:T(2,128)} %param.12) | copy-start | bytes 18436
  4.5 9.0 %collective-permute-start.2 = (bf16[256,640]{1,0:T(8,128)(2,1)S(1)}, bf16[256,640]{1,0:T(8,128)(2,1)S(1)}, u32[]{:S(2)}, u32[]{:S(2)}) collective-permute-start(bf16[256,640]{1,0:T(8,128)(2,1)S(1)} %get-tuple-element.13), channel_id=1, source_target_pairs={{0,4},{1,5},{2,6},{3,7},{4,0},{5,1},{6,2},{7,3},{8,12},{9,13},{10,... | collective-permute-start | bytes 983048 | tf_op jit(solution)/shard_map/ppermute | solution.py:232
  6.3 0.7 copy-start.5
  7.0 0.7 copy-start.6
  11.0 5.4 %collective-permute-start.3 = (bf16[80,1024]{1,0:T(8,128)(2,1)S(1)}, bf16[80,1024]{1,0:T(8,128)(2,1)S(1)}, u32[]{:S(2)}, u32[]{:S(2)}) collective-permute-start(bf16[80,1024]{1,0:T(8,128)(2,1)S(1)} %slice.6), channel_id=1, source_target_pairs={{0,1},{1,2},{2,3},{3,0},{4,5},{5,6},{6,7},{7,4},{8,9},{9,10},{10,1... | collective-permute-start | bytes 491528 | tf_op jit(solution)/shard_map/ppermute | solution.py:228
  11.5 6.6 %collective-permute-start.4 = (bf16[80,1024]{1,0:T(8,128)(2,1)S(1)}, bf16[80,1024]{1,0:T(8,128)(2,1)S(1)}, u32[]{:S(2)}, u32[]{:S(2)}) collective-permute-start(bf16[80,1024]{1,0:T(8,128)(2,1)S(1)} %slice.7), channel_id=1, source_target_pairs={{0,3},{1,0},{2,1},{3,2},{4,7},{5,4},{6,5},{7,6},{8,11},{9,8},{10,9... | collective-permute-start | bytes 491528 | tf_op jit(solution)/shard_map/ppermute | solution.py:228
  38.6 11.5 %collective-permute-start.5 = (bf16[272,256]{1,0:T(8,128)(2,1)S(1)}, bf16[272,256]{1,0:T(8,128)(2,1)S(1)}, u32[]{:S(2)}, u32[]{:S(2)}) collective-permute-start(bf16[272,256]{1,0:T(8,128)(2,1)S(1)} %shard_map.85.refs_0_), channel_id=1, source_target_pairs={{0,16},{8,24},{16,32},{24,40},{32,48},{40,56},{48,0},{56,8},{1,17}... | collective-permute-start | bytes 417800 | tf_op jit(solution)/shard_map/ppermute | solution.py:236
  41.9 11.6 %collective-permute-start.6 = (bf16[272,256]{1,0:T(8,128)(2,1)S(1)}, bf16[272,256]{1,0:T(8,128)(2,1)S(1)}, u32[]{:S(2)}, u32[]{:S(2)}) collective-permute-start(bf16[272,256]{1,0:T(8,128)(2,1)S(1)} %shard_map.85.refs_0_), channel_id=1, source_target_pairs={{0,32},{8,40},{16,48},{24,56},{32,0},{40,8},{48,16},{56,24},{1,33}... | collective-permute-start | bytes 417800 | tf_op jit(solution)/shard_map/ppermute | solution.py:236
  46.4 9.0 %collective-permute-start.7 = (bf16[272,256]{1,0:T(8,128)(2,1)S(1)}, bf16[272,256]{1,0:T(8,128)(2,1)S(1)}, u32[]{:S(2)}, u32[]{:S(2)}) collective-permute-start(bf16[272,256]{1,0:T(8,128)(2,1)S(1)} %shard_map.85.refs_0_), channel_id=1, source_target_pairs={{0,48},{8,56},{16,0},{24,8},{32,16},{40,24},{48,32},{56,40},{1,49}... | collective-permute-start | bytes 417800 | tf_op jit(solution)/shard_map/ppermute | solution.py:236
  49.1 6.4 %collective-permute-start.8 = (bf16[272,256]{1,0:T(8,128)(2,1)S(1)}, bf16[272,256]{1,0:T(8,128)(2,1)S(1)}, u32[]{:S(2)}, u32[]{:S(2)}) collective-permute-start(bf16[272,256]{1,0:T(8,128)(2,1)S(1)} %shard_map.85.refs_0_), channel_id=1, source_target_pairs={{0,8},{8,0},{16,24},{24,16},{32,40},{40,32},{48,56},{56,48},{1,9},... | collective-permute-start | bytes 417800 | tf_op jit(solution)/shard_map/ppermute | solution.py:240
  50.1 5.3 %collective-permute-start.9 = (bf16[272,256]{1,0:T(8,128)(2,1)S(1)}, bf16[272,256]{1,0:T(8,128)(2,1)S(1)}, u32[]{:S(2)}, u32[]{:S(2)}) collective-permute-start(bf16[272,256]{1,0:T(8,128)(2,1)S(1)} %collective-permute-done.5.refs_1_), channel_id=1, source_target_pairs={{0,8},{8,0},{16,24},{24,16},{32,40},{40,32},{48,56},{56,48},{1,9},... | collective-permute-start | bytes 417800 | tf_op jit(solution)/shard_map/ppermute | solution.py:240
  53.5 1.9 %collective-permute-start.10 = (bf16[272,256]{1,0:T(8,128)(2,1)S(1)}, bf16[272,256]{1,0:T(8,128)(2,1)S(1)}, u32[]{:S(2)}, u32[]{:S(2)}) collective-permute-start(bf16[272,256]{1,0:T(8,128)(2,1)S(1)} %collective-permute-done.6.refs_2_), channel_id=1, source_target_pairs={{0,8},{8,0},{16,24},{24,16},{32,40},{40,32},{48,56},{56,48},{1,9},... | collective-permute-start | bytes 417800 | tf_op jit(solution)/shard_map/ppermute | solution.py:240
  55.4 1.4 %collective-permute-start.11 = (bf16[272,256]{1,0:T(8,128)(2,1)S(1)}, bf16[272,256]{1,0:T(8,128)(2,1)S(1)}, u32[]{:S(2)}, u32[]{:S(2)}) collective-permute-start(bf16[272,256]{1,0:T(8,128)(2,1)S(1)} %collective-permute-done.7.refs_3_), channel_id=1, source_target_pairs={{0,8},{8,0},{16,24},{24,16},{32,40},{40,32},{48,56},{56,48},{1,9},... | collective-permute-start | bytes 417800 | tf_op jit(solution)/shard_map/ppermute | solution.py:240
  59.0 8.9 %collective-permute-start.12 = (bf16[144,384]{1,0:T(8,128)(2,1)S(1)}, bf16[144,384]{1,0:T(8,128)(2,1)S(1)}, u32[]{:S(2)}, u32[]{:S(2)}) collective-permute-start(bf16[144,384]{1,0:T(8,128)(2,1)S(1)} %shard_map.86.u0), channel_id=1, source_target_pairs={{0,64},{64,128},{128,192},{192,0},{1,65},{65,129},{129,193},{193,1... | collective-permute-start | bytes 331784 | tf_op jit(solution)/shard_map/ppermute | solution.py:224
  60.3 7.7 %collective-permute-start.13 = (bf16[144,384]{1,0:T(8,128)(2,1)S(1)}, bf16[144,384]{1,0:T(8,128)(2,1)S(1)}, u32[]{:S(2)}, u32[]{:S(2)}) collective-permute-start(bf16[144,384]{1,0:T(8,128)(2,1)S(1)} %shard_map.86.u0), channel_id=1, source_target_pairs={{0,128},{64,192},{128,0},{192,64},{1,129},{65,193},{129,1},{193,65... | collective-permute-start | bytes 331784 | tf_op jit(solution)/shard_map/ppermute | solution.py:224
  60.6 7.9 %collective-permute-start.14 = (bf16[144,384]{1,0:T(8,128)(2,1)S(1)}, bf16[144,384]{1,0:T(8,128)(2,1)S(1)}, u32[]{:S(2)}, u32[]{:S(2)}) collective-permute-start(bf16[144,384]{1,0:T(8,128)(2,1)S(1)} %shard_map.86.u0), channel_id=1, source_target_pairs={{0,192},{64,0},{128,64},{192,128},{1,193},{65,1},{129,65},{193,129... | collective-permute-start | bytes 331784 | tf_op jit(solution)/shard_map/ppermute | solution.py:224

commit v4 on v3

--- a/solution.py
+++ b/solution.py
@@ -65,18 +65,39 @@
         out_ref[pl.ds(128, 128), :] = jnp.transpose(tmp[:, 128:]).astype(BF16)
 
 
-def target_kernel(dest_ref, row_ref, out_ref):
+def plan_kernel(dest_ref, row_ref, turn_ref, window_ref, target_ref, tmp):
     batch, role = lax.axis_index("batch"), lax.axis_index("role")
-    lane = lax.broadcasted_iota(jnp.int32, (8, 512), 1)
+    zh = batch // 2
+    dest = dest_ref[...]
+    key = (dest & 7) >> 1
+    index = lax.broadcasted_iota(jnp.int32, (1, 512), 1)
+    key_i, order_i = key.astype(F32), (key * 512 + index).astype(F32)
+    columns = jnp.transpose(pack_rows((key_i, order_i), 128))
+    key_j, order_j = columns[:, 0:1], columns[:, 1:2]
+    one = lax.broadcasted_iota(jnp.int32, (512, 512), 0)
+    two = lax.broadcasted_iota(jnp.int32, (512, 512), 1)
+    same = (one >> 6) == (two >> 6)
+    rank = jnp.sum(jnp.where(same & (order_i < order_j), 1.0, 0.0), axis=1, keepdims=True).astype(jnp.int32)
+    less = jnp.sum(jnp.where(same & (key_i < key_j), 1.0, 0.0), axis=1, keepdims=True).astype(jnp.int32)
+    owner, slot = rank & 3, rank >> 2
+    place = slot - ((less - owner + 3) >> 2)
+    lane = lax.broadcasted_iota(jnp.int32, (512, 128), 1) >> 4
+    pick = jnp.where((owner == role) & (place == lane), 1.0, 0.0).astype(BF16)
+    request = jnp.where((dest & 7) == batch, (dest >> 3) * 16 + row_ref[...] + 1, 0)
     sub = lax.broadcasted_iota(jnp.int32, (8, 512), 0)
-    block = lax.broadcasted_iota(jnp.int32, (512, 256), 0)
-    place = lax.broadcasted_iota(jnp.int32, (512, 256), 1) >> 4
-    pick = jnp.where((((block >> 4) & 3) == role) & ((block & 15) == place), 1.0, 0.0).astype(BF16)
-    dest, row = [
-        dot(jnp.where((lane >> 6) == sub, r[...], 0).astype(F32).astype(BF16), pick, 1, 0).astype(jnp.int32)
-        for r in (dest_ref, row_ref)
-    ]
-    out_ref[...] = jnp.where((dest & 7) == batch, (dest >> 3) * 16 + row, -1)
+    spread = jnp.where((lax.broadcasted_iota(jnp.int32, (8, 512), 1) >> 6) == sub, request, 0)
+    target_ref[...] = dot(spread.astype(F32).astype(BF16), pick, 1, 0).astype(jnp.int32) - 1
+    gap = lax.broadcasted_iota(jnp.int32, (256, 128), 0) - lax.broadcasted_iota(jnp.int32, (256, 128), 1)
+    for d in range(4):
+        before = ((index >> 6) == batch) & (key < lax.rem(zh + d, 4))
+        count = jnp.sum(jnp.where(before, 1.0, 0.0), axis=1, keepdims=True).astype(jnp.int32)
+        window_ref[d] = jnp.where(gap == ((count - role + 3) >> 2) * 16, 1.0, 0.0).astype(BF16)
+    tmp[...] = jnp.broadcast_to((owner * 16 + slot).astype(F32), (512, 128))
+    own = tmp[pl.ds(pl.multiple_of(batch * 64, 64), 64), :].astype(BF16)
+    token = lax.broadcasted_iota(jnp.int32, (1024, 64), 0)
+    repeat = jnp.where((token >> 4) == lax.broadcasted_iota(jnp.int32, (1024, 64), 1), 1.0, 0.0).astype(BF16)
+    to = dot(repeat, own, 1, 0).astype(jnp.int32)[:, 0:1] * 16 + (token[:, 0:1] & 15)
+    turn_ref[...] = jnp.where(lax.broadcasted_iota(jnp.int32, (1024, 1024), 1) == to, 1.0, 0.0).astype(BF16)
 
 
 def resident_kernel(len_ref, q_ref, sc_ref, c_ref, out_ref, buf, sems):
@@ -122,14 +143,15 @@
         out_ref[pl.ds(group * 128, 128), 128:] = jnp.where(lane128 == 0, m, den)
 
 
-def project_kernel(keep_ref, got_ref, *refs):
+def project_kernel(keep_ref, got_ref, turn_ref, *refs):
     p, out_ref = refs[:5], refs[5]
     zl = lax.axis_index("tensor") // 4
-    count = p[0].shape[1] // 4
+    weight = jnp.concatenate([keep_ref[...], got_ref[...]], axis=0)
+    kv = dot(weight, jnp.concatenate([ref[...] for ref in p], axis=0), 1, 0).astype(BF16)
     for r in range(4):
-        rows = jnp.concatenate([ref[:, pl.ds(r * count, count)] for ref in p], axis=0)
-        out_ref[r * 2 + zl] = dot(keep_ref[...], rows, 1, 0).astype(BF16)
-        out_ref[r * 2 + 1 - zl] = dot(got_ref[...], rows, 1, 0).astype(BF16)
+        part = dot(kv, turn_ref[:, r * 256 : r * 256 + 256], 1, 0).astype(BF16)
+        out_ref[r * 2 + zl] = part[:256]
+        out_ref[r * 2 + 1 - zl] = part[256:]
 
 
 def total_of(ref):
@@ -152,13 +174,14 @@
     return (kv / scale).astype(BF16), scale
 
 
-def quantize_kernel(sum_ref, out_ref):
+def quantize_kernel(sum_ref, window_ref, *outs):
     kv = total_of(sum_ref)
     key_codes, key_scale = quantize(kv[:128])
     value_codes, value_scale = quantize(kv[128:])
-    out_ref[pl.ds(0, 128), :] = key_codes
-    out_ref[pl.ds(128, 128), :] = value_codes
-    out_ref[pl.ds(256, 16), :] = pack_rows(three(key_scale) + three(value_scale), 16).astype(BF16)
+    scales = pack_rows(three(key_scale) + three(value_scale), 16).astype(BF16)
+    codes = jnp.concatenate([key_codes, value_codes, scales], axis=0)
+    for d in range(4):
+        outs[d][...] = dot(codes, window_ref[d], 1, 0).astype(BF16)
 
 
 def join_kernel(target_ref, q_ref, *refs):
@@ -166,8 +189,8 @@
     batch = lax.axis_index("batch")
     zh, core = batch // 2, lax.rem(batch, 2)
     q = q_ref[...]
-    request = lax.broadcasted_iota(jnp.int32, (384, 256), 0) >> 3
-    scales, top = [], jnp.full((384, 256), LOW, F32)
+    request = lax.broadcasted_iota(jnp.int32, (384, 128), 0) >> 3
+    scales, top = [], jnp.full((384, 128), LOW, F32)
     for i in range(8):
         origin = lax.rem(zh + 4 - i % 4, 4) * 2 + (core if i < 4 else 1 - core)
         rows = parts[i][pl.ds(256, 16), :].astype(F32)
@@ -178,7 +201,7 @@
         tmp[i] = s
         top = jnp.maximum(top, s)
     top = jnp.max(top, axis=1, keepdims=True)
-    total = jnp.zeros((384, 256), F32)
+    total = jnp.zeros((384, 128), F32)
     acc = jnp.zeros((384, 128), F32)
     for i in range(8):
         e = jnp.exp(tmp[i] - top)
@@ -251,7 +274,10 @@
     )
     got = z_swap(give)
 
-    target = call(target_kernel, shape(8, 256, dtype=jnp.int32), (bdest.T, brow.reshape(1, 512)), [FETCH] * 2)
+    turn, window, target = call(
+        plan_kernel, [shape(1024, 1024), shape(4, 256, 128), shape(8, 128, dtype=jnp.int32)],
+        (bdest.T, brow.reshape(1, 512)), [FETCH] * 2, scratch=[pltpu.VMEM((512, 128), F32)], cost=2,
+    )
     (p1, p2), target = lax.optimization_barrier(((p1, p2), target))
 
     cutoff = p0.shape[0] // 2
@@ -259,16 +285,16 @@
     pieces = (held, p1, p2, p3a, p3b)
 
     count = p0.shape[1] // 4
-    outs = call(project_kernel, shape(8, 256, count), (keep, got, *pieces), [VMEM] * 7)
+    outs = call(project_kernel, shape(8, 256, count), (keep, got, turn, *pieces), [VMEM] * 8, cost=2)
     groups = [[r * 8 + z * 4 + x for r in range(4) for z in range(2)] for x in range(4)]
     sums = lax.all_to_all(outs, ("role", "tensor"), 0, 0, axis_index_groups=groups)
-    codes_out = call(quantize_kernel, shape(272, count), (sums,), [VMEM])
-
-    parts = [codes_out] + [zh_shift(codes_out, d) for d in (1, 2, 3)]
+    cuts = call(quantize_kernel, [shape(272, 128)] * 4, (sums, window), [VMEM] * 2)
+
+    parts = [cuts[0]] + [zh_shift(cuts[d], d) for d in (1, 2, 3)]
     parts = parts + [core_swap(v) for v in parts]
     sums = call(
         join_kernel, shape(144, 384), (target, queries.reshape(384, 128), *parts), [VMEM] * 10,
-        scratch=[pltpu.VMEM((8, 384, 256), F32)], cost=2.5,
+        scratch=[pltpu.VMEM((8, 384, 128), F32)], cost=1.5,
     )
     sums = [sums] + [role_shift(sums, d) for d in (1, 2, 3)]
     res = call(

time: 69.9 us -> 67.3 us (0.963)
  waiting for transfers between devices: 16.3 us -> 11.9 us
  Pallas kernels: 10 us -> 11.7 us
    ppermute x3, waiting for transfers between devices: 6.33 us -> 2.94 us  [zh_shift(): return lax.ppermute(v, 'batch', [(i, (i + 2 * d) % 8) for i in range(8)])]
    pallas_call x7, Pallas kernels: 10 us -> 11.7 us  [call(): pl.pallas_call(kernel, out_shape=outs, in_specs=specs, out_specs=jax.tree...]
    ppermute x4, waiting for transfers between devices: 7.6 us -> 6.37 us  [x_shift(): lax.ppermute(v, 'tensor', [(z * 4 + x, z * 4 + (x + d) % 4) for z in rang...]
  transfers between devices with their start and end apart: 15 -> 15, of which waited for: 11 -> 10; matrix products, arithmetic and copies ran while one was open for 0% -> 0% of each run, Pallas kernels for 7% -> 10%
where the time goes in v4:
time: 67.3 us; the launch traced here: 67 us
  starting transfers between devices  20.9 us (31%)
  blocking collectives  19 us (28%)
  waiting for transfers between devices  11.9 us (18%)
  Pallas kernels  11.7 us (17%)
  local copies, waits for them, and re-layouts  3.46 us (5%)
    all_to_all x1, blocking collectives, body(): lax.all_to_all(outs, ('role', 'tensor'), 0, 0, axis_index_groups=groups)  19 us
    pallas_call x7, Pallas kernels, call(): pl.pallas_call(kernel, out_shape=outs, in_specs=specs, out_specs=jax.tree...  11.7 us
    ppermute x3, starting transfers between devices, zh_shift(): return lax.ppermute(v, 'batch', [(i, (i + 2 * d) % 8) for i in range(8)])  10.5 us
    ppermute x4, waiting for transfers between devices, x_shift(): lax.ppermute(v, 'tensor', [(z * 4 + x, z * 4 + (x + d) % 4) for z in rang...  6.37 us
    ppermute x4, starting transfers between devices, x_shift(): lax.ppermute(v, 'tensor', [(z * 4 + x, z * 4 + (x + d) % 4) for z in rang...  4.4 us
    ppermute x3, starting transfers between devices, role_shift(): return lax.ppermute(v, 'role', [(i, (i + d) % 4) for i in range(4)])  3.65 us
    unnamed x14, local copies, waits for them, and re-layouts  3.43 us
    ppermute x3, waiting for transfers between devices, zh_shift(): return lax.ppermute(v, 'batch', [(i, (i + 2 * d) % 8) for i in range(8)])  2.94 us
  transfers between devices with their start and end apart: 15, of which 10 were waited for; matrix products, arithmetic and copies ran while one was open for 0% of the time, Pallas kernels for 10%

profile of v4, /device:TPU:6, one launch (start us, length us, event | category | flops | bytes accessed | tf_op | source)
XLA Modules:
  0.0 67.0 jit_solution(14482957724887715705)
XLA Ops:
  0.0 2.2 %collective-permute-start = (bf16[160,1024]{1,0:T(8,128)(2,1)}, bf16[160,1024]{1,0:T(8,128)(2,1)S(1)}, u32[]{:S(2)}, u32[]{:S(2)}) collective-permute-start(bf16[160,1024]{1,0:T(8,128)(2,1)} %bitcast.11), channel_id=1, source_target_pairs={{0,1},{1,2},{2,3},{3,0},{4,5},{5,6},{6,7},{7,4},{8,9},{9,10},{10,1... | collective-permute-start | bytes 983048 | tf_op jit(solution)/shard_map/ppermute | solution.py:251
  2.2 1.1 %copy-done = bf16[1280,1,256]{2,0,1:T(8,128)(2,1)S(1)} copy-done((bf16[1280,1,256]{2,0,1:T(8,128)(2,1)S(1)}, bf16[1280,1,256]{2,0,1:T(8,128)(2,1)}, u32[]{:S(2)}) %copy-start) | copy-done | bytes 655384
  3.3 1.0 %copy-done.2 = bf16[1024,160]{0,1:T(8,128)(2,1)S(1)} copy-done((bf16[1024,160]{0,1:T(8,128)(2,1)S(1)}, bf16[1024,160]{0,1:T(8,128)(2,1)}, u32[]{:S(2)}) %copy-start.2) | copy-done | bytes 327704
  4.3 0.2 shard_map.83
  4.5 1.8 %collective-permute-start.2 = (bf16[256,640]{1,0:T(8,128)(2,1)S(1)}, bf16[256,640]{1,0:T(8,128)(2,1)S(1)}, u32[]{:S(2)}, u32[]{:S(2)}) collective-permute-start(bf16[256,640]{1,0:T(8,128)(2,1)S(1)} %get-tuple-element.21), channel_id=1, source_target_pairs={{0,4},{1,5},{2,6},{3,7},{4,0},{5,1},{6,2},{7,3},{8,12},{9,13},{10,... | collective-permute-start | bytes 983048 | tf_op jit(solution)/shard_map/ppermute | solution.py:255
  6.3 0.7 %copy-done.5 = s32[512,1]{0,1:T(1,128)S(1)} copy-done((s32[512,1]{0,1:T(1,128)S(1)}, s32[512,1]{0,1:T(1,128)}, u32[]{:S(2)}) %copy-start.5) | copy-done | bytes 2072
  7.0 0.7 %copy-done.6 = s32[512]{0:T(512)S(1)} copy-done((s32[512]{0:T(512)S(1)}, s32[512]{0:T(512)}, u32[]{:S(2)}) %copy-start.6) | copy-done | bytes 2072
  7.7 1.4 %shard_map.82 = (bf16[1024,1024]{1,0:T(8,128)(2,1)S(1)}, bf16[4,256,128]{2,1,0:T(8,128)(2,1)S(1)}, s32[8,128]{1,0:T(8,128)S(1)}) custom-call(s32[1,512]{1,0:T(1,128)S(1)} %bitcast.15, s32[1,512]{1,0:T(1,128)S(1)} %bitcast.16), custom_call_target="tpu_custom_call" | custom-call | bytes 6000000 | tf_op jit(solution)/shard_map/pallas_call | solution.py:18
  9.2 0.5 collective-permute-done.refs_1_
  9.7 1.3 %collective-permute-done.1.refs_2_ = bf16[160,1024]{1,0:T(8,128)(2,1)S(1)} collective-permute-done((bf16[160,1024]{1,0:T(8,128)(2,1)}, bf16[160,1024]{1,0:T(8,128)(2,1)S(1)}, u32[]{:S(2)}, u32[]{:S(2)}) %collective-permute-start.1) | collective-permute-done | bytes 327712 | tf_op jit(solution)/shard_map/ppermute | solution.py:251
  11.0 0.5 collective-permute-start.3
  11.5 1.7 %collective-permute-start.4 = (bf16[80,1024]{1,0:T(8,128)(2,1)S(1)}, bf16[80,1024]{1,0:T(8,128)(2,1)S(1)}, u32[]{:S(2)}, u32[]{:S(2)}) collective-permute-start(bf16[80,1024]{1,0:T(8,128)(2,1)S(1)} %slice.7), channel_id=1, source_target_pairs={{0,3},{1,0},{2,1},{3,2},{4,7},{5,4},{6,5},{7,6},{8,11},{9,8},{10,9... | collective-permute-start | bytes 491528 | tf_op jit(solution)/shard_map/ppermute | solution.py:251
  13.2 0.3 collective-permute-done.2.got_ref
  13.5 2.9 %collective-permute-done.3.refs_3_ = bf16[80,1024]{1,0:T(8,128)(2,1)S(1)} collective-permute-done((bf16[80,1024]{1,0:T(8,128)(2,1)S(1)}, bf16[80,1024]{1,0:T(8,128)(2,1)S(1)}, u32[]{:S(2)}, u32[]{:S(2)}) %collective-permute-start.3) | collective-permute-done | bytes 163872 | tf_op jit(solution)/shard_map/ppermute | solution.py:251
  16.4 1.7 %collective-permute-done.4.refs_4_ = bf16[80,1024]{1,0:T(8,128)(2,1)S(1)} collective-permute-done((bf16[80,1024]{1,0:T(8,128)(2,1)S(1)}, bf16[80,1024]{1,0:T(8,128)(2,1)S(1)}, u32[]{:S(2)}, u32[]{:S(2)}) %collective-permute-start.4) | collective-permute-done | bytes 163872 | tf_op jit(solution)/shard_map/ppermute | solution.py:251
  18.1 2.1 %shard_map.84 = bf16[8,256,256]{2,1,0:T(8,128)(2,1)S(1)} custom-call(bf16[256,640]{1,0:T(8,128)(2,1)S(1)} %get-tuple-element.20.keep_ref, bf16[256,640]{1,0:T(8,128)(2,1)S(1)} %collective-permute-done.2.got_ref, bf16[1024,1024]{1,0:T(8,128)(2,1)S(1)} %get-tuple-element.22.turn_ref, bf16[160,1024]{1,0:T(8,128)(2,1)S(1)} %get-tuple-element.23.refs_0_, ...), custom_call_target="tpu_custom_call" | custom-call | bytes 6000000 | tf_op jit(solution)/shard_map/pallas_call | solution.py:18
  20.2 19.0 %all_to_all.5.sum_ref = bf16[8,256,256]{2,1,0:T(8,128)(2,1)S(1)} all-to-all(bf16[8,256,256]{2,1,0:T(8,128)(2,1)S(1)} %shard_map.84), channel_id=1, replica_groups={{0,4,64,68,128,132,192,196},{1,5,65,69,129,133,193,197},{2,6,66,70,130,..., dimensions={0} | all-to-all | bytes 2097152 | tf_op jit(solution)/shard_map/all_to_all | solution.py:290
  39.2 0.7 %shard_map.85 = (bf16[272,128]{1,0:T(8,128)(2,1)S(1)}, bf16[272,128]{1,0:T(8,128)(2,1)S(1)}, bf16[272,128]{1,0:T(8,128)(2,1)S(1)}, bf16[272,128]{1,0:T(8,128)(2,1)S(1)}) custom-call(bf16[8,256,256]{2,1,0:T(8,128)(2,1)S(1)} %all_to_all.5.sum_ref, bf16[4,256,128]{2,1,0:T(8,128)(2,1)S(1)} %get-tuple-element.26.window_ref), custom_call_target="tpu_custom_call" | custom-call | bytes 3000000 | tf_op jit(solution)/shard_map/pallas_call | solution.py:18
  39.9 3.4 %collective-permute-start.5 = (bf16[272,128]{1,0:T(8,128)(2,1)S(1)}, bf16[272,128]{1,0:T(8,128)(2,1)S(1)}, u32[]{:S(2)}, u32[]{:S(2)}) collective-permute-start(bf16[272,128]{1,0:T(8,128)(2,1)S(1)} %get-tuple-element.28), channel_id=1, source_target_pairs={{0,16},{8,24},{16,32},{24,40},{32,48},{40,56},{48,0},{56,8},{1,17}... | collective-permute-start | bytes 208904 | tf_op jit(solution)/shard_map/ppermute | solution.py:259
  43.3 4.5 %collective-permute-start.6 = (bf16[272,128]{1,0:T(8,128)(2,1)S(1)}, bf16[272,128]{1,0:T(8,128)(2,1)S(1)}, u32[]{:S(2)}, u32[]{:S(2)}) collective-permute-start(bf16[272,128]{1,0:T(8,128)(2,1)S(1)} %get-tuple-element.29), channel_id=1, source_target_pairs={{0,32},{8,40},{16,48},{24,56},{32,0},{40,8},{48,16},{56,24},{1,33}... | collective-permute-start | bytes 208904 | tf_op jit(solution)/shard_map/ppermute | solution.py:259
  47.8 2.7 %collective-permute-start.7 = (bf16[272,128]{1,0:T(8,128)(2,1)S(1)}, bf16[272,128]{1,0:T(8,128)(2,1)S(1)}, u32[]{:S(2)}, u32[]{:S(2)}) collective-permute-start(bf16[272,128]{1,0:T(8,128)(2,1)S(1)} %get-tuple-element.30), channel_id=1, source_target_pairs={{0,48},{8,56},{16,0},{24,8},{32,16},{40,24},{48,32},{56,40},{1,49}... | collective-permute-start | bytes 208904 | tf_op jit(solution)/shard_map/ppermute | solution.py:259
  50.4 0.5 collective-permute-start.9
  50.9 1.3 %collective-permute-done.6.refs_2_ = bf16[272,128]{1,0:T(8,128)(2,1)S(1)} collective-permute-done((bf16[272,128]{1,0:T(8,128)(2,1)S(1)}, bf16[272,128]{1,0:T(8,128)(2,1)S(1)}, u32[]{:S(2)}, u32[]{:S(2)}) %collective-permute-start.6) | collective-permute-done | bytes 69664 | tf_op jit(solution)/shard_map/ppermute | solution.py:259
  52.3 1.6 %collective-permute-done.7.refs_3_ = bf16[272,128]{1,0:T(8,128)(2,1)S(1)} collective-permute-done((bf16[272,128]{1,0:T(8,128)(2,1)S(1)}, bf16[272,128]{1,0:T(8,128)(2,1)S(1)}, u32[]{:S(2)}, u32[]{:S(2)}) %collective-permute-start.7) | collective-permute-done | bytes 69664 | tf_op jit(solution)/shard_map/ppermute | solution.py:259
  53.9 1.2 %collective-permute-done.11.refs_7_ = bf16[272,128]{1,0:T(8,128)(2,1)S(1)} collective-permute-done((bf16[272,128]{1,0:T(8,128)(2,1)S(1)}, bf16[272,128]{1,0:T(8,128)(2,1)S(1)}, u32[]{:S(2)}, u32[]{:S(2)}) %collective-permute-start.11) | collective-permute-done | bytes 69664 | tf_op jit(solution)/shard_map/ppermute | solution.py:263
  55.1 1.3 %shard_map.86.u0 = bf16[144,384]{1,0:T(8,128)(2,1)S(1)} custom-call(s32[8,128]{1,0:T(8,128)S(1)} %get-tuple-element.19.target_ref, bf16[384,128]{1,0:T(8,128)(2,1)S(1)} %bitcast.10, bf16[272,128]{1,0:T(8,128)(2,1)S(1)} %get-tuple-element.27.refs_0_, bf16[272,128]{1,0:T(8,128)(2,1)S(1)} %collective-permute-done.5.refs_1_, ...), custom_call_target="tpu_custom_call" | custom-call | bytes 4500000 | tf_op jit(solution)/shard_map/pallas_call | solution.py:18
  56.5 1.7 %collective-permute-start.13 = (bf16[144,384]{1,0:T(8,128)(2,1)S(1)}, bf16[144,384]{1,0:T(8,128)(2,1)S(1)}, u32[]{:S(2)}, u32[]{:S(2)}) collective-permute-start(bf16[144,384]{1,0:T(8,128)(2,1)S(1)} %shard_map.86.u0), channel_id=1, source_target_pairs={{0,128},{64,192},{128,0},{192,64},{1,129},{65,193},{129,1},{193,65... | collective-permute-start | bytes 331784 | tf_op jit(solution)/shard_map/ppermute | solution.py:247
  58.3 1.8 %collective-permute-start.14 = (bf16[144,384]{1,0:T(8,128)(2,1)S(1)}, bf16[144,384]{1,0:T(8,128)(2,1)S(1)}, u32[]{:S(2)}, u32[]{:S(2)}) collective-permute-start(bf16[144,384]{1,0:T(8,128)(2,1)S(1)} %shard_map.86.u0), channel_id=1, source_target_pairs={{0,192},{64,0},{128,64},{192,128},{1,193},{65,1},{129,65},{193,129... | collective-permute-start | bytes 331784 | tf_op jit(solution)/shard_map/ppermute | solution.py:247
  60.1 4.7 %shard_map.87.r = f32[384,256]{1,0:T(8,128)S(1)} custom-call(s32[3,16]{1,0:T(4,128)S(1)} %copy-done.4, bf16[3,16,8,128]{3,2,1,0:T(8,128)(2,1)S(1)} %copy-done.1, f32[48,2,16]{2,1,0:T(2,128)S(1)} %bitcast.14, bf16[3,16,1,256,256]{4,3,2,1,0:T(8,128)(2,1)} %c_ref.1), custom_call_target="tpu_custom_call" | custom-call | bytes 15000000 | tf_op jit(solution)/shard_map/pallas_call | solution.py:18
  64.9 0.4 collective-permute-done.12.u1
  65.2 0.6 collective-permute-done.14.u3
  65.9 1.2 %shard_map.88 = bf16[48,1024]{1,0:T(8,128)(2,1)} custom-call(bf16[144,384]{1,0:T(8,128)(2,1)S(1)} %shard_map.86.u0, bf16[144,384]{1,0:T(8,128)(2,1)S(1)} %collective-permute-done.12.u1, bf16[144,384]{1,0:T(8,128)(2,1)S(1)} %collective-permute-done.13.u2, bf16[144,384]{1,0:T(8,128)(2,1)S(1)} %collective-permute-done.14.u3, f32[384,256]{1,0:T(8,128)S(1)} %shard_map.87.r), custom_call_target="tpu_custom_call" | custom-call | bytes 3000000 | tf_op jit(solution)/shard_map/pallas_call | solution.py:18
  (22 shorter events, 0.1 us)
Async XLA Ops:
  0.0 60.1 %copy-start.4 = (s32[3,16]{1,0:T(4,128)S(1)}, s32[3,16]{1,0:T(4,128)}, u32[]{:S(2)}) copy-start(s32[3,16]{1,0:T(4,128)} %len_ref.1) | copy-start | bytes 580
  0.0 9.7 %collective-permute-start = (bf16[160,1024]{1,0:T(8,128)(2,1)}, bf16[160,1024]{1,0:T(8,128)(2,1)S(1)}, u32[]{:S(2)}, u32[]{:S(2)}) collective-permute-start(bf16[160,1024]{1,0:T(8,128)(2,1)} %bitcast.11), channel_id=1, source_target_pairs={{0,1},{1,2},{2,3},{3,0},{4,5},{5,6},{6,7},{7,4},{8,9},{9,10},{10,1... | collective-permute-start | bytes 983048 | tf_op jit(solution)/shard_map/ppermute | solution.py:251
  2.2 8.7 %collective-permute-start.1 = (bf16[160,1024]{1,0:T(8,128)(2,1)}, bf16[160,1024]{1,0:T(8,128)(2,1)S(1)}, u32[]{:S(2)}, u32[]{:S(2)}) collective-permute-start(bf16[160,1024]{1,0:T(8,128)(2,1)} %bitcast.12), channel_id=1, source_target_pairs={{0,3},{1,0},{2,1},{3,2},{4,7},{5,4},{6,5},{7,6},{8,11},{9,8},{10,9... | collective-permute-start | bytes 983048 | tf_op jit(solution)/shard_map/ppermute | solution.py:251
  2.2 1.1 %copy-start = (bf16[1280,1,256]{2,0,1:T(8,128)(2,1)S(1)}, bf16[1280,1,256]{2,0,1:T(8,128)(2,1)}, u32[]{:S(2)}) copy-start(bf16[1280,1,256]{2,0,1:T(8,128)(2,1)} %param.9) | copy-start | bytes 1966084
  3.3 1.0 %copy-start.2 = (bf16[1024,160]{0,1:T(8,128)(2,1)S(1)}, bf16[1024,160]{0,1:T(8,128)(2,1)}, u32[]{:S(2)}) copy-start(bf16[1024,160]{0,1:T(8,128)(2,1)} %param.8) | copy-start | bytes 983044
  4.3 50.9 %copy-start.1 = (bf16[3,16,8,128]{3,2,1,0:T(8,128)(2,1)S(1)}, bf16[3,16,8,128]{3,2,1,0:T(8,128)(2,1)}, u32[]{:S(2)}) copy-start(bf16[3,16,8,128]{3,2,1,0:T(8,128)(2,1)} %q_ref.1) | copy-start | bytes 294916
  4.3 55.8 %copy-start.3 = (f32[3,16,1,16,2]{3,4,2,1,0:T(2,128)S(1)}, f32[3,16,1,16,2]{3,4,2,1,0:T(2,128)}, u32[]{:S(2)}) copy-start(f32[3,16,1,16,2]{3,4,2,1,0:T(2,128)} %param.12) | copy-start | bytes 18436
  4.5 9.0 %collective-permute-start.2 = (bf16[256,640]{1,0:T(8,128)(2,1)S(1)}, bf16[256,640]{1,0:T(8,128)(2,1)S(1)}, u32[]{:S(2)}, u32[]{:S(2)}) collective-permute-start(bf16[256,640]{1,0:T(8,128)(2,1)S(1)} %get-tuple-element.21), channel_id=1, source_target_pairs={{0,4},{1,5},{2,6},{3,7},{4,0},{5,1},{6,2},{7,3},{8,12},{9,13},{10,... | collective-permute-start | bytes 983048 | tf_op jit(solution)/shard_map/ppermute | solution.py:255
  6.3 0.7 %copy-start.5 = (s32[512,1]{0,1:T(1,128)S(1)}, s32[512,1]{0,1:T(1,128)}, u32[]{:S(2)}) copy-start(s32[512,1]{0,1:T(1,128)} %param.14) | copy-start | bytes 6148
  7.0 0.7 %copy-start.6 = (s32[512]{0:T(512)S(1)}, s32[512]{0:T(512)}, u32[]{:S(2)}) copy-start(s32[512]{0:T(512)} %param.15) | copy-start | bytes 6148
  11.0 5.4 %collective-permute-start.3 = (bf16[80,1024]{1,0:T(8,128)(2,1)S(1)}, bf16[80,1024]{1,0:T(8,128)(2,1)S(1)}, u32[]{:S(2)}, u32[]{:S(2)}) collective-permute-start(bf16[80,1024]{1,0:T(8,128)(2,1)S(1)} %slice.6), channel_id=1, source_target_pairs={{0,1},{1,2},{2,3},{3,0},{4,5},{5,6},{6,7},{7,4},{8,9},{9,10},{10,1... | collective-permute-start | bytes 491528 | tf_op jit(solution)/shard_map/ppermute | solution.py:251
  11.5 6.6 %collective-permute-start.4 = (bf16[80,1024]{1,0:T(8,128)(2,1)S(1)}, bf16[80,1024]{1,0:T(8,128)(2,1)S(1)}, u32[]{:S(2)}, u32[]{:S(2)}) collective-permute-start(bf16[80,1024]{1,0:T(8,128)(2,1)S(1)} %slice.7), channel_id=1, source_target_pairs={{0,3},{1,0},{2,1},{3,2},{4,7},{5,4},{6,5},{7,6},{8,11},{9,8},{10,9... | collective-permute-start | bytes 491528 | tf_op jit(solution)/shard_map/ppermute | solution.py:251
  39.9 10.5 %collective-permute-start.5 = (bf16[272,128]{1,0:T(8,128)(2,1)S(1)}, bf16[272,128]{1,0:T(8,128)(2,1)S(1)}, u32[]{:S(2)}, u32[]{:S(2)}) collective-permute-start(bf16[272,128]{1,0:T(8,128)(2,1)S(1)} %get-tuple-element.28), channel_id=1, source_target_pairs={{0,16},{8,24},{16,32},{24,40},{32,48},{40,56},{48,0},{56,8},{1,17}... | collective-permute-start | bytes 208904 | tf_op jit(solution)/shard_map/ppermute | solution.py:259
  43.3 9.0 %collective-permute-start.6 = (bf16[272,128]{1,0:T(8,128)(2,1)S(1)}, bf16[272,128]{1,0:T(8,128)(2,1)S(1)}, u32[]{:S(2)}, u32[]{:S(2)}) collective-permute-start(bf16[272,128]{1,0:T(8,128)(2,1)S(1)} %get-tuple-element.29), channel_id=1, source_target_pairs={{0,32},{8,40},{16,48},{24,56},{32,0},{40,8},{48,16},{56,24},{1,33}... | collective-permute-start | bytes 208904 | tf_op jit(solution)/shard_map/ppermute | solution.py:259
  47.8 6.1 %collective-permute-start.7 = (bf16[272,128]{1,0:T(8,128)(2,1)S(1)}, bf16[272,128]{1,0:T(8,128)(2,1)S(1)}, u32[]{:S(2)}, u32[]{:S(2)}) collective-permute-start(bf16[272,128]{1,0:T(8,128)(2,1)S(1)} %get-tuple-element.30), channel_id=1, source_target_pairs={{0,48},{8,56},{16,0},{24,8},{32,16},{40,24},{48,32},{56,40},{1,49}... | collective-permute-start | bytes 208904 | tf_op jit(solution)/shard_map/ppermute | solution.py:259
  50.4 3.5 %collective-permute-start.8 = (bf16[272,128]{1,0:T(8,128)(2,1)S(1)}, bf16[272,128]{1,0:T(8,128)(2,1)S(1)}, u32[]{:S(2)}, u32[]{:S(2)}) collective-permute-start(bf16[272,128]{1,0:T(8,128)(2,1)S(1)} %get-tuple-element.27.refs_0_), channel_id=1, source_target_pairs={{0,8},{8,0},{16,24},{24,16},{32,40},{40,32},{48,56},{56,48},{1,9},... | collective-permute-start | bytes 208904 | tf_op jit(solution)/shard_map/ppermute | solution.py:263
  50.4 3.5 %collective-permute-start.9 = (bf16[272,128]{1,0:T(8,128)(2,1)S(1)}, bf16[272,128]{1,0:T(8,128)(2,1)S(1)}, u32[]{:S(2)}, u32[]{:S(2)}) collective-permute-start(bf16[272,128]{1,0:T(8,128)(2,1)S(1)} %collective-permute-done.5.refs_1_), channel_id=1, source_target_pairs={{0,8},{8,0},{16,24},{24,16},{32,40},{40,32},{48,56},{56,48},{1,9},... | collective-permute-start | bytes 208904 | tf_op jit(solution)/shard_map/ppermute | solution.py:263
  52.3 1.6 %collective-permute-start.10 = (bf16[272,128]{1,0:T(8,128)(2,1)S(1)}, bf16[272,128]{1,0:T(8,128)(2,1)S(1)}, u32[]{:S(2)}, u32[]{:S(2)}) collective-permute-start(bf16[272,128]{1,0:T(8,128)(2,1)S(1)} %collective-permute-done.6.refs_2_), channel_id=1, source_target_pairs={{0,8},{8,0},{16,24},{24,16},{32,40},{40,32},{48,56},{56,48},{1,9},... | collective-permute-start | bytes 208904 | tf_op jit(solution)/shard_map/ppermute | solution.py:263
  53.9 1.3 %collective-permute-start.11 = (bf16[272,128]{1,0:T(8,128)(2,1)S(1)}, bf16[272,128]{1,0:T(8,128)(2,1)S(1)}, u32[]{:S(2)}, u32[]{:S(2)}) collective-permute-start(bf16[272,128]{1,0:T(8,128)(2,1)S(1)} %collective-permute-done.7.refs_3_), channel_id=1, source_target_pairs={{0,8},{8,0},{16,24},{24,16},{32,40},{40,32},{48,56},{56,48},{1,9},... | collective-permute-start | bytes 208904 | tf_op jit(solution)/shard_map/ppermute | solution.py:263
  56.5 8.8 %collective-permute-start.12 = (bf16[144,384]{1,0:T(8,128)(2,1)S(1)}, bf16[144,384]{1,0:T(8,128)(2,1)S(1)}, u32[]{:S(2)}, u32[]{:S(2)}) collective-permute-start(bf16[144,384]{1,0:T(8,128)(2,1)S(1)} %shard_map.86.u0), channel_id=1, source_target_pairs={{0,64},{64,128},{128,192},{192,0},{1,65},{65,129},{129,193},{193,1... | collective-permute-start | bytes 331784 | tf_op jit(solution)/shard_map/ppermute | solution.py:247
  56.5 8.7 %collective-permute-start.13 = (bf16[144,384]{1,0:T(8,128)(2,1)S(1)}, bf16[144,384]{1,0:T(8,128)(2,1)S(1)}, u32[]{:S(2)}, u32[]{:S(2)}) collective-permute-start(bf16[144,384]{1,0:T(8,128)(2,1)S(1)} %shard_map.86.u0), channel_id=1, source_target_pairs={{0,128},{64,192},{128,0},{192,64},{1,129},{65,193},{129,1},{193,65... | collective-permute-start | bytes 331784 | tf_op jit(solution)/shard_map/ppermute | solution.py:247
  58.3 7.6 %collective-permute-start.14 = (bf16[144,384]{1,0:T(8,128)(2,1)S(1)}, bf16[144,384]{1,0:T(8,128)(2,1)S(1)}, u32[]{:S(2)}, u32[]{:S(2)}) collective-permute-start(bf16[144,384]{1,0:T(8,128)(2,1)S(1)} %shard_map.86.u0), channel_id=1, source_target_pairs={{0,192},{64,0},{128,64},{192,128},{1,193},{65,1},{129,65},{193,129... | collective-permute-start | bytes 331784 | tf_op jit(solution)/shard_map/ppermute | solution.py:247

commit v5 on v4

--- a/solution.py
+++ b/solution.py
@@ -143,15 +143,22 @@
         out_ref[pl.ds(group * 128, 128), 128:] = jnp.where(lane128 == 0, m, den)
 
 
-def project_kernel(keep_ref, got_ref, turn_ref, *refs):
-    p, out_ref = refs[:5], refs[5]
+def deal_kernel(turn_ref, p0, p1, p2, out_ref):
+    rows = jnp.concatenate([p0[...], p1[...], p2[...]], axis=0)
+    for r in range(4):
+        out_ref[:, r * 256 : r * 256 + 256] = dot(rows, turn_ref[:, r * 256 : r * 256 + 256], 1, 0).astype(BF16)
+
+
+def project_kernel(keep_ref, got_ref, turn_ref, early_ref, p3a, p3b, out_ref):
     zl = lax.axis_index("tensor") // 4
     weight = jnp.concatenate([keep_ref[...], got_ref[...]], axis=0)
-    kv = dot(weight, jnp.concatenate([ref[...] for ref in p], axis=0), 1, 0).astype(BF16)
+    last = jnp.concatenate([p3a[...], p3b[...]], axis=0)
     for r in range(4):
-        part = dot(kv, turn_ref[:, r * 256 : r * 256 + 256], 1, 0).astype(BF16)
-        out_ref[r * 2 + zl] = part[:256]
-        out_ref[r * 2 + 1 - zl] = part[256:]
+        part = dot(last, turn_ref[:, r * 256 : r * 256 + 256], 1, 0).astype(BF16)
+        rows = jnp.concatenate([early_ref[:, r * 256 : r * 256 + 256], part], axis=0)
+        kv = dot(weight, rows, 1, 0).astype(BF16)
+        out_ref[r * 2 + zl] = kv[:256]
+        out_ref[r * 2 + 1 - zl] = kv[256:]
 
 
 def total_of(ref):
@@ -282,10 +289,10 @@
 
     cutoff = p0.shape[0] // 2
     p3a, p3b = x_shift(p1[:cutoff], 1), x_shift(p2[cutoff:], -1)
-    pieces = (held, p1, p2, p3a, p3b)
 
     count = p0.shape[1] // 4
-    outs = call(project_kernel, shape(8, 256, count), (keep, got, turn, *pieces), [VMEM] * 8, cost=2)
+    early = call(deal_kernel, shape(3 * p0.shape[0], p0.shape[1]), (turn, held, p1, p2), [VMEM] * 4, cost=1.5)
+    outs = call(project_kernel, shape(8, 256, count), (keep, got, turn, early, p3a, p3b), [VMEM] * 6)
     groups = [[r * 8 + z * 4 + x for r in range(4) for z in range(2)] for x in range(4)]
     sums = lax.all_to_all(outs, ("role", "tensor"), 0, 0, axis_index_groups=groups)
     cuts = call(quantize_kernel, [shape(272, 128)] * 4, (sums, window), [VMEM] * 2)

time: 67.3 us -> 66.6 us (0.990)
  waiting for transfers between devices: 11.9 us -> 10.7 us
    ppermute x4, waiting for transfers between devices: 6.37 us -> 5.5 us  [x_shift(): lax.ppermute(v, 'tensor', [(z * 4 + x, z * 4 + (x + d) % 4) for z in rang...]
    pallas_call x7 -> x8, Pallas kernels: 11.7 us -> 12.2 us  [call(): pl.pallas_call(kernel, out_shape=outs, in_specs=specs, out_specs=jax.tree...]
  transfers between devices with their start and end apart: 15 -> 15, of which waited for: 10 -> 9; matrix products, arithmetic and copies ran while one was open for 0% -> 0% of each run, Pallas kernels for 10% -> 11%
where the time goes in v5:
time: 66.6 us; the launch traced here: 66.4 us
  starting transfers between devices  20.9 us (31%)
  blocking collectives  19 us (29%)
  Pallas kernels  12.2 us (18%)
  waiting for transfers between devices  10.7 us (16%)
  local copies, waits for them, and re-layouts  3.46 us (5%)
    all_to_all x1, blocking collectives, body(): lax.all_to_all(outs, ('role', 'tensor'), 0, 0, axis_index_groups=groups)  19 us
    pallas_call x8, Pallas kernels, call(): pl.pallas_call(kernel, out_shape=outs, in_specs=specs, out_specs=jax.tree...  12.2 us
    ppermute x3, starting transfers between devices, zh_shift(): return lax.ppermute(v, 'batch', [(i, (i + 2 * d) % 8) for i in range(8)])  10.5 us
    ppermute x4, waiting for transfers between devices, x_shift(): lax.ppermute(v, 'tensor', [(z * 4 + x, z * 4 + (x + d) % 4) for z in rang...  5.5 us
    ppermute x4, starting transfers between devices, x_shift(): lax.ppermute(v, 'tensor', [(z * 4 + x, z * 4 + (x + d) % 4) for z in rang...  4.4 us
    ppermute x3, starting transfers between devices, role_shift(): return lax.ppermute(v, 'role', [(i, (i + d) % 4) for i in range(4)])  3.65 us
    unnamed x14, local copies, waits for them, and re-layouts  3.43 us
    ppermute x3, waiting for transfers between devices, zh_shift(): return lax.ppermute(v, 'batch', [(i, (i + 2 * d) % 8) for i in range(8)])  2.93 us
  transfers between devices with their start and end apart: 15, of which 9 were waited for; matrix products, arithmetic and copies ran while one was open for 0% of the time, Pallas kernels for 11%

profile of v5, /device:TPU:6, one launch (start us, length us, event | category | flops | bytes accessed | tf_op | source)
XLA Modules:
  0.0 66.4 jit_solution(3968806543890198986)
XLA Ops:
  0.0 2.2 %collective-permute-start = (bf16[160,1024]{1,0:T(8,128)(2,1)}, bf16[160,1024]{1,0:T(8,128)(2,1)S(1)}, u32[]{:S(2)}, u32[]{:S(2)}) collective-permute-start(bf16[160,1024]{1,0:T(8,128)(2,1)} %bitcast.11), channel_id=1, source_target_pairs={{0,1},{1,2},{2,3},{3,0},{4,5},{5,6},{6,7},{7,4},{8,9},{9,10},{10,1... | collective-permute-start | bytes 983048 | tf_op jit(solution)/shard_map/ppermute | solution.py:258
  2.2 1.1 %copy-done = bf16[1280,1,256]{2,0,1:T(8,128)(2,1)S(1)} copy-done((bf16[1280,1,256]{2,0,1:T(8,128)(2,1)S(1)}, bf16[1280,1,256]{2,0,1:T(8,128)(2,1)}, u32[]{:S(2)}) %copy-start) | copy-done | bytes 655384
  3.3 1.0 %copy-done.2 = bf16[1024,160]{0,1:T(8,128)(2,1)S(1)} copy-done((bf16[1024,160]{0,1:T(8,128)(2,1)S(1)}, bf16[1024,160]{0,1:T(8,128)(2,1)}, u32[]{:S(2)}) %copy-start.2) | copy-done | bytes 327704
  4.3 0.2 shard_map.83
  4.5 1.8 %collective-permute-start.2 = (bf16[256,640]{1,0:T(8,128)(2,1)S(1)}, bf16[256,640]{1,0:T(8,128)(2,1)S(1)}, u32[]{:S(2)}, u32[]{:S(2)}) collective-permute-start(bf16[256,640]{1,0:T(8,128)(2,1)S(1)} %get-tuple-element.21), channel_id=1, source_target_pairs={{0,4},{1,5},{2,6},{3,7},{4,0},{5,1},{6,2},{7,3},{8,12},{9,13},{10,... | collective-permute-start | bytes 983048 | tf_op jit(solution)/shard_map/ppermute | solution.py:262
  6.3 0.7 %copy-done.5 = s32[512,1]{0,1:T(1,128)S(1)} copy-done((s32[512,1]{0,1:T(1,128)S(1)}, s32[512,1]{0,1:T(1,128)}, u32[]{:S(2)}) %copy-start.5) | copy-done | bytes 2072
  7.0 0.7 %copy-done.6 = s32[512]{0:T(512)S(1)} copy-done((s32[512]{0:T(512)S(1)}, s32[512]{0:T(512)}, u32[]{:S(2)}) %copy-start.6) | copy-done | bytes 2072
  7.7 1.4 %shard_map.82 = (bf16[1024,1024]{1,0:T(8,128)(2,1)S(1)}, bf16[4,256,128]{2,1,0:T(8,128)(2,1)S(1)}, s32[8,128]{1,0:T(8,128)S(1)}) custom-call(s32[1,512]{1,0:T(1,128)S(1)} %bitcast.15, s32[1,512]{1,0:T(1,128)S(1)} %bitcast.16), custom_call_target="tpu_custom_call" | custom-call | bytes 6000000 | tf_op jit(solution)/shard_map/pallas_call | solution.py:18
  9.1 0.5 collective-permute-done.p1
  9.7 1.2 %collective-permute-done.1.p2 = bf16[160,1024]{1,0:T(8,128)(2,1)S(1)} collective-permute-done((bf16[160,1024]{1,0:T(8,128)(2,1)}, bf16[160,1024]{1,0:T(8,128)(2,1)S(1)}, u32[]{:S(2)}, u32[]{:S(2)}) %collective-permute-start.1) | collective-permute-done | bytes 327712 | tf_op jit(solution)/shard_map/ppermute | solution.py:258
  10.9 0.6 collective-permute-start.3
  11.5 1.6 %collective-permute-start.4 = (bf16[80,1024]{1,0:T(8,128)(2,1)S(1)}, bf16[80,1024]{1,0:T(8,128)(2,1)S(1)}, u32[]{:S(2)}, u32[]{:S(2)}) collective-permute-start(bf16[80,1024]{1,0:T(8,128)(2,1)S(1)} %slice.7), channel_id=1, source_target_pairs={{0,3},{1,0},{2,1},{3,2},{4,7},{5,4},{6,5},{7,6},{8,11},{9,8},{10,9... | collective-permute-start | bytes 491528 | tf_op jit(solution)/shard_map/ppermute | solution.py:258
  13.1 1.2 %shard_map.84.early_ref = bf16[480,1024]{1,0:T(8,128)(2,1)S(1)} custom-call(bf16[1024,1024]{1,0:T(8,128)(2,1)S(1)} %get-tuple-element.22.turn_ref, bf16[160,1024]{1,0:T(8,128)(2,1)S(1)} %get-tuple-element.23.p0, bf16[160,1024]{1,0:T(8,128)(2,1)S(1)} %collective-permute-done.p1, bf16[160,1024]{1,0:T(8,128)(2,1)S(1)} %collective-permute-done.1.p2), custom_call_target="tpu_custom_call" | custom-call | bytes 4500000 | tf_op jit(solution)/shard_map/pallas_call | solution.py:18
  14.3 2.0 %collective-permute-done.3.p3a = bf16[80,1024]{1,0:T(8,128)(2,1)S(1)} collective-permute-done((bf16[80,1024]{1,0:T(8,128)(2,1)S(1)}, bf16[80,1024]{1,0:T(8,128)(2,1)S(1)}, u32[]{:S(2)}, u32[]{:S(2)}) %collective-permute-start.3) | collective-permute-done | bytes 163872 | tf_op jit(solution)/shard_map/ppermute | solution.py:258
  16.3 1.8 %collective-permute-done.4.p3b = bf16[80,1024]{1,0:T(8,128)(2,1)S(1)} collective-permute-done((bf16[80,1024]{1,0:T(8,128)(2,1)S(1)}, bf16[80,1024]{1,0:T(8,128)(2,1)S(1)}, u32[]{:S(2)}, u32[]{:S(2)}) %collective-permute-start.4) | collective-permute-done | bytes 163872 | tf_op jit(solution)/shard_map/ppermute | solution.py:258
  18.1 1.5 %shard_map.85 = bf16[8,256,256]{2,1,0:T(8,128)(2,1)S(1)} custom-call(bf16[256,640]{1,0:T(8,128)(2,1)S(1)} %get-tuple-element.20.keep_ref, bf16[256,640]{1,0:T(8,128)(2,1)S(1)} %collective-permute-done.2.got_ref, bf16[1024,1024]{1,0:T(8,128)(2,1)S(1)} %get-tuple-element.22.turn_ref, bf16[480,1024]{1,0:T(8,128)(2,1)S(1)} %shard_map.84.early_ref, ...), custom_call_target="tpu_custom_call" | custom-call | bytes 3000000 | tf_op jit(solution)/shard_map/pallas_call | solution.py:18
  19.5 19.0 %all_to_all.5.sum_ref = bf16[8,256,256]{2,1,0:T(8,128)(2,1)S(1)} all-to-all(bf16[8,256,256]{2,1,0:T(8,128)(2,1)S(1)} %shard_map.85), channel_id=1, replica_groups={{0,4,64,68,128,132,192,196},{1,5,65,69,129,133,193,197},{2,6,66,70,130,..., dimensions={0} | all-to-all | bytes 2097152 | tf_op jit(solution)/shard_map/all_to_all | solution.py:297
  38.6 0.7 %shard_map.86 = (bf16[272,128]{1,0:T(8,128)(2,1)S(1)}, bf16[272,128]{1,0:T(8,128)(2,1)S(1)}, bf16[272,128]{1,0:T(8,128)(2,1)S(1)}, bf16[272,128]{1,0:T(8,128)(2,1)S(1)}) custom-call(bf16[8,256,256]{2,1,0:T(8,128)(2,1)S(1)} %all_to_all.5.sum_ref, bf16[4,256,128]{2,1,0:T(8,128)(2,1)S(1)} %get-tuple-element.26.window_ref), custom_call_target="tpu_custom_call" | custom-call | bytes 3000000 | tf_op jit(solution)/shard_map/pallas_call | solution.py:18
  39.3 3.3 %collective-permute-start.5 = (bf16[272,128]{1,0:T(8,128)(2,1)S(1)}, bf16[272,128]{1,0:T(8,128)(2,1)S(1)}, u32[]{:S(2)}, u32[]{:S(2)}) collective-permute-start(bf16[272,128]{1,0:T(8,128)(2,1)S(1)} %get-tuple-element.28), channel_id=1, source_target_pairs={{0,16},{8,24},{16,32},{24,40},{32,48},{40,56},{48,0},{56,8},{1,17}... | collective-permute-start | bytes 208904 | tf_op jit(solution)/shard_map/ppermute | solution.py:266
  42.6 4.5 %collective-permute-start.6 = (bf16[272,128]{1,0:T(8,128)(2,1)S(1)}, bf16[272,128]{1,0:T(8,128)(2,1)S(1)}, u32[]{:S(2)}, u32[]{:S(2)}) collective-permute-start(bf16[272,128]{1,0:T(8,128)(2,1)S(1)} %get-tuple-element.29), channel_id=1, source_target_pairs={{0,32},{8,40},{16,48},{24,56},{32,0},{40,8},{48,16},{56,24},{1,33}... | collective-permute-start | bytes 208904 | tf_op jit(solution)/shard_map/ppermute | solution.py:266
  47.1 2.7 %collective-permute-start.7 = (bf16[272,128]{1,0:T(8,128)(2,1)S(1)}, bf16[272,128]{1,0:T(8,128)(2,1)S(1)}, u32[]{:S(2)}, u32[]{:S(2)}) collective-permute-start(bf16[272,128]{1,0:T(8,128)(2,1)S(1)} %get-tuple-element.30), channel_id=1, source_target_pairs={{0,48},{8,56},{16,0},{24,8},{32,16},{40,24},{48,32},{56,40},{1,49}... | collective-permute-start | bytes 208904 | tf_op jit(solution)/shard_map/ppermute | solution.py:266
  49.8 0.5 collective-permute-start.9
  50.3 1.3 %collective-permute-done.6.refs_2_ = bf16[272,128]{1,0:T(8,128)(2,1)S(1)} collective-permute-done((bf16[272,128]{1,0:T(8,128)(2,1)S(1)}, bf16[272,128]{1,0:T(8,128)(2,1)S(1)}, u32[]{:S(2)}, u32[]{:S(2)}) %collective-permute-start.6) | collective-permute-done | bytes 69664 | tf_op jit(solution)/shard_map/ppermute | solution.py:266
  51.6 1.6 %collective-permute-done.7.refs_3_ = bf16[272,128]{1,0:T(8,128)(2,1)S(1)} collective-permute-done((bf16[272,128]{1,0:T(8,128)(2,1)S(1)}, bf16[272,128]{1,0:T(8,128)(2,1)S(1)}, u32[]{:S(2)}, u32[]{:S(2)}) %collective-permute-start.7) | collective-permute-done | bytes 69664 | tf_op jit(solution)/shard_map/ppermute | solution.py:266
  53.2 1.2 %collective-permute-done.11.refs_7_ = bf16[272,128]{1,0:T(8,128)(2,1)S(1)} collective-permute-done((bf16[272,128]{1,0:T(8,128)(2,1)S(1)}, bf16[272,128]{1,0:T(8,128)(2,1)S(1)}, u32[]{:S(2)}, u32[]{:S(2)}) %collective-permute-start.11) | collective-permute-done | bytes 69664 | tf_op jit(solution)/shard_map/ppermute | solution.py:270
  54.5 1.3 %shard_map.87.u0 = bf16[144,384]{1,0:T(8,128)(2,1)S(1)} custom-call(s32[8,128]{1,0:T(8,128)S(1)} %get-tuple-element.19.target_ref, bf16[384,128]{1,0:T(8,128)(2,1)S(1)} %bitcast.10, bf16[272,128]{1,0:T(8,128)(2,1)S(1)} %get-tuple-element.27.refs_0_, bf16[272,128]{1,0:T(8,128)(2,1)S(1)} %collective-permute-done.5.refs_1_, ...), custom_call_target="tpu_custom_call" | custom-call | bytes 4500000 | tf_op jit(solution)/shard_map/pallas_call | solution.py:18
  55.9 1.8 %collective-permute-start.13 = (bf16[144,384]{1,0:T(8,128)(2,1)S(1)}, bf16[144,384]{1,0:T(8,128)(2,1)S(1)}, u32[]{:S(2)}, u32[]{:S(2)}) collective-permute-start(bf16[144,384]{1,0:T(8,128)(2,1)S(1)} %shard_map.87.u0), channel_id=1, source_target_pairs={{0,128},{64,192},{128,0},{192,64},{1,129},{65,193},{129,1},{193,65... | collective-permute-start | bytes 331784 | tf_op jit(solution)/shard_map/ppermute | solution.py:254
  57.6 1.8 %collective-permute-start.14 = (bf16[144,384]{1,0:T(8,128)(2,1)S(1)}, bf16[144,384]{1,0:T(8,128)(2,1)S(1)}, u32[]{:S(2)}, u32[]{:S(2)}) collective-permute-start(bf16[144,384]{1,0:T(8,128)(2,1)S(1)} %shard_map.87.u0), channel_id=1, source_target_pairs={{0,192},{64,0},{128,64},{192,128},{1,193},{65,1},{129,65},{193,129... | collective-permute-start | bytes 331784 | tf_op jit(solution)/shard_map/ppermute | solution.py:254
  59.5 4.7 %shard_map.88.r = f32[384,256]{1,0:T(8,128)S(1)} custom-call(s32[3,16]{1,0:T(4,128)S(1)} %copy-done.4, bf16[3,16,8,128]{3,2,1,0:T(8,128)(2,1)S(1)} %copy-done.1, f32[48,2,16]{2,1,0:T(2,128)S(1)} %bitcast.14, bf16[3,16,1,256,256]{4,3,2,1,0:T(8,128)(2,1)} %c_ref.1), custom_call_target="tpu_custom_call" | custom-call | bytes 15000000 | tf_op jit(solution)/shard_map/pallas_call | solution.py:18
  64.2 0.4 collective-permute-done.12.u1
  64.6 0.6 collective-permute-done.14.u3
  65.2 1.2 %shard_map.89 = bf16[48,1024]{1,0:T(8,128)(2,1)} custom-call(bf16[144,384]{1,0:T(8,128)(2,1)S(1)} %shard_map.87.u0, bf16[144,384]{1,0:T(8,128)(2,1)S(1)} %collective-permute-done.12.u1, bf16[144,384]{1,0:T(8,128)(2,1)S(1)} %collective-permute-done.13.u2, bf16[144,384]{1,0:T(8,128)(2,1)S(1)} %collective-permute-done.14.u3, f32[384,256]{1,0:T(8,128)S(1)} %shard_map.88.r), custom_call_target="tpu_custom_call" | custom-call | bytes 3000000 | tf_op jit(solution)/shard_map/pallas_call | solution.py:18
  (23 shorter events, 0.1 us)
Async XLA Ops:
  0.0 9.7 %collective-permute-start = (bf16[160,1024]{1,0:T(8,128)(2,1)}, bf16[160,1024]{1,0:T(8,128)(2,1)S(1)}, u32[]{:S(2)}, u32[]{:S(2)}) collective-permute-start(bf16[160,1024]{1,0:T(8,128)(2,1)} %bitcast.11), channel_id=1, source_target_pairs={{0,1},{1,2},{2,3},{3,0},{4,5},{5,6},{6,7},{7,4},{8,9},{9,10},{10,1... | collective-permute-start | bytes 983048 | tf_op jit(solution)/shard_map/ppermute | solution.py:258
  2.2 8.7 %collective-permute-start.1 = (bf16[160,1024]{1,0:T(8,128)(2,1)}, bf16[160,1024]{1,0:T(8,128)(2,1)S(1)}, u32[]{:S(2)}, u32[]{:S(2)}) collective-permute-start(bf16[160,1024]{1,0:T(8,128)(2,1)} %bitcast.12), channel_id=1, source_target_pairs={{0,3},{1,0},{2,1},{3,2},{4,7},{5,4},{6,5},{7,6},{8,11},{9,8},{10,9... | collective-permute-start | bytes 983048 | tf_op jit(solution)/shard_map/ppermute | solution.py:258
  2.2 1.1 %copy-start = (bf16[1280,1,256]{2,0,1:T(8,128)(2,1)S(1)}, bf16[1280,1,256]{2,0,1:T(8,128)(2,1)}, u32[]{:S(2)}) copy-start(bf16[1280,1,256]{2,0,1:T(8,128)(2,1)} %param.9) | copy-start | bytes 1966084
  3.3 1.0 %copy-start.2 = (bf16[1024,160]{0,1:T(8,128)(2,1)S(1)}, bf16[1024,160]{0,1:T(8,128)(2,1)}, u32[]{:S(2)}) copy-start(bf16[1024,160]{0,1:T(8,128)(2,1)} %param.8) | copy-start | bytes 983044
  4.5 9.8 %collective-permute-start.2 = (bf16[256,640]{1,0:T(8,128)(2,1)S(1)}, bf16[256,640]{1,0:T(8,128)(2,1)S(1)}, u32[]{:S(2)}, u32[]{:S(2)}) collective-permute-start(bf16[256,640]{1,0:T(8,128)(2,1)S(1)} %get-tuple-element.21), channel_id=1, source_target_pairs={{0,4},{1,5},{2,6},{3,7},{4,0},{5,1},{6,2},{7,3},{8,12},{9,13},{10,... | collective-permute-start | bytes 983048 | tf_op jit(solution)/shard_map/ppermute | solution.py:262
  6.3 0.7 %copy-start.5 = (s32[512,1]{0,1:T(1,128)S(1)}, s32[512,1]{0,1:T(1,128)}, u32[]{:S(2)}) copy-start(s32[512,1]{0,1:T(1,128)} %param.14) | copy-start | bytes 6148
  7.0 0.7 %copy-start.6 = (s32[512]{0:T(512)S(1)}, s32[512]{0:T(512)}, u32[]{:S(2)}) copy-start(s32[512]{0:T(512)} %param.15) | copy-start | bytes 6148
  10.9 5.4 %collective-permute-start.3 = (bf16[80,1024]{1,0:T(8,128)(2,1)S(1)}, bf16[80,1024]{1,0:T(8,128)(2,1)S(1)}, u32[]{:S(2)}, u32[]{:S(2)}) collective-permute-start(bf16[80,1024]{1,0:T(8,128)(2,1)S(1)} %slice.6), channel_id=1, source_target_pairs={{0,1},{1,2},{2,3},{3,0},{4,5},{5,6},{6,7},{7,4},{8,9},{9,10},{10,1... | collective-permute-start | bytes 491528 | tf_op jit(solution)/shard_map/ppermute | solution.py:258
  11.5 6.6 %collective-permute-start.4 = (bf16[80,1024]{1,0:T(8,128)(2,1)S(1)}, bf16[80,1024]{1,0:T(8,128)(2,1)S(1)}, u32[]{:S(2)}, u32[]{:S(2)}) collective-permute-start(bf16[80,1024]{1,0:T(8,128)(2,1)S(1)} %slice.7), channel_id=1, source_target_pairs={{0,3},{1,0},{2,1},{3,2},{4,7},{5,4},{6,5},{7,6},{8,11},{9,8},{10,9... | collective-permute-start | bytes 491528 | tf_op jit(solution)/shard_map/ppermute | solution.py:258
  13.1 41.4 %copy-start.1 = (bf16[3,16,8,128]{3,2,1,0:T(8,128)(2,1)S(1)}, bf16[3,16,8,128]{3,2,1,0:T(8,128)(2,1)}, u32[]{:S(2)}) copy-start(bf16[3,16,8,128]{3,2,1,0:T(8,128)(2,1)} %q_ref.1) | copy-start | bytes 294916
  13.1 46.4 %copy-start.3 = (f32[3,16,1,16,2]{3,4,2,1,0:T(2,128)S(1)}, f32[3,16,1,16,2]{3,4,2,1,0:T(2,128)}, u32[]{:S(2)}) copy-start(f32[3,16,1,16,2]{3,4,2,1,0:T(2,128)} %param.12) | copy-start | bytes 18436
  13.1 46.4 %copy-start.4 = (s32[3,16]{1,0:T(4,128)S(1)}, s32[3,16]{1,0:T(4,128)}, u32[]{:S(2)}) copy-start(s32[3,16]{1,0:T(4,128)} %len_ref.1) | copy-start | bytes 580
  39.3 10.5 %collective-permute-start.5 = (bf16[272,128]{1,0:T(8,128)(2,1)S(1)}, bf16[272,128]{1,0:T(8,128)(2,1)S(1)}, u32[]{:S(2)}, u32[]{:S(2)}) collective-permute-start(bf16[272,128]{1,0:T(8,128)(2,1)S(1)} %get-tuple-element.28), channel_id=1, source_target_pairs={{0,16},{8,24},{16,32},{24,40},{32,48},{40,56},{48,0},{56,8},{1,17}... | collective-permute-start | bytes 208904 | tf_op jit(solution)/shard_map/ppermute | solution.py:266
  42.6 9.0 %collective-permute-start.6 = (bf16[272,128]{1,0:T(8,128)(2,1)S(1)}, bf16[272,128]{1,0:T(8,128)(2,1)S(1)}, u32[]{:S(2)}, u32[]{:S(2)}) collective-permute-start(bf16[272,128]{1,0:T(8,128)(2,1)S(1)} %get-tuple-element.29), channel_id=1, source_target_pairs={{0,32},{8,40},{16,48},{24,56},{32,0},{40,8},{48,16},{56,24},{1,33}... | collective-permute-start | bytes 208904 | tf_op jit(solution)/shard_map/ppermute | solution.py:266
  47.1 6.1 %collective-permute-start.7 = (bf16[272,128]{1,0:T(8,128)(2,1)S(1)}, bf16[272,128]{1,0:T(8,128)(2,1)S(1)}, u32[]{:S(2)}, u32[]{:S(2)}) collective-permute-start(bf16[272,128]{1,0:T(8,128)(2,1)S(1)} %get-tuple-element.30), channel_id=1, source_target_pairs={{0,48},{8,56},{16,0},{24,8},{32,16},{40,24},{48,32},{56,40},{1,49}... | collective-permute-start | bytes 208904 | tf_op jit(solution)/shard_map/ppermute | solution.py:266
  49.8 3.4 %collective-permute-start.8 = (bf16[272,128]{1,0:T(8,128)(2,1)S(1)}, bf16[272,128]{1,0:T(8,128)(2,1)S(1)}, u32[]{:S(2)}, u32[]{:S(2)}) collective-permute-start(bf16[272,128]{1,0:T(8,128)(2,1)S(1)} %get-tuple-element.27.refs_0_), channel_id=1, source_target_pairs={{0,8},{8,0},{16,24},{24,16},{32,40},{40,32},{48,56},{56,48},{1,9},... | collective-permute-start | bytes 208904 | tf_op jit(solution)/shard_map/ppermute | solution.py:270
  49.8 3.4 %collective-permute-start.9 = (bf16[272,128]{1,0:T(8,128)(2,1)S(1)}, bf16[272,128]{1,0:T(8,128)(2,1)S(1)}, u32[]{:S(2)}, u32[]{:S(2)}) collective-permute-start(bf16[272,128]{1,0:T(8,128)(2,1)S(1)} %collective-permute-done.5.refs_1_), channel_id=1, source_target_pairs={{0,8},{8,0},{16,24},{24,16},{32,40},{40,32},{48,56},{56,48},{1,9},... | collective-permute-start | bytes 208904 | tf_op jit(solution)/shard_map/ppermute | solution.py:270
  51.6 1.6 %collective-permute-start.10 = (bf16[272,128]{1,0:T(8,128)(2,1)S(1)}, bf16[272,128]{1,0:T(8,128)(2,1)S(1)}, u32[]{:S(2)}, u32[]{:S(2)}) collective-permute-start(bf16[272,128]{1,0:T(8,128)(2,1)S(1)} %collective-permute-done.6.refs_2_), channel_id=1, source_target_pairs={{0,8},{8,0},{16,24},{24,16},{32,40},{40,32},{48,56},{56,48},{1,9},... | collective-permute-start | bytes 208904 | tf_op jit(solution)/shard_map/ppermute | solution.py:270
  53.2 1.3 %collective-permute-start.11 = (bf16[272,128]{1,0:T(8,128)(2,1)S(1)}, bf16[272,128]{1,0:T(8,128)(2,1)S(1)}, u32[]{:S(2)}, u32[]{:S(2)}) collective-permute-start(bf16[272,128]{1,0:T(8,128)(2,1)S(1)} %collective-permute-done.7.refs_3_), channel_id=1, source_target_pairs={{0,8},{8,0},{16,24},{24,16},{32,40},{40,32},{48,56},{56,48},{1,9},... | collective-permute-start | bytes 208904 | tf_op jit(solution)/shard_map/ppermute | solution.py:270
  55.8 8.8 %collective-permute-start.12 = (bf16[144,384]{1,0:T(8,128)(2,1)S(1)}, bf16[144,384]{1,0:T(8,128)(2,1)S(1)}, u32[]{:S(2)}, u32[]{:S(2)}) collective-permute-start(bf16[144,384]{1,0:T(8,128)(2,1)S(1)} %shard_map.87.u0), channel_id=1, source_target_pairs={{0,64},{64,128},{128,192},{192,0},{1,65},{65,129},{129,193},{193,1... | collective-permute-start | bytes 331784 | tf_op jit(solution)/shard_map/ppermute | solution.py:254
  55.9 8.7 %collective-permute-start.13 = (bf16[144,384]{1,0:T(8,128)(2,1)S(1)}, bf16[144,384]{1,0:T(8,128)(2,1)S(1)}, u32[]{:S(2)}, u32[]{:S(2)}) collective-permute-start(bf16[144,384]{1,0:T(8,128)(2,1)S(1)} %shard_map.87.u0), channel_id=1, source_target_pairs={{0,128},{64,192},{128,0},{192,64},{1,129},{65,193},{129,1},{193,65... | collective-permute-start | bytes 331784 | tf_op jit(solution)/shard_map/ppermute | solution.py:254
  57.6 7.6 %collective-permute-start.14 = (bf16[144,384]{1,0:T(8,128)(2,1)S(1)}, bf16[144,384]{1,0:T(8,128)(2,1)S(1)}, u32[]{:S(2)}, u32[]{:S(2)}) collective-permute-start(bf16[144,384]{1,0:T(8,128)(2,1)S(1)} %shard_map.87.u0), channel_id=1, source_target_pairs={{0,192},{64,0},{128,64},{192,128},{1,193},{65,1},{129,65},{193,129... | collective-permute-start | bytes 331784 | tf_op jit(solution)/shard_map/ppermute | solution.py:254

commit v6 on v5

--- a/solution.py
+++ b/solution.py
@@ -102,8 +102,8 @@
 
 def resident_kernel(len_ref, q_ref, sc_ref, c_ref, out_ref, buf, sems):
     copies = [
-        pltpu.make_async_copy(c_ref.at[i // 2, pl.ds(i % 2 * 8, 8), 0], buf.at[i // 2, pl.ds(i % 2 * 8, 8)], sems.at[i])
-        for i in range(6)
+        pltpu.make_async_copy(c_ref.at[i, :, 0], buf.at[i], sems.at[i])
+        for i in range(3)
     ]
     for c in copies:
         c.start()
@@ -118,11 +118,10 @@
             parts = [p.astype(BF16) for p in three(sc_ref[pl.ds(group * 16, 16), half, :])]
             spread.append((dot(parts[0], pick, 1, 0) + dot(parts[1], pick, 1, 0)) + dot(parts[2], pick, 1, 0))
         ks, vs = spread[0] * (128.0**-0.5), spread[1]
-        turned = jnp.transpose(jnp.concatenate([q_ref[group, n].astype(F32) for n in range(16)], axis=0))
+        turned = jnp.transpose(q_ref[pl.ds(group * 128, 128), :].astype(F32))
+        copies[group].wait()
         s = jnp.zeros((256, 128), F32)
         for n in range(0, 16, 2):
-            if n % 8 == 0:
-                copies[group * 2 + n // 8].wait()
             keys = jnp.concatenate([buf[group, n, :, :128], buf[group, n + 1, :, :128]], axis=1)
             own = [jnp.where((lane128 >> 3) == n + i, turned, 0.0).astype(BF16) for i in range(2)]
             s = s + dot(keys, jnp.concatenate(own, axis=0), 1, 0)
@@ -191,30 +190,43 @@
         outs[d][...] = dot(codes, window_ref[d], 1, 0).astype(BF16)
 
 
-def join_kernel(target_ref, q_ref, *refs):
-    parts, out_ref, tmp = refs[:8], refs[8], refs[9]
+def join(steps, target_ref, q_ref, parts, tmp, acc, top, den):
     batch = lax.axis_index("batch")
     zh, core = batch // 2, lax.rem(batch, 2)
     q = q_ref[...]
     request = lax.broadcasted_iota(jnp.int32, (384, 128), 0) >> 3
-    scales, top = [], jnp.full((384, 128), LOW, F32)
-    for i in range(8):
-        origin = lax.rem(zh + 4 - i % 4, 4) * 2 + (core if i < 4 else 1 - core)
-        rows = parts[i][pl.ds(256, 16), :].astype(F32)
+    scales, highest = [], jnp.broadcast_to(top, (384, 128))
+    for i, part in enumerate(parts):
+        half = len(steps)
+        origin = lax.rem(zh + 4 - steps[i % half], 4) * 2 + (core if i < half else 1 - core)
+        rows = part[pl.ds(256, 16), :].astype(F32)
         key_scale = (rows[0:1] + rows[1:2]) + rows[2:3]
         scales.append((rows[3:4] + rows[4:5]) + rows[5:6])
-        s = dot(q, parts[i][pl.ds(0, 128), :], 1, 0) * (key_scale * (128.0**-0.5))
+        s = dot(q, part[pl.ds(0, 128), :], 1, 0) * (key_scale * (128.0**-0.5))
         s = jnp.where(request == target_ref[pl.ds(origin, 1), :], s, -jnp.inf)
         tmp[i] = s
-        top = jnp.maximum(top, s)
-    top = jnp.max(top, axis=1, keepdims=True)
-    total = jnp.zeros((384, 128), F32)
-    acc = jnp.zeros((384, 128), F32)
-    for i in range(8):
-        e = jnp.exp(tmp[i] - top)
+        highest = jnp.maximum(highest, s)
+    highest = jnp.max(highest, axis=1, keepdims=True)
+    share = jnp.exp(top - highest)
+    acc, total = acc * share, jnp.zeros((384, 128), F32)
+    for i, part in enumerate(parts):
+        e = jnp.exp(tmp[i] - highest)
         total = total + e
-        acc = acc + dot((e * scales[i]).astype(BF16), parts[i][pl.ds(128, 128), :], 1, 1)
-    den = jnp.sum(total, axis=1, keepdims=True)
+        acc = acc + dot((e * scales[i]).astype(BF16), part[pl.ds(128, 128), :], 1, 1)
+    return acc, highest, den * share + jnp.sum(total, axis=1, keepdims=True)
+
+
+def first_kernel(target_ref, q_ref, *refs):
+    parts, (acc_ref, stat_ref, tmp) = refs[:6], refs[6:]
+    low = jnp.full((384, 1), LOW, F32)
+    acc, top, den = join((0, 1, 2), target_ref, q_ref, parts, tmp, jnp.zeros((384, 128), F32), low, jnp.zeros((384, 1), F32))
+    acc_ref[...] = acc
+    stat_ref[...] = pack_columns((top, den))
+
+
+def last_kernel(target_ref, q_ref, acc_ref, stat_ref, own_ref, oth_ref, out_ref, tmp):
+    top, den = stat_ref[:, 0:1], stat_ref[:, 1:2]
+    acc, top, den = join((3,), target_ref, q_ref, (own_ref, oth_ref), tmp, acc_ref[...], top, den)
     out_ref[pl.ds(0, 128), :] = jnp.transpose(acc).astype(BF16)
     stats = pack_columns(three(top) + three(den))
     out_ref[pl.ds(128, 16), :] = jnp.transpose(stats)[:16].astype(BF16)
@@ -298,15 +310,20 @@
     cuts = call(quantize_kernel, [shape(272, 128)] * 4, (sums, window), [VMEM] * 2)
 
     parts = [cuts[0]] + [zh_shift(cuts[d], d) for d in (1, 2, 3)]
-    parts = parts + [core_swap(v) for v in parts]
+    swapped = [core_swap(v) for v in parts]
+    flat = queries.reshape(384, 128)
+    so_far = call(
+        first_kernel, [shape(384, 128, dtype=F32)] * 2, (target, flat, *parts[:3], *swapped[:3]), [VMEM] * 8,
+        scratch=[pltpu.VMEM((6, 384, 128), F32)], cost=1,
+    )
     sums = call(
-        join_kernel, shape(144, 384), (target, queries.reshape(384, 128), *parts), [VMEM] * 10,
-        scratch=[pltpu.VMEM((8, 384, 128), F32)], cost=1.5,
+        last_kernel, shape(144, 384), (target, flat, *so_far, parts[3], swapped[3]), [VMEM] * 6,
+        scratch=[pltpu.VMEM((2, 384, 128), F32)], cost=0.7,
     )
     sums = [sums] + [role_shift(sums, d) for d in (1, 2, 3)]
     res = call(
-        resident_kernel, shape(384, 256, dtype=F32), (clen, queries, jnp.swapaxes(scales, 3, 4).reshape(48, 2, 16), codes),
-        [SMEM, VMEM, VMEM, ANY], scratch=[pltpu.VMEM((3, 16, 256, 256), BF16), pltpu.SemaphoreType.DMA((6,))], cost=5,
+        resident_kernel, shape(384, 256, dtype=F32), (clen, flat, jnp.swapaxes(scales, 3, 4).reshape(48, 2, 16), codes),
+        [SMEM, VMEM, VMEM, ANY], scratch=[pltpu.VMEM((3, 16, 256, 256), BF16), pltpu.SemaphoreType.DMA((3,))], cost=5,
     )
     out = call(final_kernel, shape(48, 1024), (*sums, res), [VMEM] * 5, scratch=[pltpu.VMEM((384, 128), F32)])
     return out.reshape(3, 16, 1024)

time: 66.6 us -> 66.3 us (level)
  waiting for transfers between devices: 10.7 us -> 9.93 us
    ppermute x4, waiting for transfers between devices: 1.25 us -> 0.29 us  [core_swap(): return lax.ppermute(v, 'batch', [(i, i ^ 1) for i in range(8)])]
    pallas_call x8 -> x9, Pallas kernels: 12.2 us -> 12.7 us  [call(): pl.pallas_call(kernel, out_shape=outs, in_specs=specs, out_specs=jax.tree...]
  transfers between devices with their start and end apart: 15 -> 15, of which waited for: 9 -> 9; matrix products, arithmetic and copies ran while one was open for 0% -> 0% of each run, Pallas kernels for 11% -> 13%
where the time goes in v6:
time: 66.3 us; the launch traced here: 66.1 us
  starting transfers between devices  20.9 us (32%)
  blocking collectives  19 us (29%)
  Pallas kernels  12.7 us (19%)
  waiting for transfers between devices  9.93 us (15%)
  local copies, waits for them, and re-layouts  3.46 us (5%)
    all_to_all x1, blocking collectives, body(): lax.all_to_all(outs, ('role', 'tensor'), 0, 0, axis_index_groups=groups)  19 us
    pallas_call x9, Pallas kernels, call(): pl.pallas_call(kernel, out_shape=outs, in_specs=specs, out_specs=jax.tree...  12.7 us
    ppermute x3, starting transfers between devices, zh_shift(): return lax.ppermute(v, 'batch', [(i, (i + 2 * d) % 8) for i in range(8)])  10.5 us
    ppermute x4, waiting for transfers between devices, x_shift(): lax.ppermute(v, 'tensor', [(z * 4 + x, z * 4 + (x + d) % 4) for z in rang...  5.5 us
    ppermute x4, starting transfers between devices, x_shift(): lax.ppermute(v, 'tensor', [(z * 4 + x, z * 4 + (x + d) % 4) for z in rang...  4.4 us
    ppermute x3, starting transfers between devices, role_shift(): return lax.ppermute(v, 'role', [(i, (i + d) % 4) for i in range(4)])  3.66 us
    unnamed x14, local copies, waits for them, and re-layouts  3.43 us
    ppermute x3, waiting for transfers between devices, zh_shift(): return lax.ppermute(v, 'batch', [(i, (i + 2 * d) % 8) for i in range(8)])  2.93 us
  transfers between devices with their start and end apart: 15, of which 9 were waited for; matrix products, arithmetic and copies ran while one was open for 0% of the time, Pallas kernels for 13%

profile of v6, /device:TPU:6, one launch (start us, length us, event | category | flops | bytes accessed | tf_op | source)
XLA Modules:
  0.0 66.1 jit_solution(9460045717741503763)
XLA Ops:
  0.0 2.2 %collective-permute-start = (bf16[160,1024]{1,0:T(8,128)(2,1)}, bf16[160,1024]{1,0:T(8,128)(2,1)S(1)}, u32[]{:S(2)}, u32[]{:S(2)}) collective-permute-start(bf16[160,1024]{1,0:T(8,128)(2,1)} %bitcast.13), channel_id=1, source_target_pairs={{0,1},{1,2},{2,3},{3,0},{4,5},{5,6},{6,7},{7,4},{8,9},{9,10},{10,1... | collective-permute-start | bytes 983048 | tf_op jit(solution)/shard_map/ppermute | solution.py:270
  2.2 1.1 %copy-done.1 = bf16[1280,1,256]{2,0,1:T(8,128)(2,1)S(1)} copy-done((bf16[1280,1,256]{2,0,1:T(8,128)(2,1)S(1)}, bf16[1280,1,256]{2,0,1:T(8,128)(2,1)}, u32[]{:S(2)}) %copy-start.1) | copy-done | bytes 655384
  3.3 1.0 %copy-done.2 = bf16[1024,160]{0,1:T(8,128)(2,1)S(1)} copy-done((bf16[1024,160]{0,1:T(8,128)(2,1)S(1)}, bf16[1024,160]{0,1:T(8,128)(2,1)}, u32[]{:S(2)}) %copy-start.2) | copy-done | bytes 327704
  4.5 1.8 %collective-permute-start.2 = (bf16[256,640]{1,0:T(8,128)(2,1)S(1)}, bf16[256,640]{1,0:T(8,128)(2,1)S(1)}, u32[]{:S(2)}, u32[]{:S(2)}) collective-permute-start(bf16[256,640]{1,0:T(8,128)(2,1)S(1)} %get-tuple-element.23), channel_id=1, source_target_pairs={{0,4},{1,5},{2,6},{3,7},{4,0},{5,1},{6,2},{7,3},{8,12},{9,13},{10,... | collective-permute-start | bytes 983048 | tf_op jit(solution)/shard_map/ppermute | solution.py:274
  6.3 0.7 %copy-done.5 = s32[512,1]{0,1:T(1,128)S(1)} copy-done((s32[512,1]{0,1:T(1,128)S(1)}, s32[512,1]{0,1:T(1,128)}, u32[]{:S(2)}) %copy-start.5) | copy-done | bytes 2072
  7.0 0.7 %copy-done.6 = s32[512]{0:T(512)S(1)} copy-done((s32[512]{0:T(512)S(1)}, s32[512]{0:T(512)}, u32[]{:S(2)}) %copy-start.6) | copy-done | bytes 2072
  7.7 1.4 %shard_map.82 = (bf16[1024,1024]{1,0:T(8,128)(2,1)S(1)}, bf16[4,256,128]{2,1,0:T(8,128)(2,1)S(1)}, s32[8,128]{1,0:T(8,128)S(1)}) custom-call(s32[1,512]{1,0:T(1,128)S(1)} %bitcast.17, s32[1,512]{1,0:T(1,128)S(1)} %bitcast.18), custom_call_target="tpu_custom_call" | custom-call | bytes 6000000 | tf_op jit(solution)/shard_map/pallas_call | solution.py:18
  9.1 0.5 collective-permute-done.p1
  9.7 1.2 %collective-permute-done.1.p2 = bf16[160,1024]{1,0:T(8,128)(2,1)S(1)} collective-permute-done((bf16[160,1024]{1,0:T(8,128)(2,1)}, bf16[160,1024]{1,0:T(8,128)(2,1)S(1)}, u32[]{:S(2)}, u32[]{:S(2)}) %collective-permute-start.1) | collective-permute-done | bytes 327712 | tf_op jit(solution)/shard_map/ppermute | solution.py:270
  10.9 0.6 collective-permute-start.3
  11.5 1.6 %collective-permute-start.4 = (bf16[80,1024]{1,0:T(8,128)(2,1)S(1)}, bf16[80,1024]{1,0:T(8,128)(2,1)S(1)}, u32[]{:S(2)}, u32[]{:S(2)}) collective-permute-start(bf16[80,1024]{1,0:T(8,128)(2,1)S(1)} %slice.7), channel_id=1, source_target_pairs={{0,3},{1,0},{2,1},{3,2},{4,7},{5,4},{6,5},{7,6},{8,11},{9,8},{10,9... | collective-permute-start | bytes 491528 | tf_op jit(solution)/shard_map/ppermute | solution.py:270
  13.1 1.2 %shard_map.84.early_ref = bf16[480,1024]{1,0:T(8,128)(2,1)S(1)} custom-call(bf16[1024,1024]{1,0:T(8,128)(2,1)S(1)} %get-tuple-element.24.turn_ref, bf16[160,1024]{1,0:T(8,128)(2,1)S(1)} %get-tuple-element.25.p0, bf16[160,1024]{1,0:T(8,128)(2,1)S(1)} %collective-permute-done.p1, bf16[160,1024]{1,0:T(8,128)(2,1)S(1)} %collective-permute-done.1.p2), custom_call_target="tpu_custom_call" | custom-call | bytes 4500000 | tf_op jit(solution)/shard_map/pallas_call | solution.py:18
  14.3 2.0 %collective-permute-done.3.p3a = bf16[80,1024]{1,0:T(8,128)(2,1)S(1)} collective-permute-done((bf16[80,1024]{1,0:T(8,128)(2,1)S(1)}, bf16[80,1024]{1,0:T(8,128)(2,1)S(1)}, u32[]{:S(2)}, u32[]{:S(2)}) %collective-permute-start.3) | collective-permute-done | bytes 163872 | tf_op jit(solution)/shard_map/ppermute | solution.py:270
  16.3 1.8 %collective-permute-done.4.p3b = bf16[80,1024]{1,0:T(8,128)(2,1)S(1)} collective-permute-done((bf16[80,1024]{1,0:T(8,128)(2,1)S(1)}, bf16[80,1024]{1,0:T(8,128)(2,1)S(1)}, u32[]{:S(2)}, u32[]{:S(2)}) %collective-permute-start.4) | collective-permute-done | bytes 163872 | tf_op jit(solution)/shard_map/ppermute | solution.py:270
  18.1 1.5 %shard_map.85 = bf16[8,256,256]{2,1,0:T(8,128)(2,1)S(1)} custom-call(bf16[256,640]{1,0:T(8,128)(2,1)S(1)} %get-tuple-element.22.keep_ref, bf16[256,640]{1,0:T(8,128)(2,1)S(1)} %collective-permute-done.2.got_ref, bf16[1024,1024]{1,0:T(8,128)(2,1)S(1)} %get-tuple-element.24.turn_ref, bf16[480,1024]{1,0:T(8,128)(2,1)S(1)} %shard_map.84.early_ref, ...), custom_call_target="tpu_custom_call" | custom-call | bytes 3000000 | tf_op jit(solution)/shard_map/pallas_call | solution.py:18
  19.5 19.0 %all_to_all.5.sum_ref = bf16[8,256,256]{2,1,0:T(8,128)(2,1)S(1)} all-to-all(bf16[8,256,256]{2,1,0:T(8,128)(2,1)S(1)} %shard_map.85), channel_id=1, replica_groups={{0,4,64,68,128,132,192,196},{1,5,65,69,129,133,193,197},{2,6,66,70,130,..., dimensions={0} | all-to-all | bytes 2097152 | tf_op jit(solution)/shard_map/all_to_all | solution.py:309
  38.6 0.7 %shard_map.86 = (bf16[272,128]{1,0:T(8,128)(2,1)S(1)}, bf16[272,128]{1,0:T(8,128)(2,1)S(1)}, bf16[272,128]{1,0:T(8,128)(2,1)S(1)}, bf16[272,128]{1,0:T(8,128)(2,1)S(1)}) custom-call(bf16[8,256,256]{2,1,0:T(8,128)(2,1)S(1)} %all_to_all.5.sum_ref, bf16[4,256,128]{2,1,0:T(8,128)(2,1)S(1)} %get-tuple-element.28.window_ref), custom_call_target="tpu_custom_call" | custom-call | bytes 3000000 | tf_op jit(solution)/shard_map/pallas_call | solution.py:18
  39.3 3.3 %collective-permute-start.5 = (bf16[272,128]{1,0:T(8,128)(2,1)S(1)}, bf16[272,128]{1,0:T(8,128)(2,1)S(1)}, u32[]{:S(2)}, u32[]{:S(2)}) collective-permute-start(bf16[272,128]{1,0:T(8,128)(2,1)S(1)} %get-tuple-element.30), channel_id=1, source_target_pairs={{0,16},{8,24},{16,32},{24,40},{32,48},{40,56},{48,0},{56,8},{1,17}... | collective-permute-start | bytes 208904 | tf_op jit(solution)/shard_map/ppermute | solution.py:278
  42.6 4.5 %collective-permute-start.6 = (bf16[272,128]{1,0:T(8,128)(2,1)S(1)}, bf16[272,128]{1,0:T(8,128)(2,1)S(1)}, u32[]{:S(2)}, u32[]{:S(2)}) collective-permute-start(bf16[272,128]{1,0:T(8,128)(2,1)S(1)} %get-tuple-element.31), channel_id=1, source_target_pairs={{0,32},{8,40},{16,48},{24,56},{32,0},{40,8},{48,16},{56,24},{1,33}... | collective-permute-start | bytes 208904 | tf_op jit(solution)/shard_map/ppermute | solution.py:278
  47.1 2.7 %collective-permute-start.10 = (bf16[272,128]{1,0:T(8,128)(2,1)S(1)}, bf16[272,128]{1,0:T(8,128)(2,1)S(1)}, u32[]{:S(2)}, u32[]{:S(2)}) collective-permute-start(bf16[272,128]{1,0:T(8,128)(2,1)S(1)} %get-tuple-element.34), channel_id=1, source_target_pairs={{0,48},{8,56},{16,0},{24,8},{32,16},{40,24},{48,32},{56,40},{1,49}... | collective-permute-start | bytes 208904 | tf_op jit(solution)/shard_map/ppermute | solution.py:278
  49.8 0.5 collective-permute-start.8
  50.3 1.3 %collective-permute-done.6.refs_2_ = bf16[272,128]{1,0:T(8,128)(2,1)S(1)} collective-permute-done((bf16[272,128]{1,0:T(8,128)(2,1)S(1)}, bf16[272,128]{1,0:T(8,128)(2,1)S(1)}, u32[]{:S(2)}, u32[]{:S(2)}) %collective-permute-start.6) | collective-permute-done | bytes 69664 | tf_op jit(solution)/shard_map/ppermute | solution.py:278
  51.6 1.6 %collective-permute-done.10.own_ref = bf16[272,128]{1,0:T(8,128)(2,1)S(1)} collective-permute-done((bf16[272,128]{1,0:T(8,128)(2,1)S(1)}, bf16[272,128]{1,0:T(8,128)(2,1)S(1)}, u32[]{:S(2)}, u32[]{:S(2)}) %collective-permute-start.10) | collective-permute-done | bytes 69664 | tf_op jit(solution)/shard_map/ppermute | solution.py:278
  53.2 0.9 %shard_map.87 = (f32[384,128]{1,0:T(8,128)S(1)}, f32[384,128]{1,0:T(8,128)S(1)}) custom-call(s32[8,128]{1,0:T(8,128)S(1)} %get-tuple-element.21.target_ref, bf16[384,128]{1,0:T(8,128)(2,1)S(1)} %bitcast.9, bf16[272,128]{1,0:T(8,128)(2,1)S(1)} %get-tuple-element.29.refs_0_, bf16[272,128]{1,0:T(8,128)(2,1)S(1)} %collective-permute-done.5.refs_1_, ...), custom_call_target="tpu_custom_call" | custom-call | bytes 3000000 | tf_op jit(solution)/shard_map/pallas_call | solution.py:18
  54.2 0.3 collective-permute-done.11.oth_ref
  54.5 1.0 %shard_map.88.u0 = bf16[144,384]{1,0:T(8,128)(2,1)S(1)} custom-call(s32[8,128]{1,0:T(8,128)S(1)} %get-tuple-element.21.target_ref, bf16[384,128]{1,0:T(8,128)(2,1)S(1)} %bitcast.10, f32[384,128]{1,0:T(8,128)S(1)} %get-tuple-element.32.acc_ref, f32[384,128]{1,0:T(8,128)S(1)} %get-tuple-element.33.stat_ref, ...), custom_call_target="tpu_custom_call" | custom-call | bytes 2100000 | tf_op jit(solution)/shard_map/pallas_call | solution.py:18
  55.5 1.8 %collective-permute-start.13 = (bf16[144,384]{1,0:T(8,128)(2,1)S(1)}, bf16[144,384]{1,0:T(8,128)(2,1)S(1)}, u32[]{:S(2)}, u32[]{:S(2)}) collective-permute-start(bf16[144,384]{1,0:T(8,128)(2,1)S(1)} %shard_map.88.u0), channel_id=1, source_target_pairs={{0,128},{64,192},{128,0},{192,64},{1,129},{65,193},{129,1},{193,65... | collective-permute-start | bytes 331784 | tf_op jit(solution)/shard_map/ppermute | solution.py:266
  57.3 1.8 %collective-permute-start.14 = (bf16[144,384]{1,0:T(8,128)(2,1)S(1)}, bf16[144,384]{1,0:T(8,128)(2,1)S(1)}, u32[]{:S(2)}, u32[]{:S(2)}) collective-permute-start(bf16[144,384]{1,0:T(8,128)(2,1)S(1)} %shard_map.88.u0), channel_id=1, source_target_pairs={{0,192},{64,0},{128,64},{192,128},{1,193},{65,1},{129,65},{193,129... | collective-permute-start | bytes 331784 | tf_op jit(solution)/shard_map/ppermute | solution.py:266
  59.1 4.6 %shard_map.89.r = f32[384,256]{1,0:T(8,128)S(1)} custom-call(s32[3,16]{1,0:T(4,128)S(1)} %copy-done.4, bf16[384,128]{1,0:T(8,128)(2,1)S(1)} %bitcast.11, f32[48,2,16]{2,1,0:T(2,128)S(1)} %bitcast.16, bf16[3,16,1,256,256]{4,3,2,1,0:T(8,128)(2,1)} %c_ref.1), custom_call_target="tpu_custom_call" | custom-call | bytes 15000000 | tf_op jit(solution)/shard_map/pallas_call | solution.py:18
  63.7 0.6 collective-permute-done.12.u1
  64.3 0.6 collective-permute-done.14.u3
  64.9 1.2 %shard_map.90 = bf16[48,1024]{1,0:T(8,128)(2,1)} custom-call(bf16[144,384]{1,0:T(8,128)(2,1)S(1)} %shard_map.88.u0, bf16[144,384]{1,0:T(8,128)(2,1)S(1)} %collective-permute-done.12.u1, bf16[144,384]{1,0:T(8,128)(2,1)S(1)} %collective-permute-done.13.u2, bf16[144,384]{1,0:T(8,128)(2,1)S(1)} %collective-permute-done.14.u3, f32[384,256]{1,0:T(8,128)S(1)} %shard_map.89.r), custom_call_target="tpu_custom_call" | custom-call | bytes 3000000 | tf_op jit(solution)/shard_map/pallas_call | solution.py:18
  (24 shorter events, 0.4 us)
Async XLA Ops:
  0.0 9.7 %collective-permute-start = (bf16[160,1024]{1,0:T(8,128)(2,1)}, bf16[160,1024]{1,0:T(8,128)(2,1)S(1)}, u32[]{:S(2)}, u32[]{:S(2)}) collective-permute-start(bf16[160,1024]{1,0:T(8,128)(2,1)} %bitcast.13), channel_id=1, source_target_pairs={{0,1},{1,2},{2,3},{3,0},{4,5},{5,6},{6,7},{7,4},{8,9},{9,10},{10,1... | collective-permute-start | bytes 983048 | tf_op jit(solution)/shard_map/ppermute | solution.py:270
  2.2 8.7 %collective-permute-start.1 = (bf16[160,1024]{1,0:T(8,128)(2,1)}, bf16[160,1024]{1,0:T(8,128)(2,1)S(1)}, u32[]{:S(2)}, u32[]{:S(2)}) collective-permute-start(bf16[160,1024]{1,0:T(8,128)(2,1)} %bitcast.14), channel_id=1, source_target_pairs={{0,3},{1,0},{2,1},{3,2},{4,7},{5,4},{6,5},{7,6},{8,11},{9,8},{10,9... | collective-permute-start | bytes 983048 | tf_op jit(solution)/shard_map/ppermute | solution.py:270
  2.2 1.1 %copy-start.1 = (bf16[1280,1,256]{2,0,1:T(8,128)(2,1)S(1)}, bf16[1280,1,256]{2,0,1:T(8,128)(2,1)}, u32[]{:S(2)}) copy-start(bf16[1280,1,256]{2,0,1:T(8,128)(2,1)} %param.9) | copy-start | bytes 1966084
  3.3 1.0 %copy-start.2 = (bf16[1024,160]{0,1:T(8,128)(2,1)S(1)}, bf16[1024,160]{0,1:T(8,128)(2,1)}, u32[]{:S(2)}) copy-start(bf16[1024,160]{0,1:T(8,128)(2,1)} %param.8) | copy-start | bytes 983044
  4.5 9.8 %collective-permute-start.2 = (bf16[256,640]{1,0:T(8,128)(2,1)S(1)}, bf16[256,640]{1,0:T(8,128)(2,1)S(1)}, u32[]{:S(2)}, u32[]{:S(2)}) collective-permute-start(bf16[256,640]{1,0:T(8,128)(2,1)S(1)} %get-tuple-element.23), channel_id=1, source_target_pairs={{0,4},{1,5},{2,6},{3,7},{4,0},{5,1},{6,2},{7,3},{8,12},{9,13},{10,... | collective-permute-start | bytes 983048 | tf_op jit(solution)/shard_map/ppermute | solution.py:274
  6.3 0.7 %copy-start.5 = (s32[512,1]{0,1:T(1,128)S(1)}, s32[512,1]{0,1:T(1,128)}, u32[]{:S(2)}) copy-start(s32[512,1]{0,1:T(1,128)} %param.14) | copy-start | bytes 6148
  7.0 0.7 %copy-start.6 = (s32[512]{0:T(512)S(1)}, s32[512]{0:T(512)}, u32[]{:S(2)}) copy-start(s32[512]{0:T(512)} %param.15) | copy-start | bytes 6148
  10.9 5.4 %collective-permute-start.3 = (bf16[80,1024]{1,0:T(8,128)(2,1)S(1)}, bf16[80,1024]{1,0:T(8,128)(2,1)S(1)}, u32[]{:S(2)}, u32[]{:S(2)}) collective-permute-start(bf16[80,1024]{1,0:T(8,128)(2,1)S(1)} %slice.6), channel_id=1, source_target_pairs={{0,1},{1,2},{2,3},{3,0},{4,5},{5,6},{6,7},{7,4},{8,9},{9,10},{10,1... | collective-permute-start | bytes 491528 | tf_op jit(solution)/shard_map/ppermute | solution.py:270
  11.5 6.6 %collective-permute-start.4 = (bf16[80,1024]{1,0:T(8,128)(2,1)S(1)}, bf16[80,1024]{1,0:T(8,128)(2,1)S(1)}, u32[]{:S(2)}, u32[]{:S(2)}) collective-permute-start(bf16[80,1024]{1,0:T(8,128)(2,1)S(1)} %slice.7), channel_id=1, source_target_pairs={{0,3},{1,0},{2,1},{3,2},{4,7},{5,4},{6,5},{7,6},{8,11},{9,8},{10,9... | collective-permute-start | bytes 491528 | tf_op jit(solution)/shard_map/ppermute | solution.py:270
  13.1 40.2 %copy-start = (bf16[3,16,8,128]{3,2,1,0:T(8,128)(2,1)S(1)}, bf16[3,16,8,128]{3,2,1,0:T(8,128)(2,1)}, u32[]{:S(2)}) copy-start(bf16[3,16,8,128]{3,2,1,0:T(8,128)(2,1)} %param.10) | copy-start | bytes 294916
  13.1 46.0 %copy-start.3 = (f32[3,16,1,16,2]{3,4,2,1,0:T(2,128)S(1)}, f32[3,16,1,16,2]{3,4,2,1,0:T(2,128)}, u32[]{:S(2)}) copy-start(f32[3,16,1,16,2]{3,4,2,1,0:T(2,128)} %param.12) | copy-start | bytes 18436
  13.1 46.0 %copy-start.4 = (s32[3,16]{1,0:T(4,128)S(1)}, s32[3,16]{1,0:T(4,128)}, u32[]{:S(2)}) copy-start(s32[3,16]{1,0:T(4,128)} %len_ref.1) | copy-start | bytes 580
  39.3 10.5 %collective-permute-start.5 = (bf16[272,128]{1,0:T(8,128)(2,1)S(1)}, bf16[272,128]{1,0:T(8,128)(2,1)S(1)}, u32[]{:S(2)}, u32[]{:S(2)}) collective-permute-start(bf16[272,128]{1,0:T(8,128)(2,1)S(1)} %get-tuple-element.30), channel_id=1, source_target_pairs={{0,16},{8,24},{16,32},{24,40},{32,48},{40,56},{48,0},{56,8},{1,17}... | collective-permute-start | bytes 208904 | tf_op jit(solution)/shard_map/ppermute | solution.py:278
  42.6 9.0 %collective-permute-start.6 = (bf16[272,128]{1,0:T(8,128)(2,1)S(1)}, bf16[272,128]{1,0:T(8,128)(2,1)S(1)}, u32[]{:S(2)}, u32[]{:S(2)}) collective-permute-start(bf16[272,128]{1,0:T(8,128)(2,1)S(1)} %get-tuple-element.31), channel_id=1, source_target_pairs={{0,32},{8,40},{16,48},{24,56},{32,0},{40,8},{48,16},{56,24},{1,33}... | collective-permute-start | bytes 208904 | tf_op jit(solution)/shard_map/ppermute | solution.py:278
  47.1 6.1 %collective-permute-start.10 = (bf16[272,128]{1,0:T(8,128)(2,1)S(1)}, bf16[272,128]{1,0:T(8,128)(2,1)S(1)}, u32[]{:S(2)}, u32[]{:S(2)}) collective-permute-start(bf16[272,128]{1,0:T(8,128)(2,1)S(1)} %get-tuple-element.34), channel_id=1, source_target_pairs={{0,48},{8,56},{16,0},{24,8},{32,16},{40,24},{48,32},{56,40},{1,49}... | collective-permute-start | bytes 208904 | tf_op jit(solution)/shard_map/ppermute | solution.py:278
  49.8 3.4 %collective-permute-start.7 = (bf16[272,128]{1,0:T(8,128)(2,1)S(1)}, bf16[272,128]{1,0:T(8,128)(2,1)S(1)}, u32[]{:S(2)}, u32[]{:S(2)}) collective-permute-start(bf16[272,128]{1,0:T(8,128)(2,1)S(1)} %get-tuple-element.29.refs_0_), channel_id=1, source_target_pairs={{0,8},{8,0},{16,24},{24,16},{32,40},{40,32},{48,56},{56,48},{1,9},... | collective-permute-start | bytes 208904 | tf_op jit(solution)/shard_map/ppermute | solution.py:282
  49.8 3.4 %collective-permute-start.8 = (bf16[272,128]{1,0:T(8,128)(2,1)S(1)}, bf16[272,128]{1,0:T(8,128)(2,1)S(1)}, u32[]{:S(2)}, u32[]{:S(2)}) collective-permute-start(bf16[272,128]{1,0:T(8,128)(2,1)S(1)} %collective-permute-done.5.refs_1_), channel_id=1, source_target_pairs={{0,8},{8,0},{16,24},{24,16},{32,40},{40,32},{48,56},{56,48},{1,9},... | collective-permute-start | bytes 208904 | tf_op jit(solution)/shard_map/ppermute | solution.py:282
  51.6 1.6 %collective-permute-start.9 = (bf16[272,128]{1,0:T(8,128)(2,1)S(1)}, bf16[272,128]{1,0:T(8,128)(2,1)S(1)}, u32[]{:S(2)}, u32[]{:S(2)}) collective-permute-start(bf16[272,128]{1,0:T(8,128)(2,1)S(1)} %collective-permute-done.6.refs_2_), channel_id=1, source_target_pairs={{0,8},{8,0},{16,24},{24,16},{32,40},{40,32},{48,56},{56,48},{1,9},... | collective-permute-start | bytes 208904 | tf_op jit(solution)/shard_map/ppermute | solution.py:282
  53.2 1.3 %collective-permute-start.11 = (bf16[272,128]{1,0:T(8,128)(2,1)S(1)}, bf16[272,128]{1,0:T(8,128)(2,1)S(1)}, u32[]{:S(2)}, u32[]{:S(2)}) collective-permute-start(bf16[272,128]{1,0:T(8,128)(2,1)S(1)} %collective-permute-done.10.own_ref), channel_id=1, source_target_pairs={{0,8},{8,0},{16,24},{24,16},{32,40},{40,32},{48,56},{56,48},{1,9},... | collective-permute-start | bytes 208904 | tf_op jit(solution)/shard_map/ppermute | solution.py:282
  55.4 8.9 %collective-permute-start.12 = (bf16[144,384]{1,0:T(8,128)(2,1)S(1)}, bf16[144,384]{1,0:T(8,128)(2,1)S(1)}, u32[]{:S(2)}, u32[]{:S(2)}) collective-permute-start(bf16[144,384]{1,0:T(8,128)(2,1)S(1)} %shard_map.88.u0), channel_id=1, source_target_pairs={{0,64},{64,128},{128,192},{192,0},{1,65},{65,129},{129,193},{193,1... | collective-permute-start | bytes 331784 | tf_op jit(solution)/shard_map/ppermute | solution.py:266
  55.5 8.8 %collective-permute-start.13 = (bf16[144,384]{1,0:T(8,128)(2,1)S(1)}, bf16[144,384]{1,0:T(8,128)(2,1)S(1)}, u32[]{:S(2)}, u32[]{:S(2)}) collective-permute-start(bf16[144,384]{1,0:T(8,128)(2,1)S(1)} %shard_map.88.u0), channel_id=1, source_target_pairs={{0,128},{64,192},{128,0},{192,64},{1,129},{65,193},{129,1},{193,65... | collective-permute-start | bytes 331784 | tf_op jit(solution)/shard_map/ppermute | solution.py:266
  57.3 7.6 %collective-permute-start.14 = (bf16[144,384]{1,0:T(8,128)(2,1)S(1)}, bf16[144,384]{1,0:T(8,128)(2,1)S(1)}, u32[]{:S(2)}, u32[]{:S(2)}) collective-permute-start(bf16[144,384]{1,0:T(8,128)(2,1)S(1)} %shard_map.88.u0), channel_id=1, source_target_pairs={{0,192},{64,0},{128,64},{192,128},{1,193},{65,1},{129,65},{193,129... | collective-permute-start | bytes 331784 | tf_op jit(solution)/shard_map/ppermute | solution.py:266

commit v7 on v6

--- a/solution.py
+++ b/solution.py
@@ -228,8 +228,8 @@
     top, den = stat_ref[:, 0:1], stat_ref[:, 1:2]
     acc, top, den = join((3,), target_ref, q_ref, (own_ref, oth_ref), tmp, acc_ref[...], top, den)
     out_ref[pl.ds(0, 128), :] = jnp.transpose(acc).astype(BF16)
-    stats = pack_columns(three(top) + three(den))
-    out_ref[pl.ds(128, 16), :] = jnp.transpose(stats)[:16].astype(BF16)
+    rows = jnp.transpose(pack_columns((top, den)))
+    out_ref[pl.ds(128, 16), :] = pack_rows(three(rows[0:1]) + three(rows[1:2]), 16).astype(BF16)
 
 
 def final_kernel(u0, u1, u2, u3, r, out_ref, tmp):

time: 66.3 us -> 66.3 us (level)
  no operation moved by 1% of the time
where the time goes in v7:
time: 66.3 us; the launch traced here: 66 us
  starting transfers between devices  20.9 us (32%)
  blocking collectives  19 us (29%)
  Pallas kernels  12.6 us (19%)
  waiting for transfers between devices  9.92 us (15%)
  local copies, waits for them, and re-layouts  3.46 us (5%)
    all_to_all x1, blocking collectives, body(): lax.all_to_all(outs, ('role', 'tensor'), 0, 0, axis_index_groups=groups)  19 us
    pallas_call x9, Pallas kernels, call(): pl.pallas_call(kernel, out_shape=outs, in_specs=specs, out_specs=jax.tree...  12.6 us
    ppermute x3, starting transfers between devices, zh_shift(): return lax.ppermute(v, 'batch', [(i, (i + 2 * d) % 8) for i in range(8)])  10.5 us
    ppermute x4, waiting for transfers between devices, x_shift(): lax.ppermute(v, 'tensor', [(z * 4 + x, z * 4 + (x + d) % 4) for z in rang...  5.5 us
    ppermute x4, starting transfers between devices, x_shift(): lax.ppermute(v, 'tensor', [(z * 4 + x, z * 4 + (x + d) % 4) for z in rang...  4.4 us
    ppermute x3, starting transfers between devices, role_shift(): return lax.ppermute(v, 'role', [(i, (i + d) % 4) for i in range(4)])  3.64 us
    unnamed x14, local copies, waits for them, and re-layouts  3.43 us
    ppermute x3, waiting for transfers between devices, zh_shift(): return lax.ppermute(v, 'batch', [(i, (i + 2 * d) % 8) for i in range(8)])  2.93 us
  transfers between devices with their start and end apart: 15, of which 9 were waited for; matrix products, arithmetic and copies ran while one was open for 0% of the time, Pallas kernels for 13%

profile of v7, /device:TPU:6, one launch (start us, length us, event | category | flops | bytes accessed | tf_op | source)
XLA Modules:
  0.0 66.0 jit_solution(15778251169495785010)
XLA Ops:
  0.0 2.2 %collective-permute-start = (bf16[160,1024]{1,0:T(8,128)(2,1)}, bf16[160,1024]{1,0:T(8,128)(2,1)S(1)}, u32[]{:S(2)}, u32[]{:S(2)}) collective-permute-start(bf16[160,1024]{1,0:T(8,128)(2,1)} %bitcast.13), channel_id=1, source_target_pairs={{0,1},{1,2},{2,3},{3,0},{4,5},{5,6},{6,7},{7,4},{8,9},{9,10},{10,1... | collective-permute-start | bytes 983048 | tf_op jit(solution)/shard_map/ppermute | solution.py:270
  2.2 1.1 %copy-done.1 = bf16[1280,1,256]{2,0,1:T(8,128)(2,1)S(1)} copy-done((bf16[1280,1,256]{2,0,1:T(8,128)(2,1)S(1)}, bf16[1280,1,256]{2,0,1:T(8,128)(2,1)}, u32[]{:S(2)}) %copy-start.1) | copy-done | bytes 655384
  3.3 1.0 %copy-done.2 = bf16[1024,160]{0,1:T(8,128)(2,1)S(1)} copy-done((bf16[1024,160]{0,1:T(8,128)(2,1)S(1)}, bf16[1024,160]{0,1:T(8,128)(2,1)}, u32[]{:S(2)}) %copy-start.2) | copy-done | bytes 327704
  4.5 1.8 %collective-permute-start.2 = (bf16[256,640]{1,0:T(8,128)(2,1)S(1)}, bf16[256,640]{1,0:T(8,128)(2,1)S(1)}, u32[]{:S(2)}, u32[]{:S(2)}) collective-permute-start(bf16[256,640]{1,0:T(8,128)(2,1)S(1)} %get-tuple-element.23), channel_id=1, source_target_pairs={{0,4},{1,5},{2,6},{3,7},{4,0},{5,1},{6,2},{7,3},{8,12},{9,13},{10,... | collective-permute-start | bytes 983048 | tf_op jit(solution)/shard_map/ppermute | solution.py:274
  6.3 0.7 %copy-done.5 = s32[512,1]{0,1:T(1,128)S(1)} copy-done((s32[512,1]{0,1:T(1,128)S(1)}, s32[512,1]{0,1:T(1,128)}, u32[]{:S(2)}) %copy-start.5) | copy-done | bytes 2072
  7.0 0.7 %copy-done.6 = s32[512]{0:T(512)S(1)} copy-done((s32[512]{0:T(512)S(1)}, s32[512]{0:T(512)}, u32[]{:S(2)}) %copy-start.6) | copy-done | bytes 2072
  7.7 1.4 %shard_map.82 = (bf16[1024,1024]{1,0:T(8,128)(2,1)S(1)}, bf16[4,256,128]{2,1,0:T(8,128)(2,1)S(1)}, s32[8,128]{1,0:T(8,128)S(1)}) custom-call(s32[1,512]{1,0:T(1,128)S(1)} %bitcast.17, s32[1,512]{1,0:T(1,128)S(1)} %bitcast.18), custom_call_target="tpu_custom_call" | custom-call | bytes 6000000 | tf_op jit(solution)/shard_map/pallas_call | solution.py:18
  9.1 0.5 collective-permute-done.p1
  9.7 1.2 %collective-permute-done.1.p2 = bf16[160,1024]{1,0:T(8,128)(2,1)S(1)} collective-permute-done((bf16[160,1024]{1,0:T(8,128)(2,1)}, bf16[160,1024]{1,0:T(8,128)(2,1)S(1)}, u32[]{:S(2)}, u32[]{:S(2)}) %collective-permute-start.1) | collective-permute-done | bytes 327712 | tf_op jit(solution)/shard_map/ppermute | solution.py:270
  10.9 0.6 collective-permute-start.3
  11.5 1.6 %collective-permute-start.4 = (bf16[80,1024]{1,0:T(8,128)(2,1)S(1)}, bf16[80,1024]{1,0:T(8,128)(2,1)S(1)}, u32[]{:S(2)}, u32[]{:S(2)}) collective-permute-start(bf16[80,1024]{1,0:T(8,128)(2,1)S(1)} %slice.7), channel_id=1, source_target_pairs={{0,3},{1,0},{2,1},{3,2},{4,7},{5,4},{6,5},{7,6},{8,11},{9,8},{10,9... | collective-permute-start | bytes 491528 | tf_op jit(solution)/shard_map/ppermute | solution.py:270
  13.1 1.2 %shard_map.84.early_ref = bf16[480,1024]{1,0:T(8,128)(2,1)S(1)} custom-call(bf16[1024,1024]{1,0:T(8,128)(2,1)S(1)} %get-tuple-element.24.turn_ref, bf16[160,1024]{1,0:T(8,128)(2,1)S(1)} %get-tuple-element.25.p0, bf16[160,1024]{1,0:T(8,128)(2,1)S(1)} %collective-permute-done.p1, bf16[160,1024]{1,0:T(8,128)(2,1)S(1)} %collective-permute-done.1.p2), custom_call_target="tpu_custom_call" | custom-call | bytes 4500000 | tf_op jit(solution)/shard_map/pallas_call | solution.py:18
  14.3 2.0 %collective-permute-done.3.p3a = bf16[80,1024]{1,0:T(8,128)(2,1)S(1)} collective-permute-done((bf16[80,1024]{1,0:T(8,128)(2,1)S(1)}, bf16[80,1024]{1,0:T(8,128)(2,1)S(1)}, u32[]{:S(2)}, u32[]{:S(2)}) %collective-permute-start.3) | collective-permute-done | bytes 163872 | tf_op jit(solution)/shard_map/ppermute | solution.py:270
  16.3 1.8 %collective-permute-done.4.p3b = bf16[80,1024]{1,0:T(8,128)(2,1)S(1)} collective-permute-done((bf16[80,1024]{1,0:T(8,128)(2,1)S(1)}, bf16[80,1024]{1,0:T(8,128)(2,1)S(1)}, u32[]{:S(2)}, u32[]{:S(2)}) %collective-permute-start.4) | collective-permute-done | bytes 163872 | tf_op jit(solution)/shard_map/ppermute | solution.py:270
  18.1 1.5 %shard_map.85 = bf16[8,256,256]{2,1,0:T(8,128)(2,1)S(1)} custom-call(bf16[256,640]{1,0:T(8,128)(2,1)S(1)} %get-tuple-element.22.keep_ref, bf16[256,640]{1,0:T(8,128)(2,1)S(1)} %collective-permute-done.2.got_ref, bf16[1024,1024]{1,0:T(8,128)(2,1)S(1)} %get-tuple-element.24.turn_ref, bf16[480,1024]{1,0:T(8,128)(2,1)S(1)} %shard_map.84.early_ref, ...), custom_call_target="tpu_custom_call" | custom-call | bytes 3000000 | tf_op jit(solution)/shard_map/pallas_call | solution.py:18
  19.5 19.0 %all_to_all.5.sum_ref = bf16[8,256,256]{2,1,0:T(8,128)(2,1)S(1)} all-to-all(bf16[8,256,256]{2,1,0:T(8,128)(2,1)S(1)} %shard_map.85), channel_id=1, replica_groups={{0,4,64,68,128,132,192,196},{1,5,65,69,129,133,193,197},{2,6,66,70,130,..., dimensions={0} | all-to-all | bytes 2097152 | tf_op jit(solution)/shard_map/all_to_all | solution.py:309
  38.6 0.7 %shard_map.86 = (bf16[272,128]{1,0:T(8,128)(2,1)S(1)}, bf16[272,128]{1,0:T(8,128)(2,1)S(1)}, bf16[272,128]{1,0:T(8,128)(2,1)S(1)}, bf16[272,128]{1,0:T(8,128)(2,1)S(1)}) custom-call(bf16[8,256,256]{2,1,0:T(8,128)(2,1)S(1)} %all_to_all.5.sum_ref, bf16[4,256,128]{2,1,0:T(8,128)(2,1)S(1)} %get-tuple-element.28.window_ref), custom_call_target="tpu_custom_call" | custom-call | bytes 3000000 | tf_op jit(solution)/shard_map/pallas_call | solution.py:18
  39.3 3.3 %collective-permute-start.5 = (bf16[272,128]{1,0:T(8,128)(2,1)S(1)}, bf16[272,128]{1,0:T(8,128)(2,1)S(1)}, u32[]{:S(2)}, u32[]{:S(2)}) collective-permute-start(bf16[272,128]{1,0:T(8,128)(2,1)S(1)} %get-tuple-element.30), channel_id=1, source_target_pairs={{0,16},{8,24},{16,32},{24,40},{32,48},{40,56},{48,0},{56,8},{1,17}... | collective-permute-start | bytes 208904 | tf_op jit(solution)/shard_map/ppermute | solution.py:278
  42.6 4.5 %collective-permute-start.6 = (bf16[272,128]{1,0:T(8,128)(2,1)S(1)}, bf16[272,128]{1,0:T(8,128)(2,1)S(1)}, u32[]{:S(2)}, u32[]{:S(2)}) collective-permute-start(bf16[272,128]{1,0:T(8,128)(2,1)S(1)} %get-tuple-element.31), channel_id=1, source_target_pairs={{0,32},{8,40},{16,48},{24,56},{32,0},{40,8},{48,16},{56,24},{1,33}... | collective-permute-start | bytes 208904 | tf_op jit(solution)/shard_map/ppermute | solution.py:278
  47.1 2.7 %collective-permute-start.10 = (bf16[272,128]{1,0:T(8,128)(2,1)S(1)}, bf16[272,128]{1,0:T(8,128)(2,1)S(1)}, u32[]{:S(2)}, u32[]{:S(2)}) collective-permute-start(bf16[272,128]{1,0:T(8,128)(2,1)S(1)} %get-tuple-element.34), channel_id=1, source_target_pairs={{0,48},{8,56},{16,0},{24,8},{32,16},{40,24},{48,32},{56,40},{1,49}... | collective-permute-start | bytes 208904 | tf_op jit(solution)/shard_map/ppermute | solution.py:278
  49.8 0.5 collective-permute-start.8
  50.3 1.3 %collective-permute-done.6.refs_2_ = bf16[272,128]{1,0:T(8,128)(2,1)S(1)} collective-permute-done((bf16[272,128]{1,0:T(8,128)(2,1)S(1)}, bf16[272,128]{1,0:T(8,128)(2,1)S(1)}, u32[]{:S(2)}, u32[]{:S(2)}) %collective-permute-start.6) | collective-permute-done | bytes 69664 | tf_op jit(solution)/shard_map/ppermute | solution.py:278
  51.6 1.6 %collective-permute-done.10.own_ref = bf16[272,128]{1,0:T(8,128)(2,1)S(1)} collective-permute-done((bf16[272,128]{1,0:T(8,128)(2,1)S(1)}, bf16[272,128]{1,0:T(8,128)(2,1)S(1)}, u32[]{:S(2)}, u32[]{:S(2)}) %collective-permute-start.10) | collective-permute-done | bytes 69664 | tf_op jit(solution)/shard_map/ppermute | solution.py:278
  53.2 0.9 %shard_map.87 = (f32[384,128]{1,0:T(8,128)S(1)}, f32[384,128]{1,0:T(8,128)S(1)}) custom-call(s32[8,128]{1,0:T(8,128)S(1)} %get-tuple-element.21.target_ref, bf16[384,128]{1,0:T(8,128)(2,1)S(1)} %bitcast.9, bf16[272,128]{1,0:T(8,128)(2,1)S(1)} %get-tuple-element.29.refs_0_, bf16[272,128]{1,0:T(8,128)(2,1)S(1)} %collective-permute-done.5.refs_1_, ...), custom_call_target="tpu_custom_call" | custom-call | bytes 3000000 | tf_op jit(solution)/shard_map/pallas_call | solution.py:18
  54.2 0.3 collective-permute-done.11.oth_ref
  54.5 0.9 %shard_map.88.u0 = bf16[144,384]{1,0:T(8,128)(2,1)S(1)} custom-call(s32[8,128]{1,0:T(8,128)S(1)} %get-tuple-element.21.target_ref, bf16[384,128]{1,0:T(8,128)(2,1)S(1)} %bitcast.10, f32[384,128]{1,0:T(8,128)S(1)} %get-tuple-element.32.acc_ref, f32[384,128]{1,0:T(8,128)S(1)} %get-tuple-element.33.stat_ref, ...), custom_call_target="tpu_custom_call" | custom-call | bytes 2100000 | tf_op jit(solution)/shard_map/pallas_call | solution.py:18
  55.5 1.7 %collective-permute-start.13 = (bf16[144,384]{1,0:T(8,128)(2,1)S(1)}, bf16[144,384]{1,0:T(8,128)(2,1)S(1)}, u32[]{:S(2)}, u32[]{:S(2)}) collective-permute-start(bf16[144,384]{1,0:T(8,128)(2,1)S(1)} %shard_map.88.u0), channel_id=1, source_target_pairs={{0,128},{64,192},{128,0},{192,64},{1,129},{65,193},{129,1},{193,65... | collective-permute-start | bytes 331784 | tf_op jit(solution)/shard_map/ppermute | solution.py:266
  57.2 1.8 %collective-permute-start.14 = (bf16[144,384]{1,0:T(8,128)(2,1)S(1)}, bf16[144,384]{1,0:T(8,128)(2,1)S(1)}, u32[]{:S(2)}, u32[]{:S(2)}) collective-permute-start(bf16[144,384]{1,0:T(8,128)(2,1)S(1)} %shard_map.88.u0), channel_id=1, source_target_pairs={{0,192},{64,0},{128,64},{192,128},{1,193},{65,1},{129,65},{193,129... | collective-permute-start | bytes 331784 | tf_op jit(solution)/shard_map/ppermute | solution.py:266
  59.1 4.6 %shard_map.89.r = f32[384,256]{1,0:T(8,128)S(1)} custom-call(s32[3,16]{1,0:T(4,128)S(1)} %copy-done.4, bf16[384,128]{1,0:T(8,128)(2,1)S(1)} %bitcast.11, f32[48,2,16]{2,1,0:T(2,128)S(1)} %bitcast.16, bf16[3,16,1,256,256]{4,3,2,1,0:T(8,128)(2,1)} %c_ref.1), custom_call_target="tpu_custom_call" | custom-call | bytes 15000000 | tf_op jit(solution)/shard_map/pallas_call | solution.py:18
  63.7 0.6 collective-permute-done.12.u1
  64.2 0.6 collective-permute-done.14.u3
  64.9 1.2 %shard_map.90 = bf16[48,1024]{1,0:T(8,128)(2,1)} custom-call(bf16[144,384]{1,0:T(8,128)(2,1)S(1)} %shard_map.88.u0, bf16[144,384]{1,0:T(8,128)(2,1)S(1)} %collective-permute-done.12.u1, bf16[144,384]{1,0:T(8,128)(2,1)S(1)} %collective-permute-done.13.u2, bf16[144,384]{1,0:T(8,128)(2,1)S(1)} %collective-permute-done.14.u3, f32[384,256]{1,0:T(8,128)S(1)} %shard_map.89.r), custom_call_target="tpu_custom_call" | custom-call | bytes 3000000 | tf_op jit(solution)/shard_map/pallas_call | solution.py:18
  (24 shorter events, 0.4 us)
Async XLA Ops:
  0.0 9.7 %collective-permute-start = (bf16[160,1024]{1,0:T(8,128)(2,1)}, bf16[160,1024]{1,0:T(8,128)(2,1)S(1)}, u32[]{:S(2)}, u32[]{:S(2)}) collective-permute-start(bf16[160,1024]{1,0:T(8,128)(2,1)} %bitcast.13), channel_id=1, source_target_pairs={{0,1},{1,2},{2,3},{3,0},{4,5},{5,6},{6,7},{7,4},{8,9},{9,10},{10,1... | collective-permute-start | bytes 983048 | tf_op jit(solution)/shard_map/ppermute | solution.py:270
  2.2 8.7 %collective-permute-start.1 = (bf16[160,1024]{1,0:T(8,128)(2,1)}, bf16[160,1024]{1,0:T(8,128)(2,1)S(1)}, u32[]{:S(2)}, u32[]{:S(2)}) collective-permute-start(bf16[160,1024]{1,0:T(8,128)(2,1)} %bitcast.14), channel_id=1, source_target_pairs={{0,3},{1,0},{2,1},{3,2},{4,7},{5,4},{6,5},{7,6},{8,11},{9,8},{10,9... | collective-permute-start | bytes 983048 | tf_op jit(solution)/shard_map/ppermute | solution.py:270
  2.2 1.1 %copy-start.1 = (bf16[1280,1,256]{2,0,1:T(8,128)(2,1)S(1)}, bf16[1280,1,256]{2,0,1:T(8,128)(2,1)}, u32[]{:S(2)}) copy-start(bf16[1280,1,256]{2,0,1:T(8,128)(2,1)} %param.9) | copy-start | bytes 1966084
  3.3 1.0 %copy-start.2 = (bf16[1024,160]{0,1:T(8,128)(2,1)S(1)}, bf16[1024,160]{0,1:T(8,128)(2,1)}, u32[]{:S(2)}) copy-start(bf16[1024,160]{0,1:T(8,128)(2,1)} %param.8) | copy-start | bytes 983044
  4.5 9.8 %collective-permute-start.2 = (bf16[256,640]{1,0:T(8,128)(2,1)S(1)}, bf16[256,640]{1,0:T(8,128)(2,1)S(1)}, u32[]{:S(2)}, u32[]{:S(2)}) collective-permute-start(bf16[256,640]{1,0:T(8,128)(2,1)S(1)} %get-tuple-element.23), channel_id=1, source_target_pairs={{0,4},{1,5},{2,6},{3,7},{4,0},{5,1},{6,2},{7,3},{8,12},{9,13},{10,... | collective-permute-start | bytes 983048 | tf_op jit(solution)/shard_map/ppermute | solution.py:274
  6.3 0.7 %copy-start.5 = (s32[512,1]{0,1:T(1,128)S(1)}, s32[512,1]{0,1:T(1,128)}, u32[]{:S(2)}) copy-start(s32[512,1]{0,1:T(1,128)} %param.14) | copy-start | bytes 6148
  7.0 0.7 %copy-start.6 = (s32[512]{0:T(512)S(1)}, s32[512]{0:T(512)}, u32[]{:S(2)}) copy-start(s32[512]{0:T(512)} %param.15) | copy-start | bytes 6148
  10.9 5.4 %collective-permute-start.3 = (bf16[80,1024]{1,0:T(8,128)(2,1)S(1)}, bf16[80,1024]{1,0:T(8,128)(2,1)S(1)}, u32[]{:S(2)}, u32[]{:S(2)}) collective-permute-start(bf16[80,1024]{1,0:T(8,128)(2,1)S(1)} %slice.6), channel_id=1, source_target_pairs={{0,1},{1,2},{2,3},{3,0},{4,5},{5,6},{6,7},{7,4},{8,9},{9,10},{10,1... | collective-permute-start | bytes 491528 | tf_op jit(solution)/shard_map/ppermute | solution.py:270
  11.5 6.6 %collective-permute-start.4 = (bf16[80,1024]{1,0:T(8,128)(2,1)S(1)}, bf16[80,1024]{1,0:T(8,128)(2,1)S(1)}, u32[]{:S(2)}, u32[]{:S(2)}) collective-permute-start(bf16[80,1024]{1,0:T(8,128)(2,1)S(1)} %slice.7), channel_id=1, source_target_pairs={{0,3},{1,0},{2,1},{3,2},{4,7},{5,4},{6,5},{7,6},{8,11},{9,8},{10,9... | collective-permute-start | bytes 491528 | tf_op jit(solution)/shard_map/ppermute | solution.py:270
  13.1 40.2 %copy-start = (bf16[3,16,8,128]{3,2,1,0:T(8,128)(2,1)S(1)}, bf16[3,16,8,128]{3,2,1,0:T(8,128)(2,1)}, u32[]{:S(2)}) copy-start(bf16[3,16,8,128]{3,2,1,0:T(8,128)(2,1)} %param.10) | copy-start | bytes 294916
  13.1 46.0 %copy-start.3 = (f32[3,16,1,16,2]{3,4,2,1,0:T(2,128)S(1)}, f32[3,16,1,16,2]{3,4,2,1,0:T(2,128)}, u32[]{:S(2)}) copy-start(f32[3,16,1,16,2]{3,4,2,1,0:T(2,128)} %param.12) | copy-start | bytes 18436
  13.1 46.0 %copy-start.4 = (s32[3,16]{1,0:T(4,128)S(1)}, s32[3,16]{1,0:T(4,128)}, u32[]{:S(2)}) copy-start(s32[3,16]{1,0:T(4,128)} %len_ref.1) | copy-start | bytes 580
  39.3 10.5 %collective-permute-start.5 = (bf16[272,128]{1,0:T(8,128)(2,1)S(1)}, bf16[272,128]{1,0:T(8,128)(2,1)S(1)}, u32[]{:S(2)}, u32[]{:S(2)}) collective-permute-start(bf16[272,128]{1,0:T(8,128)(2,1)S(1)} %get-tuple-element.30), channel_id=1, source_target_pairs={{0,16},{8,24},{16,32},{24,40},{32,48},{40,56},{48,0},{56,8},{1,17}... | collective-permute-start | bytes 208904 | tf_op jit(solution)/shard_map/ppermute | solution.py:278
  42.6 9.0 %collective-permute-start.6 = (bf16[272,128]{1,0:T(8,128)(2,1)S(1)}, bf16[272,128]{1,0:T(8,128)(2,1)S(1)}, u32[]{:S(2)}, u32[]{:S(2)}) collective-permute-start(bf16[272,128]{1,0:T(8,128)(2,1)S(1)} %get-tuple-element.31), channel_id=1, source_target_pairs={{0,32},{8,40},{16,48},{24,56},{32,0},{40,8},{48,16},{56,24},{1,33}... | collective-permute-start | bytes 208904 | tf_op jit(solution)/shard_map/ppermute | solution.py:278
  47.1 6.1 %collective-permute-start.10 = (bf16[272,128]{1,0:T(8,128)(2,1)S(1)}, bf16[272,128]{1,0:T(8,128)(2,1)S(1)}, u32[]{:S(2)}, u32[]{:S(2)}) collective-permute-start(bf16[272,128]{1,0:T(8,128)(2,1)S(1)} %get-tuple-element.34), channel_id=1, source_target_pairs={{0,48},{8,56},{16,0},{24,8},{32,16},{40,24},{48,32},{56,40},{1,49}... | collective-permute-start | bytes 208904 | tf_op jit(solution)/shard_map/ppermute | solution.py:278
  49.8 3.4 %collective-permute-start.7 = (bf16[272,128]{1,0:T(8,128)(2,1)S(1)}, bf16[272,128]{1,0:T(8,128)(2,1)S(1)}, u32[]{:S(2)}, u32[]{:S(2)}) collective-permute-start(bf16[272,128]{1,0:T(8,128)(2,1)S(1)} %get-tuple-element.29.refs_0_), channel_id=1, source_target_pairs={{0,8},{8,0},{16,24},{24,16},{32,40},{40,32},{48,56},{56,48},{1,9},... | collective-permute-start | bytes 208904 | tf_op jit(solution)/shard_map/ppermute | solution.py:282
  49.8 3.4 %collective-permute-start.8 = (bf16[272,128]{1,0:T(8,128)(2,1)S(1)}, bf16[272,128]{1,0:T(8,128)(2,1)S(1)}, u32[]{:S(2)}, u32[]{:S(2)}) collective-permute-start(bf16[272,128]{1,0:T(8,128)(2,1)S(1)} %collective-permute-done.5.refs_1_), channel_id=1, source_target_pairs={{0,8},{8,0},{16,24},{24,16},{32,40},{40,32},{48,56},{56,48},{1,9},... | collective-permute-start | bytes 208904 | tf_op jit(solution)/shard_map/ppermute | solution.py:282
  51.6 1.6 %collective-permute-start.9 = (bf16[272,128]{1,0:T(8,128)(2,1)S(1)}, bf16[272,128]{1,0:T(8,128)(2,1)S(1)}, u32[]{:S(2)}, u32[]{:S(2)}) collective-permute-start(bf16[272,128]{1,0:T(8,128)(2,1)S(1)} %collective-permute-done.6.refs_2_), channel_id=1, source_target_pairs={{0,8},{8,0},{16,24},{24,16},{32,40},{40,32},{48,56},{56,48},{1,9},... | collective-permute-start | bytes 208904 | tf_op jit(solution)/shard_map/ppermute | solution.py:282
  53.2 1.3 %collective-permute-start.11 = (bf16[272,128]{1,0:T(8,128)(2,1)S(1)}, bf16[272,128]{1,0:T(8,128)(2,1)S(1)}, u32[]{:S(2)}, u32[]{:S(2)}) collective-permute-start(bf16[272,128]{1,0:T(8,128)(2,1)S(1)} %collective-permute-done.10.own_ref), channel_id=1, source_target_pairs={{0,8},{8,0},{16,24},{24,16},{32,40},{40,32},{48,56},{56,48},{1,9},... | collective-permute-start | bytes 208904 | tf_op jit(solution)/shard_map/ppermute | solution.py:282
  55.4 8.8 %collective-permute-start.12 = (bf16[144,384]{1,0:T(8,128)(2,1)S(1)}, bf16[144,384]{1,0:T(8,128)(2,1)S(1)}, u32[]{:S(2)}, u32[]{:S(2)}) collective-permute-start(bf16[144,384]{1,0:T(8,128)(2,1)S(1)} %shard_map.88.u0), channel_id=1, source_target_pairs={{0,64},{64,128},{128,192},{192,0},{1,65},{65,129},{129,193},{193,1... | collective-permute-start | bytes 331784 | tf_op jit(solution)/shard_map/ppermute | solution.py:266
  55.5 8.8 %collective-permute-start.13 = (bf16[144,384]{1,0:T(8,128)(2,1)S(1)}, bf16[144,384]{1,0:T(8,128)(2,1)S(1)}, u32[]{:S(2)}, u32[]{:S(2)}) collective-permute-start(bf16[144,384]{1,0:T(8,128)(2,1)S(1)} %shard_map.88.u0), channel_id=1, source_target_pairs={{0,128},{64,192},{128,0},{192,64},{1,129},{65,193},{129,1},{193,65... | collective-permute-start | bytes 331784 | tf_op jit(solution)/shard_map/ppermute | solution.py:266
  57.2 7.6 %collective-permute-start.14 = (bf16[144,384]{1,0:T(8,128)(2,1)S(1)}, bf16[144,384]{1,0:T(8,128)(2,1)S(1)}, u32[]{:S(2)}, u32[]{:S(2)}) collective-permute-start(bf16[144,384]{1,0:T(8,128)(2,1)S(1)} %shard_map.88.u0), channel_id=1, source_target_pairs={{0,192},{64,0},{128,64},{192,128},{1,193},{65,1},{129,65},{193,129... | collective-permute-start | bytes 331784 | tf_op jit(solution)/shard_map/ppermute | solution.py:266
